TPU v7x, 32 devices: a whole 2x2x4 slice. The times are simulated.
32 devices in a mesh: row: 2 (over x), col: 16 (over z, y, core).
Axes of the slice: x: 2, y: 2, z: 4, core: 2. Of those that a mesh axis runs over, the one named last changes fastest.
Arguments:
- displacement: float32 [3, 16, 64, 2048], P(None, None, 'row', 'col'), may hold values from -1.75 to 1.75
- materials: int32 [15, 64, 2048], P(None, 'row', 'col'), may hold values from 0 to 7
- heating: float32 [15, 64, 2048], P(None, 'row', 'col'), may hold values from 0.5 to 1.5
- densities: float32 [2, 1024, 1920], P('row', 'col'), may hold values from 0 to 0.45
- block_target: int32 [2, 1024], P('row', 'col'), may hold values from 0 to 1023, as said below
- modulus: float32 [8], replicated, may hold values from 0.5 to 5
- poisson: float32 [8], replicated, may hold values from 0.15 to 0.35
- expansion: float32 [8], replicated, may hold values from 0.2 to 1
Outputs:
- settled: float32 [3, 16, 64, 2048], P(None, None, 'row', 'col')
- imbalance: float32 [3, 16, 64, 2048], P(None, None, 'row', 'col')
Inputs may be any that keep to these rules, and one draw needn't show every extreme that they name: `block_target`: row r lists, device after device of mesh row r, the 64 blocks each floorplan owner holds. Each row is a permutation; m names tile column m // 64 of the same mesh row and position m % 64 in it. Every owner holds exactly 4 blocks of every tile column of its mesh row.
All inputs are finite; a program needn't handle non-finite values.
Results may differ from a plain program's by a relative error of at most 0.00024.
Values sent between devices are 32-bit elements; how exact they have to be, the bound alone decides.
No kernel may reach another device: no remote copies, remote signals or barrier semaphores. Data moves between devices by JAX's collectives and lax.ppermute only.
A program may use at most 128 MiB of HBM per device.

v0:
```python
import functools

import jax
import jax.numpy as jnp
from jax import lax
from jax.experimental import pallas as pl
from jax.experimental.pallas import tpu as pltpu
from jax.sharding import PartitionSpec as P

BX = 4
BY = 16
ITERS = 3
HALO = 4
GROUP = 24
PER_MESSAGE = 6

hourglass_gain = 0.3
spring_stiffness = 1.0
relaxation = 0.5
copper_modulus = 3.0
copper_poisson = 0.34
copper_expansion = 0.4
solder_modulus = 1.0
solder_poisson = 0.36
solder_expansion = 0.6

in_vmem = pl.BlockSpec(memory_space=pltpu.VMEM)
in_smem = pl.BlockSpec(memory_space=pltpu.SMEM)
roomy = pltpu.CompilerParams(vmem_limit_bytes=48 * 1024 * 1024)


def f32(*shape):
    return jax.ShapeDtypeStruct(shape, jnp.float32)


def lanes_of():
    return lax.broadcasted_iota(jnp.int32, (8, 128), 1)


def sublanes_of():
    return lax.broadcasted_iota(jnp.int32, (8, 128), 0)


def roll_lanes(x, by):
    by %= 128
    return x if by == 0 else pltpu.roll(x, by, 1)


def strip_groups():
    lane = lanes_of()
    group = sum((lane >= GROUP * k).astype(jnp.int32) for k in range(1, 6))
    return group, lane - GROUP * group


def pack_kernel(tile_blocks, columns, quota, target_ref, density_ref, out_ref, count_ref):
    rows = density_ref.shape[1] // 128
    for column in range(columns):
        count_ref[column] = 0
    for block in range(density_ref.shape[0]):
        target = target_ref[0, block]
        column = lax.div(target, tile_blocks)
        rank = count_ref[column]
        count_ref[column] = rank + 1
        slot = column * quota + rank
        for c in range(rows):
            out_ref[slot, c : c + 1, :] = density_ref[block : block + 1, c * 128 : (c + 1) * 128]
        position = (target - column * tile_blocks).astype(jnp.float32)
        out_ref[slot, rows : rows + 1, :] = jnp.full((1, 128), position)


def edge_pair(a_low, a_high, b_low, b_high, row):
    first = sublanes_of() < HALO
    low = jnp.where(first, a_low, pltpu.roll(b_low, HALO, 0))
    high = jnp.where(first, pltpu.roll(a_high, HALO, 0), b_high)
    return [jnp.where(row == 0, high, low)] if row is not None else [low, high]


def unpack_kernel(paired, block_cols, arrived_ref, out_ref, *rest):
    edge_refs, sorted_ref = rest[:-1], rest[-1]
    blocks, depth, _ = arrived_ref.shape
    cells = depth - 1
    position = arrived_ref[:, depth - 1, :].astype(jnp.int32)
    for slot in range(blocks):
        start = pl.multiple_of(position[slot, 0] * depth, depth)
        sorted_ref[pl.ds(start, depth), :] = arrived_ref[slot]
    lane = lanes_of()
    for c in range(cells):
        tiles = [
            sorted_ref[pl.ds(k * depth + c, 8, stride=block_cols * depth), :]
            for k in range(block_cols)
        ]
        for bit in (1, 2, 4):
            stay = (lane & (BY * bit)) == 0
            swapped = list(tiles)
            for i in range(8):
                if i & bit == 0:
                    swapped[i] = jnp.where(stay, tiles[i], roll_lanes(tiles[i + bit], BY * bit))
                    swapped[i + bit] = jnp.where(
                        stay, roll_lanes(tiles[i], -BY * bit), tiles[i + bit]
                    )
            tiles = swapped
        for g in range(8):
            half, a = divmod(g, BX)
            out_ref[2 * c + half, pl.ds(a, 8, stride=BX), :] = tiles[g]
    row = lax.axis_index("row") if paired else None
    layers = out_ref.shape[0] // 2
    for l in range(layers):
        edges = edge_pair(
            out_ref[l, 0:8, :], out_ref[l, 24:32, :],
            out_ref[layers + l, 0:8, :], out_ref[layers + l, 24:32, :], row,
        )
        for ref, edge in zip(edge_refs, edges):
            ref[l] = edge


def edges_kernel(paired, displacement_ref, heating_ref, materials_ref, *edge_refs):
    row = lax.axis_index("row") if paired else None
    components, nodes = displacement_ref.shape[:2]
    layers = heating_ref.shape[0]
    k = 0
    for c in range(components):
        for z in range(0, nodes, 2):
            edges = edge_pair(
                displacement_ref[c, z, 0:8, :], displacement_ref[c, z, 24:32, :],
                displacement_ref[c, z + 1, 0:8, :], displacement_ref[c, z + 1, 24:32, :], row,
            )
            for ref, edge in zip(edge_refs, edges):
                ref[k] = edge
            k += 1
    for l in range(layers):
        edges = edge_pair(
            heating_ref[l, 0:8, :], heating_ref[l, 24:32, :],
            materials_ref[l, 0:8, :].astype(jnp.float32),
            materials_ref[l, 24:32, :].astype(jnp.float32), row,
        )
        for ref, edge in zip(edge_refs, edges):
            ref[k] = edge
        k += 1


def halo_rows(above, below, odd):
    first = sublanes_of() < HALO
    if odd:
        return jnp.where(first, pltpu.roll(above, HALO, 0), below)
    return jnp.where(first, above, pltpu.roll(below, HALO, 0))


def strip_of(chunks, group, place):
    strip = jnp.zeros((8, 128), jnp.float32)
    for k, chunk in enumerate(chunks):
        here = group == k
        strip = jnp.where(here & (place < 8), roll_lanes(chunk, GROUP * k + 8), strip)
        strip = jnp.where(here & (place >= 16), roll_lanes(chunk, GROUP * k + 16), strip)
    return strip


def write_messages(strips, place, left_ref, right_ref):
    for m in range(0, len(strips), PER_MESSAGE):
        left = jnp.zeros((8, 128), jnp.float32)
        right = left
        for k, strip in enumerate(strips[m : m + PER_MESSAGE]):
            here = (place >= HALO * k) & (place < HALO * (k + 1))
            left = jnp.where(here, roll_lanes(strip, HALO * k - 16), left)
            right = jnp.where(here, roll_lanes(strip, HALO * k - 4), right)
        left_ref[m // PER_MESSAGE] = left
        right_ref[m // PER_MESSAGE] = right


def with_halo(strip, item, from_right_ref, from_left_ref, place):
    m, k = divmod(item, PER_MESSAGE)
    strip = jnp.where(
        (place >= 8) & (place < 12), roll_lanes(from_right_ref[m], 8 - HALO * k), strip
    )
    return jnp.where(
        (place >= 12) & (place < 16), roll_lanes(from_left_ref[m], 12 - HALO * k), strip
    )


def own_chunks(ref, index, kind=None):
    chunks = [ref[(*index, pl.ds(8 * k, 8), slice(None))] for k in range(4)]
    return [chunk.astype(jnp.float32) for chunk in chunks]


def field_strips_kernel(
    displacement_ref, heating_ref, materials_ref, above_ref, below_ref, strip_ref, left_ref, right_ref
):
    components, nodes = displacement_ref.shape[:2]
    layers = heating_ref.shape[0]
    group, place = strip_groups()
    fields = [(displacement_ref, (c, z), (c * nodes + z) // 2, z % 2) for c in range(components) for z in range(nodes)]
    half = components * nodes // 2
    fields += [(heating_ref, (l,), half + l, 0) for l in range(layers)]
    fields += [(materials_ref, (l,), half + l, 1) for l in range(layers)]
    strips = []
    for k, (ref, index, edge, odd) in enumerate(fields):
        chunks = own_chunks(ref, index) + [halo_rows(above_ref[edge], below_ref[edge], odd)]
        strip = strip_of(chunks, group, place)
        strip_ref[k] = strip
        strips.append(strip)
    write_messages(strips, place, left_ref, right_ref)


def metal_strips_kernel(metals_ref, above_ref, below_ref, strip_ref, left_ref, right_ref):
    layers = metals_ref.shape[0] // 2
    group, place = strip_groups()
    strips = []
    for k in range(2 * layers):
        odd, l = divmod(k, layers)
        chunks = own_chunks(metals_ref, (k,)) + [halo_rows(above_ref[l], below_ref[l], odd)]
        strip = strip_of(chunks, group, place)
        strip_ref[k] = strip
        strips.append(strip)
    write_messages(strips, place, left_ref, right_ref)


def cell_properties(tables, material, copper, solder, heating, valid):
    modulus, poisson, expansion = (table[0] for table in tables)
    modulus, poisson, expansion = (jnp.full((8, 128), x) for x in (modulus, poisson, expansion))
    for code in range(1, len(tables[0])):
        here = material == float(code)
        modulus = jnp.where(here, tables[0][code], modulus)
        poisson = jnp.where(here, tables[1][code], poisson)
        expansion = jnp.where(here, tables[2][code], expansion)
    share = 1.0 - copper - solder
    young = share * modulus + copper * copper_modulus + solder * solder_modulus
    nu = share * poisson + copper * copper_poisson + solder * solder_poisson
    grow = share * expansion + copper * copper_expansion + solder * solder_expansion
    inverse = young / ((1.0 + nu) * (1.0 - 2.0 * nu))
    lame = inverse * nu
    shear = inverse * (0.5 - nu)
    thermal = (3.0 * lame + 2.0 * shear) * grow * heating
    zero = jnp.zeros((8, 128), jnp.float32)
    return (
        jnp.where(valid, lame * (1.0 / 16.0), zero),
        jnp.where(valid, shear * (1.0 / 16.0), zero),
        jnp.where(valid, thermal * 0.25, zero),
    )


def in_plane(v_ref, z, offset):
    faces = []
    for c in range(3):
        low = v_ref[c, z, pl.ds(offset, 8), :]
        high = v_ref[c, z, pl.ds(offset + 1, 8), :]
        pair, diff = low + high, high - low
        pair_next, diff_next = roll_lanes(pair, -1), roll_lanes(diff, -1)
        faces.append((pair + pair_next, pair_next - pair, diff + diff_next, diff_next - diff))
    return faces


def cell_forces(low, high, lame, shear, thermal):
    grad_x = [high[c][2] + low[c][2] for c in range(3)]
    grad_y = [high[c][1] + low[c][1] for c in range(3)]
    grad_z = [high[c][0] - low[c][0] for c in range(3)]
    weight = (2.0 * hourglass_gain) * shear
    double = shear + shear
    normal = lame * (grad_x[0] + grad_y[1] + grad_z[2]) - thermal
    xx = normal + double * grad_x[0]
    yy = normal + double * grad_y[1]
    zz = normal + double * grad_z[2]
    xy = shear * (grad_y[0] + grad_x[1])
    xz = shear * (grad_z[0] + grad_x[2])
    yz = shear * (grad_z[1] + grad_y[2])
    along = ((xx, xy, xz), (xy, yy, yz), (xz, yz, zz))
    below, above = [], []
    for c in range(3):
        one = weight * (high[c][1] - low[c][1])
        two = weight * (high[c][2] - low[c][2])
        three = weight * (high[c][3] + low[c][3])
        four = weight * (high[c][3] - low[c][3])
        sx, sy, sz = along[0][c], along[1][c], along[2][c]
        below.append((sx - two, sy - one, three - four, -sz))
        above.append((sx + two, sy + one, three + four, sz))
    return below, above


def scatter_in_plane(terms):
    diff_pair, pair_diff, diff_diff, pair_pair = terms
    of_diff = (diff_pair - diff_diff) + roll_lanes(diff_pair + diff_diff, 1)
    of_pair = (pair_pair - pair_diff) + roll_lanes(pair_pair + pair_diff, 1)
    return of_diff - of_pair, of_pair + of_diff


def sweep_kernel(
    rows_total,
    columns_total,
    displacement_ref,
    heating_ref,
    materials_ref,
    above_ref,
    below_ref,
    strip_ref,
    from_right_ref,
    from_left_ref,
    metals_ref,
    metal_above_ref,
    metal_below_ref,
    metal_strip_ref,
    metal_from_right_ref,
    metal_from_left_ref,
    modulus_ref,
    poisson_ref,
    expansion_ref,
    settled_ref,
    imbalance_ref,
    v_ref,
    own_ref,
    next_ref,
    lame_ref,
    shear_ref,
    thermal_ref,
    weight_ref,
    cell_strip_ref,
):
    nodes = displacement_ref.shape[1]
    layers = nodes - 1
    row_cells, col_cells = displacement_ref.shape[2:]
    lane, sub = lanes_of(), sublanes_of()
    group, place = strip_groups()

    def next_group(x):
        return jnp.where(lane < 4 * GROUP, roll_lanes(x, -GROUP), roll_lanes(x, 4 * GROUP))

    def previous_group(x):
        return jnp.where(lane >= GROUP, roll_lanes(x, GROUP), roll_lanes(x, -4 * GROUP))

    def store_nodes(c, z, j, x):
        if j < 5:
            v_ref[c, z, 8 * j : 8 * j + 8, :] = x
            if j == 0:
                v_ref[c, z, 40:48, :] = x
        else:
            v_ref[c, z, 48:56, :] = x
            v_ref[c, z, 56:64, :] = next_group(x)

    for c in range(3):
        for z in range(nodes):
            for j in range(4):
                store_nodes(c, z, j, displacement_ref[c, z, 8 * j : 8 * j + 8, :])
            k = (c * nodes + z) // 2
            store_nodes(c, z, 4, halo_rows(above_ref[k], below_ref[k], z % 2))
            item = c * nodes + z
            store_nodes(
                c, z, 5, with_halo(strip_ref[item], item, from_right_ref, from_left_ref, place)
            )
    for k in range(2 * layers):
        item = 3 * nodes + k
        cell_strip_ref[k] = with_halo(strip_ref[item], item, from_right_ref, from_left_ref, place)
    for k in range(2 * layers):
        cell_strip_ref[2 * layers + k] = with_halo(
            metal_strip_ref[k], k, metal_from_right_ref, metal_from_left_ref, place
        )

    first_x = lax.axis_index("row") * row_cells
    first_y = lax.axis_index("col") * col_cells
    last_x = rows_total - 1
    last_y = columns_total - 1

    def inside(x, y):
        return (x >= 0) & (x < last_x) & (y >= 0) & (y < last_y)

    valid = []
    for j in range(4):
        valid.append(inside(first_x + 8 * j + sub, first_y + lane))
    halo_x = jnp.where(sub < HALO, sub + row_cells, sub - 8)
    valid.append(inside(first_x + halo_x, first_y + lane))
    strip_x = jnp.where(group < 4, 8 * group + sub, halo_x)
    strip_y = jnp.where(place < 12, place + (col_cells - 8), place - 16)
    valid.append(inside(first_x + strip_x, first_y + strip_y) & (group < 5))
    tables = [
        [ref[k] for k in range(ref.shape[0])] for ref in (modulus_ref, poisson_ref, expansion_ref)
    ]
    half = 3 * nodes // 2

    def properties(l, _):
        for j in range(6):
            if j < 4:
                rows = slice(8 * j, 8 * j + 8)
                heat = heating_ref[l, rows, :]
                material = materials_ref[l, rows, :].astype(jnp.float32)
                copper = metals_ref[l, rows, :]
                solder = metals_ref[layers + l, rows, :]
            elif j == 4:
                heat = halo_rows(above_ref[half + l], below_ref[half + l], 0)
                material = halo_rows(above_ref[half + l], below_ref[half + l], 1)
                copper = halo_rows(metal_above_ref[l], metal_below_ref[l], 0)
                solder = halo_rows(metal_above_ref[l], metal_below_ref[l], 1)
            else:
                heat = cell_strip_ref[l]
                material = cell_strip_ref[layers + l]
                copper = cell_strip_ref[2 * layers + l]
                solder = cell_strip_ref[3 * layers + l]
            lame, shear, thermal = cell_properties(tables, material, copper, solder, heat, valid[j])
            lame_ref[l, 8 * j : 8 * j + 8, :] = lame
            shear_ref[l, 8 * j : 8 * j + 8, :] = shear
            thermal_ref[l, 8 * j : 8 * j + 8, :] = thermal
        return 0

    lax.fori_loop(0, layers, properties, 0)

    def shifted_in(ref, c, z):
        ref[c, z, 0:8, :] = ref[c, z, 40:48, :]
        ref[c, z, 48:56, :] = previous_group(ref[c, z, 56:64, :])

    def before(ref, c, z, j):
        start = 7 + 8 * j + (8 if j == 5 else 0)
        return ref[c, z, start : start + 8, :]

    for j in range(6):
        previous = jnp.zeros((8, 128), jnp.float32)
        rows = slice(8 * j, 8 * j + 8)
        start = 8 + 8 * j + (8 if j == 5 else 0)
        for z in range(nodes):
            total = previous
            if z < layers:
                term = lame_ref[z, rows, :] + (4.0 + 8.0 * hourglass_gain) * shear_ref[z, rows, :]
                total = total + term
                previous = term
            total = total + roll_lanes(total, 1)
            own_ref[0, z, rows, :] = total
            next_ref[0, z, start : start + 8, :] = total

    def weights(z, _):
        shifted_in(next_ref, 0, z)
        spring = jnp.where(z == 0, spring_stiffness, 0.0)
        for j in range(6):
            rows = slice(8 * j, 8 * j + 8)
            diagonal = own_ref[0, z, rows, :] + before(next_ref, 0, z, j) + spring
            some = diagonal > 0.0
            weight_ref[z, rows, :] = jnp.where(
                some, relaxation / jnp.where(some, diagonal, 1.0), 0.0
            )
        return 0

    lax.fori_loop(0, nodes, weights, 0)

    def forces():
        def chunk(j, _):
            rows = pl.ds(pl.multiple_of(8 * j, 8), 8)
            extra = jnp.where(j == 5, 8, 0)
            offset = pl.multiple_of(8 * j + extra, 8)
            start = pl.multiple_of(8 * j + extra + 8, 8)
            low = in_plane(v_ref, 0, offset)
            carried = None
            for z in range(nodes):
                below = above = None
                if z < layers:
                    high = in_plane(v_ref, z + 1, offset)
                    below, above = cell_forces(
                        low, high, lame_ref[z, rows, :], shear_ref[z, rows, :], thermal_ref[z, rows, :]
                    )
                    low = high
                for c in range(3):
                    if carried is None:
                        terms = below[c]
                    elif below is None:
                        terms = carried[c]
                    else:
                        terms = [a + b for a, b in zip(below[c], carried[c])]
                    here, there = scatter_in_plane(terms)
                    own_ref[c, z, rows, :] = here
                    next_ref[c, z, pl.ds(start, 8), :] = there
                carried = above
            return 0

        lax.fori_loop(0, 6, chunk, 0)

    def residual(c, z, j, v, spring):
        return own_ref[c, z, 8 * j : 8 * j + 8, :] - before(next_ref, c, z, j) - spring * v

    def nodes_of(c, z, j):
        start = 8 * j if j < 5 else 48
        return v_ref[c, z, start : start + 8, :]

    def sweep(_, carry):
        forces()

        def update(z, _):
            spring = jnp.where(z == 0, spring_stiffness, 0.0)
            for c in range(3):
                shifted_in(next_ref, c, z)
                for j in range(6):
                    v = nodes_of(c, z, j)
                    store_nodes(
                        c, z, j, v + weight_ref[z, 8 * j : 8 * j + 8, :] * residual(c, z, j, v, spring)
                    )
            return 0

        return lax.fori_loop(0, nodes, update, carry)

    lax.fori_loop(0, ITERS, sweep, 0)
    forces()

    def merged(inner, strip, k):
        inner = jnp.where(lane < HALO, roll_lanes(strip, -(GROUP * k + 16)), inner)
        return jnp.where(
            lane >= col_cells - HALO, roll_lanes(strip, col_cells - HALO - (GROUP * k + 4)), inner
        )

    def finish(z, _):
        spring = jnp.where(z == 0, spring_stiffness, 0.0)
        for c in range(3):
            shifted_in(next_ref, c, z)
            strip = nodes_of(c, z, 5)
            strip_residual = residual(c, z, 5, strip, spring)
            for j in range(4):
                v = nodes_of(c, z, j)
                settled_ref[c, z, 8 * j : 8 * j + 8, :] = merged(v, strip, j)
                imbalance_ref[c, z, 8 * j : 8 * j + 8, :] = merged(
                    residual(c, z, j, v, spring), strip_residual, j
                )
        return 0

    lax.fori_loop(0, nodes, finish, 0)


def exchange_rows(edges):
    count = lax.axis_size("row")
    if count == 2:
        other = lax.ppermute(edges[0], "row", [(0, 1), (1, 0)])
        return other, other
    above = lax.ppermute(edges[0], "row", [(i, i - 1) for i in range(1, count)])
    below = lax.ppermute(edges[1], "row", [(i, i + 1) for i in range(count - 1)])
    return above, below


def exchange_columns(to_left, to_right):
    count = lax.axis_size("col")
    from_right = lax.ppermute(to_left, "col", [(i, i - 1) for i in range(1, count)])
    from_left = lax.ppermute(to_right, "col", [(i, i + 1) for i in range(count - 1)])
    return from_right, from_left


def body(displacement, materials, heating, densities, block_target, modulus, poisson, expansion):
    nodes, row_cells, col_cells = displacement.shape[1:]
    layers = nodes - 1
    columns = lax.axis_size("col")
    paired = lax.axis_size("row") == 2
    edge_count = 1 if paired else 2
    blocks, payload = densities.shape[1:]
    depth = payload // 128 + 1
    block_cols = col_cells // BY
    tile_blocks = (row_cells // BX) * block_cols

    packed = pl.pallas_call(
        functools.partial(pack_kernel, tile_blocks, columns, blocks // columns),
        out_shape=f32(blocks, depth, 128),
        in_specs=[in_smem, in_vmem],
        out_specs=in_vmem,
        scratch_shapes=[pltpu.SMEM((columns,), jnp.int32)],
        compiler_params=roomy,
        name="pack_blocks",
    )(block_target, densities.reshape(blocks, payload))
    arrived = lax.all_to_all(packed, "col", split_axis=0, concat_axis=0, tiled=True)

    pairs = 3 * nodes // 2 + layers
    edges = pl.pallas_call(
        functools.partial(edges_kernel, paired),
        out_shape=[f32(pairs, 8, 128)] * edge_count,
        in_specs=[in_vmem] * 3,
        out_specs=[in_vmem] * edge_count,
        compiler_params=roomy,
        name="field_edges",
    )(displacement, heating, materials)
    above, below = exchange_rows(edges)
    fields = 2 * pairs
    messages = pl.cdiv(fields, PER_MESSAGE)
    strips, to_left, to_right = pl.pallas_call(
        field_strips_kernel,
        out_shape=[f32(fields, 8, 128), f32(messages, 8, 128), f32(messages, 8, 128)],
        in_specs=[in_vmem] * 5,
        out_specs=[in_vmem] * 3,
        compiler_params=roomy,
        name="field_strips",
    )(displacement, heating, materials, above, below)
    from_right, from_left = exchange_columns(to_left, to_right)

    metals, *metal_edges = pl.pallas_call(
        functools.partial(unpack_kernel, paired, block_cols),
        out_shape=[f32(2 * layers, row_cells, col_cells)] + [f32(layers, 8, 128)] * edge_count,
        in_specs=[in_vmem],
        out_specs=[in_vmem] * (1 + edge_count),
        scratch_shapes=[pltpu.VMEM((blocks * depth, 128), jnp.float32)],
        compiler_params=roomy,
        name="unpack_blocks",
    )(arrived)
    metal_above, metal_below = exchange_rows(metal_edges)
    metal_messages = pl.cdiv(2 * layers, PER_MESSAGE)
    metal_strips, to_left, to_right = pl.pallas_call(
        metal_strips_kernel,
        out_shape=[f32(2 * layers, 8, 128), f32(metal_messages, 8, 128), f32(metal_messages, 8, 128)],
        in_specs=[in_vmem] * 3,
        out_specs=[in_vmem] * 3,
        compiler_params=roomy,
        name="metal_strips",
    )(metals, metal_above, metal_below)
    metal_from_right, metal_from_left = exchange_columns(to_left, to_right)

    return pl.pallas_call(
        functools.partial(
            sweep_kernel, lax.axis_size("row") * row_cells, columns * col_cells
        ),
        out_shape=[f32(*displacement.shape)] * 2,
        in_specs=[in_vmem] * 14 + [in_smem] * 3,
        out_specs=[in_vmem] * 2,
        scratch_shapes=[
            pltpu.VMEM((3, nodes, 64, 128), jnp.float32),
            pltpu.VMEM((3, nodes, 48, 128), jnp.float32),
            pltpu.VMEM((3, nodes, 64, 128), jnp.float32),
            pltpu.VMEM((layers, 48, 128), jnp.float32),
            pltpu.VMEM((layers, 48, 128), jnp.float32),
            pltpu.VMEM((layers, 48, 128), jnp.float32),
            pltpu.VMEM((nodes, 48, 128), jnp.float32),
            pltpu.VMEM((4 * layers, 8, 128), jnp.float32),
        ],
        compiler_params=roomy,
        name="sweeps",
    )(
        displacement, heating, materials, above, below, strips, from_right, from_left,
        metals, metal_above, metal_below, metal_strips, metal_from_right, metal_from_left,
        modulus, poisson, expansion,
    )


def solution(mesh):
    placed = (
        P(None, None, "row", "col"),
        P(None, "row", "col"),
        P(None, "row", "col"),
        P("row", "col", None),
        P("row", "col"),
        P(),
        P(),
        P(),
    )
    return jax.shard_map(
        body,
        mesh=mesh,
        in_specs=placed,
        out_specs=(P(None, None, "row", "col"), P(None, None, "row", "col")),
        check_vma=False,
    )
```

profile of v0, /device:TPU:8, one launch (start us, length us, event | category | flops | bytes accessed | tf_op | source)
XLA Modules:
  0.0 77.7 jit_solution(7690590367029047282)
XLA Ops:
  0.6 0.0 copy-start.4
  0.6 0.6 copy-done.4
  1.3 1.0 %copy-done.3 = f32[1,64,1920]{2,1,0:T(8,128)S(1)} copy-done((f32[1,64,1920]{2,1,0:T(8,128)S(1)}, f32[1,64,1920]{2,1,0:T(8,128)}, u32[]{:S(2)}) %copy-start.3) | copy-done | bytes 491544
  2.3 0.0 copy-start
  2.3 1.9 %pack_blocks.1 = f32[64,16,128]{2,1,0:T(8,128)} custom-call(s32[1,64]{1,0:T(1,128)S(1)} %copy-done.4, f32[64,1920]{1,0:T(8,128)S(1)} %bitcast.1), custom_call_target="tpu_custom_call" | custom-call | tf_op jit(solution)/shard_map/pack_blocks/pallas_call | solution.py:545
  4.2 0.0 copy-start.1
  4.2 0.0 copy-start.2
  4.2 6.4 %all-to-all-start = ((f32[64,16,128]{2,1,0:T(8,128)}), f32[64,16,128]{2,1,0:T(8,128)S(1)}, u32[]{:S(2)}, u32[]{:S(2)}) async-start(f32[64,16,128]{2,1,0:T(8,128)} %pack_blocks.1), calls=%async_computation | async-start | bytes 1048576 | tf_op jit(solution)/shard_map/all_to_all | solution.py:554
  10.6 0.0 copy-done
  10.6 0.0 copy-done.1
  10.6 0.0 copy-done.2
  10.7 1.6 %collective-permute-start = (f32[39,8,128]{2,1,0:T(8,128)S(1)}, f32[39,8,128]{2,1,0:T(8,128)S(1)}, u32[]{:S(2)}, u32[]{:S(2)}) collective-permute-start(f32[39,8,128]{2,1,0:T(8,128)S(1)} %field_edges.1), channel_id=1, source_target_pairs={{0,16},{16,0},{1,17},{17,1},{2,18},{18,2},{3,19},{19,3},{4,20},{20... | collective-permute-start | bytes 479240 | tf_op jit(solution)/shard_map/ppermute | solution.py:520
  12.3 12.0 %all-to-all-done.arrived_ref = f32[64,16,128]{2,1,0:T(8,128)S(1)} async-done(((f32[64,16,128]{2,1,0:T(8,128)}), f32[64,16,128]{2,1,0:T(8,128)S(1)}, u32[]{:S(2)}, u32[]{:S(2)}) %all-to-all-start) | async-done | bytes 524320 | tf_op jit(solution)/shard_map/all_to_all | solution.py:554
  24.3 1.0 %unpack_blocks.1 = (f32[30,32,128]{2,1,0:T(8,128)S(1)}, f32[15,8,128]{2,1,0:T(8,128)S(1)}) custom-call(f32[64,16,128]{2,1,0:T(8,128)S(1)} %all-to-all-done.arrived_ref), custom_call_target="tpu_custom_call" | custom-call | tf_op jit(solution)/shard_map/unpack_blocks/pallas_call | solution.py:578
  25.2 1.6 %collective-permute-start.3 = (f32[15,8,128]{2,1,0:T(8,128)S(1)}, f32[15,8,128]{2,1,0:T(8,128)S(1)}, u32[]{:S(2)}, u32[]{:S(2)}) collective-permute-start(f32[15,8,128]{2,1,0:T(8,128)S(1)} %get-tuple-element.14), channel_id=1, source_target_pairs={{0,16},{16,0},{1,17},{17,1},{2,18},{18,2},{3,19},{19,3},{4,20},{20... | collective-permute-start | bytes 184328 | tf_op jit(solution)/shard_map/ppermute | solution.py:520
  26.8 0.0 collective-permute-done.above_ref.below_ref
  26.8 1.0 %field_strips.1 = (f32[78,8,128]{2,1,0:T(8,128)S(1)}, f32[13,8,128]{2,1,0:T(8,128)S(1)}, f32[13,8,128]{2,1,0:T(8,128)S(1)}) custom-call(f32[3,16,32,128]{3,2,1,0:T(8,128)S(1)} %copy-done, f32[15,32,128]{2,1,0:T(8,128)S(1)} %copy-done.1, s32[15,32,128]{2,1,0:T(8,128)S(1)} %copy-done.2, f32[39,8,128]{2,1,0:T(8,128)S(1)} %collective-permute-done.above_ref.below_ref, ...), custom_call_target="tpu_custom_call" | custom-call | tf_op jit(solution)/shard_map/field_strips/pallas_call | solution.py:568
  27.8 2.8 %collective-permute-start.1 = (f32[13,8,128]{2,1,0:T(8,128)S(1)}, f32[13,8,128]{2,1,0:T(8,128)S(1)}, u32[]{:S(2)}, u32[]{:S(2)}) collective-permute-start(f32[13,8,128]{2,1,0:T(8,128)S(1)} %get-tuple-element.11), channel_id=1, source_target_pairs={{1,0},{2,1},{3,2},{4,3},{5,4},{6,5},{7,6},{8,7},{9,8},{10,9},{11,1... | collective-permute-start | bytes 159752 | tf_op jit(solution)/shard_map/ppermute | solution.py:529
  30.6 1.9 %collective-permute-start.2 = (f32[13,8,128]{2,1,0:T(8,128)S(1)}, f32[13,8,128]{2,1,0:T(8,128)S(1)}, u32[]{:S(2)}, u32[]{:S(2)}) collective-permute-start(f32[13,8,128]{2,1,0:T(8,128)S(1)} %get-tuple-element.12), channel_id=1, source_target_pairs={{0,1},{1,2},{2,3},{3,4},{4,5},{5,6},{6,7},{7,8},{8,9},{9,10},{10,1... | collective-permute-start | bytes 159752 | tf_op jit(solution)/shard_map/ppermute | solution.py:530
  32.5 0.0 collective-permute-done.3.above_ref.below_ref.metal_above_ref.metal_below_ref
  32.5 0.5 metal_strips.1
  33.0 4.5 %collective-permute-start.4 = (f32[5,8,128]{2,1,0:T(8,128)S(1)}, f32[5,8,128]{2,1,0:T(8,128)S(1)}, u32[]{:S(2)}, u32[]{:S(2)}) collective-permute-start(f32[5,8,128]{2,1,0:T(8,128)S(1)} %get-tuple-element.16), channel_id=1, source_target_pairs={{1,0},{2,1},{3,2},{4,3},{5,4},{6,5},{7,6},{8,7},{9,8},{10,9},{11,1... | collective-permute-start | bytes 61448 | tf_op jit(solution)/shard_map/ppermute | solution.py:529
  37.6 1.9 %collective-permute-start.5 = (f32[5,8,128]{2,1,0:T(8,128)S(1)}, f32[5,8,128]{2,1,0:T(8,128)S(1)}, u32[]{:S(2)}, u32[]{:S(2)}) collective-permute-start(f32[5,8,128]{2,1,0:T(8,128)S(1)} %get-tuple-element.17), channel_id=1, source_target_pairs={{0,1},{1,2},{2,3},{3,4},{4,5},{5,6},{6,7},{7,8},{8,9},{9,10},{10,1... | collective-permute-start | bytes 61448 | tf_op jit(solution)/shard_map/ppermute | solution.py:530
  39.5 0.0 collective-permute-done.1.from_right_ref
  39.5 0.0 collective-permute-done.2.from_left_ref
  39.5 0.0 collective-permute-done.4.metal_from_right_ref
  39.5 4.0 %collective-permute-done.5.metal_from_left_ref = f32[5,8,128]{2,1,0:T(8,128)S(1)} collective-permute-done((f32[5,8,128]{2,1,0:T(8,128)S(1)}, f32[5,8,128]{2,1,0:T(8,128)S(1)}, u32[]{:S(2)}, u32[]{:S(2)}) %collective-permute-start.5) | collective-permute-done | bytes 20512 | tf_op jit(solution)/shard_map/ppermute | solution.py:530
  43.6 0.0 copy-start.5
  43.6 0.6 copy-done.5
  44.2 0.0 copy-done.6
  44.2 0.0 copy-done.7
  44.3 33.4 %sweeps.1 = (f32[3,16,32,128]{3,2,1,0:T(8,128)}, f32[3,16,32,128]{3,2,1,0:T(8,128)}) custom-call(f32[3,16,32,128]{3,2,1,0:T(8,128)S(1)} %copy-done, f32[15,32,128]{2,1,0:T(8,128)S(1)} %copy-done.1, s32[15,32,128]{2,1,0:T(8,128)S(1)} %copy-done.2, f32[39,8,128]{2,1,0:T(8,128)S(1)} %collective-permute-done.above_ref.below_ref, ...), custom_call_target="tpu_custom_call" | custom-call | tf_op jit(solution)/shard_map/sweeps/pallas_call | solution.py:599
  (4 shorter events, 0.1 us)
Async XLA Ops:
  0.6 0.7 copy-start.4
  1.3 1.0 %copy-start.3 = (f32[1,64,1920]{2,1,0:T(8,128)S(1)}, f32[1,64,1920]{2,1,0:T(8,128)}, u32[]{:S(2)}) copy-start(f32[1,64,1920]{2,1,0:T(8,128)} %param.11) | copy-start | bytes 1474564
  2.3 8.3 %copy-start = (f32[3,16,32,128]{3,2,1,0:T(8,128)S(1)}, f32[3,16,32,128]{3,2,1,0:T(8,128)}, u32[]{:S(2)}) copy-start(f32[3,16,32,128]{3,2,1,0:T(8,128)} %displacement_ref.5) | copy-start | bytes 2359300
  4.2 6.4 %copy-start.1 = (f32[15,32,128]{2,1,0:T(8,128)S(1)}, f32[15,32,128]{2,1,0:T(8,128)}, u32[]{:S(2)}) copy-start(f32[15,32,128]{2,1,0:T(8,128)} %heating_ref.5) | copy-start | bytes 737284
  4.2 6.4 %copy-start.2 = (s32[15,32,128]{2,1,0:T(8,128)S(1)}, s32[15,32,128]{2,1,0:T(8,128)}, u32[]{:S(2)}) copy-start(s32[15,32,128]{2,1,0:T(8,128)} %materials_ref.5) | copy-start | bytes 737284
  4.2 20.1 %all-to-all-start = ((f32[64,16,128]{2,1,0:T(8,128)}), f32[64,16,128]{2,1,0:T(8,128)S(1)}, u32[]{:S(2)}, u32[]{:S(2)}) async-start(f32[64,16,128]{2,1,0:T(8,128)} %pack_blocks.1), calls=%async_computation | async-start | bytes 1048576 | tf_op jit(solution)/shard_map/all_to_all | solution.py:554
  10.7 16.1 %collective-permute-start = (f32[39,8,128]{2,1,0:T(8,128)S(1)}, f32[39,8,128]{2,1,0:T(8,128)S(1)}, u32[]{:S(2)}, u32[]{:S(2)}) collective-permute-start(f32[39,8,128]{2,1,0:T(8,128)S(1)} %field_edges.1), channel_id=1, source_target_pairs={{0,16},{16,0},{1,17},{17,1},{2,18},{18,2},{3,19},{19,3},{4,20},{20... | collective-permute-start | bytes 479240 | tf_op jit(solution)/shard_map/ppermute | solution.py:520
  25.2 7.3 %collective-permute-start.3 = (f32[15,8,128]{2,1,0:T(8,128)S(1)}, f32[15,8,128]{2,1,0:T(8,128)S(1)}, u32[]{:S(2)}, u32[]{:S(2)}) collective-permute-start(f32[15,8,128]{2,1,0:T(8,128)S(1)} %get-tuple-element.14), channel_id=1, source_target_pairs={{0,16},{16,0},{1,17},{17,1},{2,18},{18,2},{3,19},{19,3},{4,20},{20... | collective-permute-start | bytes 184328 | tf_op jit(solution)/shard_map/ppermute | solution.py:520
  27.8 11.7 %collective-permute-start.1 = (f32[13,8,128]{2,1,0:T(8,128)S(1)}, f32[13,8,128]{2,1,0:T(8,128)S(1)}, u32[]{:S(2)}, u32[]{:S(2)}) collective-permute-start(f32[13,8,128]{2,1,0:T(8,128)S(1)} %get-tuple-element.11), channel_id=1, source_target_pairs={{1,0},{2,1},{3,2},{4,3},{5,4},{6,5},{7,6},{8,7},{9,8},{10,9},{11,1... | collective-permute-start | bytes 159752 | tf_op jit(solution)/shard_map/ppermute | solution.py:529
  30.6 8.9 %collective-permute-start.2 = (f32[13,8,128]{2,1,0:T(8,128)S(1)}, f32[13,8,128]{2,1,0:T(8,128)S(1)}, u32[]{:S(2)}, u32[]{:S(2)}) collective-permute-start(f32[13,8,128]{2,1,0:T(8,128)S(1)} %get-tuple-element.12), channel_id=1, source_target_pairs={{0,1},{1,2},{2,3},{3,4},{4,5},{5,6},{6,7},{7,8},{8,9},{9,10},{10,1... | collective-permute-start | bytes 159752 | tf_op jit(solution)/shard_map/ppermute | solution.py:530
  33.0 6.5 %collective-permute-start.4 = (f32[5,8,128]{2,1,0:T(8,128)S(1)}, f32[5,8,128]{2,1,0:T(8,128)S(1)}, u32[]{:S(2)}, u32[]{:S(2)}) collective-permute-start(f32[5,8,128]{2,1,0:T(8,128)S(1)} %get-tuple-element.16), channel_id=1, source_target_pairs={{1,0},{2,1},{3,2},{4,3},{5,4},{6,5},{7,6},{8,7},{9,8},{10,9},{11,1... | collective-permute-start | bytes 61448 | tf_op jit(solution)/shard_map/ppermute | solution.py:529
  37.6 6.0 %collective-permute-start.5 = (f32[5,8,128]{2,1,0:T(8,128)S(1)}, f32[5,8,128]{2,1,0:T(8,128)S(1)}, u32[]{:S(2)}, u32[]{:S(2)}) collective-permute-start(f32[5,8,128]{2,1,0:T(8,128)S(1)} %get-tuple-element.17), channel_id=1, source_target_pairs={{0,1},{1,2},{2,3},{3,4},{4,5},{5,6},{6,7},{7,8},{8,9},{9,10},{10,1... | collective-permute-start | bytes 61448 | tf_op jit(solution)/shard_map/ppermute | solution.py:530
  43.6 0.7 copy-start.5
  43.6 0.7 copy-start.6
  43.6 0.7 copy-start.7
where the time goes:
time: 78 us; the launch traced here: 77.7 us
  Pallas kernels  37.8 us (48%)
  starting transfers between devices  20.7 us (27%)
  waiting for transfers between devices  16.1 us (21%)
  local copies, waits for them, and re-layouts  2.37 us (3%)
    pallas_call x1, Pallas kernels, body(): pl.pallas_call(functools.partial(sweep_kernel, lax.axis_size('row') * row...  33.4 us
    all_to_all x1, waiting for transfers between devices, body(): lax.all_to_all(packed, 'col', split_axis=0, concat_axis=0, tiled=True)  12 us
    ppermute x2, starting transfers between devices, exchange_columns(): lax.ppermute(to_left, 'col', [(i, i - 1) for i in range(1, count)])  7.3 us
    all_to_all x1, starting transfers between devices, body(): lax.all_to_all(packed, 'col', split_axis=0, concat_axis=0, tiled=True)  6.43 us
    ppermute x2, waiting for transfers between devices, exchange_columns(): lax.ppermute(to_right, 'col', [(i, i + 1) for i in range(count - 1)])  4.04 us
    ppermute x2, starting transfers between devices, exchange_columns(): lax.ppermute(to_right, 'col', [(i, i + 1) for i in range(count - 1)])  3.84 us
    ppermute x2, starting transfers between devices, exchange_rows(): other = lax.ppermute(edges[0], 'row', [(0, 1), (1, 0)])  3.11 us
    unnamed x16, local copies, waits for them, and re-layouts  2.37 us
  transfers between devices with their start and end apart: 7, of which 2 were waited for; matrix products, arithmetic and copies ran while one was open for 0% of the time, Pallas kernels for 3%

commit v1 on v0

--- a/solution.py
+++ b/solution.py
@@ -12,6 +12,7 @@
 ITERS = 3
 HALO = 4
 GROUP = 24
+BATCH = 16
 PER_MESSAGE = 6
 
 hourglass_gain = 0.3
@@ -44,6 +45,11 @@
 def roll_lanes(x, by):
     by %= 128
     return x if by == 0 else pltpu.roll(x, by, 1)
+
+
+def roll_rows(x, by):
+    by %= 8
+    return x if by == 0 else pltpu.roll(x, by, 0)
 
 
 def strip_groups():
@@ -145,13 +151,14 @@
     return jnp.where(first, above, pltpu.roll(below, HALO, 0))
 
 
-def strip_of(chunks, group, place):
-    strip = jnp.zeros((8, 128), jnp.float32)
-    for k, chunk in enumerate(chunks):
-        here = group == k
-        strip = jnp.where(here & (place < 8), roll_lanes(chunk, GROUP * k + 8), strip)
-        strip = jnp.where(here & (place >= 16), roll_lanes(chunk, GROUP * k + 16), strip)
-    return strip
+def strips_of(fields, group, place):
+    joined = []
+    for chunks in fields:
+        both = jnp.zeros((8, 128), jnp.float32)
+        for k, chunk in enumerate(chunks):
+            both = jnp.where(group == k, roll_lanes(chunk, GROUP * k + 8), both)
+        joined.append(both)
+    return [jnp.where(place < 8, both, roll_lanes(both, 8)) for both in joined]
 
 
 def write_messages(strips, place, left_ref, right_ref):
@@ -176,7 +183,7 @@
     )
 
 
-def own_chunks(ref, index, kind=None):
+def own_chunks(ref, index):
     chunks = [ref[(*index, pl.ds(8 * k, 8), slice(None))] for k in range(4)]
     return [chunk.astype(jnp.float32) for chunk in chunks]
 
@@ -191,25 +198,28 @@
     half = components * nodes // 2
     fields += [(heating_ref, (l,), half + l, 0) for l in range(layers)]
     fields += [(materials_ref, (l,), half + l, 1) for l in range(layers)]
-    strips = []
-    for k, (ref, index, edge, odd) in enumerate(fields):
-        chunks = own_chunks(ref, index) + [halo_rows(above_ref[edge], below_ref[edge], odd)]
-        strip = strip_of(chunks, group, place)
+    strips = strips_of(
+        [
+            own_chunks(ref, index) + [halo_rows(above_ref[edge], below_ref[edge], odd)]
+            for ref, index, edge, odd in fields
+        ],
+        group, place,
+    )
+    for k, strip in enumerate(strips):
         strip_ref[k] = strip
-        strips.append(strip)
     write_messages(strips, place, left_ref, right_ref)
 
 
 def metal_strips_kernel(metals_ref, above_ref, below_ref, strip_ref, left_ref, right_ref):
     layers = metals_ref.shape[0] // 2
     group, place = strip_groups()
-    strips = []
+    fields = []
     for k in range(2 * layers):
         odd, l = divmod(k, layers)
-        chunks = own_chunks(metals_ref, (k,)) + [halo_rows(above_ref[l], below_ref[l], odd)]
-        strip = strip_of(chunks, group, place)
+        fields.append(own_chunks(metals_ref, (k,)) + [halo_rows(above_ref[l], below_ref[l], odd)])
+    strips = strips_of(fields, group, place)
+    for k, strip in enumerate(strips):
         strip_ref[k] = strip
-        strips.append(strip)
     write_messages(strips, place, left_ref, right_ref)
 
 
@@ -237,14 +247,12 @@
     )
 
 
-def in_plane(v_ref, z, offset):
+def in_plane(s_ref, d_ref, z, offset):
     faces = []
     for c in range(3):
-        low = v_ref[c, z, pl.ds(offset, 8), :]
-        high = v_ref[c, z, pl.ds(offset + 1, 8), :]
-        pair, diff = low + high, high - low
-        pair_next, diff_next = roll_lanes(pair, -1), roll_lanes(diff, -1)
-        faces.append((pair + pair_next, pair_next - pair, diff + diff_next, diff_next - diff))
+        pair, pair_next = s_ref[c, z, pl.ds(offset, 8), :], s_ref[c, z, pl.ds(offset + 1, 8), :]
+        diff, diff_next = d_ref[c, z, pl.ds(offset, 8), :], d_ref[c, z, pl.ds(offset + 1, 8), :]
+        faces.append((pair + pair_next, diff + diff_next, pair_next - pair, diff_next - diff))
     return faces
 
 
@@ -276,9 +284,9 @@
 
 def scatter_in_plane(terms):
     diff_pair, pair_diff, diff_diff, pair_pair = terms
-    of_diff = (diff_pair - diff_diff) + roll_lanes(diff_pair + diff_diff, 1)
-    of_pair = (pair_pair - pair_diff) + roll_lanes(pair_pair + pair_diff, 1)
-    return of_diff - of_pair, of_pair + of_diff
+    own_pair, next_pair = pair_pair - diff_pair, pair_pair + diff_pair
+    own_diff, next_diff = pair_diff - diff_diff, pair_diff + diff_diff
+    return own_pair - own_diff, own_pair + own_diff, next_pair - next_diff, next_pair + next_diff
 
 
 def sweep_kernel(
@@ -304,6 +312,8 @@
     settled_ref,
     imbalance_ref,
     v_ref,
+    s_ref,
+    d_ref,
     own_ref,
     next_ref,
     lame_ref,
@@ -324,25 +334,45 @@
     def previous_group(x):
         return jnp.where(lane >= GROUP, roll_lanes(x, GROUP), roll_lanes(x, -4 * GROUP))
 
-    def store_nodes(c, z, j, x):
-        if j < 5:
-            v_ref[c, z, 8 * j : 8 * j + 8, :] = x
-            if j == 0:
-                v_ref[c, z, 40:48, :] = x
-        else:
-            v_ref[c, z, 48:56, :] = x
-            v_ref[c, z, 56:64, :] = next_group(x)
-
-    for c in range(3):
-        for z in range(nodes):
-            for j in range(4):
-                store_nodes(c, z, j, displacement_ref[c, z, 8 * j : 8 * j + 8, :])
+    def store_nodes(zs, layers_of):
+        edges = []
+        for z, v in zip(zs, layers_of):
+            edge = jnp.zeros((8, 128), jnp.float32)
+            for c in range(3):
+                for j in (5, 0, 1, 2, 3, 4):
+                    x = v[c][j]
+                    after = roll_lanes(x, -1)
+                    pair, diff = x + after, after - x
+                    v_ref[c, z, 8 * j : 8 * j + 8, :] = x
+                    start = 8 * j if j < 5 else 48
+                    s_ref[c, z, start : start + 8, :] = pair
+                    d_ref[c, z, start : start + 8, :] = diff
+                    if j == 0:
+                        s_ref[c, z, 40:48, :] = pair
+                        d_ref[c, z, 40:48, :] = diff
+                    if j == 5:
+                        edge = jnp.where(sub == 2 * c, roll_rows(pair, 2 * c), edge)
+                        edge = jnp.where(sub == 2 * c + 1, roll_rows(diff, 2 * c + 1), edge)
+            edges.append(edge)
+        edges = [next_group(edge) for edge in edges]
+        for z, edge in zip(zs, edges):
+            for c in range(3):
+                s_ref[c, z, 56:64, :] = roll_rows(edge, -2 * c)
+                d_ref[c, z, 56:64, :] = roll_rows(edge, -2 * c - 1)
+
+    tile = []
+    for z in range(nodes):
+        layer = []
+        for c in range(3):
             k = (c * nodes + z) // 2
-            store_nodes(c, z, 4, halo_rows(above_ref[k], below_ref[k], z % 2))
             item = c * nodes + z
-            store_nodes(
-                c, z, 5, with_halo(strip_ref[item], item, from_right_ref, from_left_ref, place)
+            layer.append(
+                [displacement_ref[c, z, 8 * j : 8 * j + 8, :] for j in range(4)]
+                + [halo_rows(above_ref[k], below_ref[k], z % 2)]
+                + [with_halo(strip_ref[item], item, from_right_ref, from_left_ref, place)]
             )
+        tile.append(layer)
+    store_nodes(range(nodes), tile)
     for k in range(2 * layers):
         item = 3 * nodes + k
         cell_strip_ref[k] = with_halo(strip_ref[item], item, from_right_ref, from_left_ref, place)
@@ -398,13 +428,23 @@
 
     lax.fori_loop(0, layers, properties, 0)
 
-    def shifted_in(ref, c, z):
-        ref[c, z, 0:8, :] = ref[c, z, 40:48, :]
-        ref[c, z, 48:56, :] = previous_group(ref[c, z, 56:64, :])
-
-    def before(ref, c, z, j):
+    def shifted_in(zs, fields):
+        edges = []
+        for z in zs:
+            edge = jnp.zeros((8, 128), jnp.float32)
+            for k, (f, c) in enumerate(fields):
+                next_ref[f, c, z, 0:8, :] = next_ref[f, c, z, 40:48, :]
+                last = next_ref[f, c, z, 56:64, :]
+                edge = jnp.where(sub == k, roll_rows(last, k - 7), edge)
+            edges.append(edge)
+        edges = [previous_group(edge) for edge in edges]
+        for z, edge in zip(zs, edges):
+            for k, (f, c) in enumerate(fields):
+                next_ref[f, c, z, 48:56, :] = roll_rows(edge, 7 - k)
+
+    def before(f, c, z, j):
         start = 7 + 8 * j + (8 if j == 5 else 0)
-        return ref[c, z, start : start + 8, :]
+        return next_ref[f, c, z, start : start + 8, :]
 
     for j in range(6):
         previous = jnp.zeros((8, 128), jnp.float32)
@@ -417,22 +457,19 @@
                 total = total + term
                 previous = term
             total = total + roll_lanes(total, 1)
-            own_ref[0, z, rows, :] = total
-            next_ref[0, z, start : start + 8, :] = total
-
-    def weights(z, _):
-        shifted_in(next_ref, 0, z)
-        spring = jnp.where(z == 0, spring_stiffness, 0.0)
+            own_ref[0, 0, z, rows, :] = total
+            next_ref[0, 0, z, start : start + 8, :] = total
+
+    shifted_in(range(nodes), [(0, 0)])
+    for z in range(nodes):
+        spring = spring_stiffness if z == 0 else 0.0
         for j in range(6):
             rows = slice(8 * j, 8 * j + 8)
-            diagonal = own_ref[0, z, rows, :] + before(next_ref, 0, z, j) + spring
+            diagonal = own_ref[0, 0, z, rows, :] + before(0, 0, z, j) + spring
             some = diagonal > 0.0
             weight_ref[z, rows, :] = jnp.where(
                 some, relaxation / jnp.where(some, diagonal, 1.0), 0.0
             )
-        return 0
-
-    lax.fori_loop(0, nodes, weights, 0)
 
     def forces():
         def chunk(j, _):
@@ -440,12 +477,12 @@
             extra = jnp.where(j == 5, 8, 0)
             offset = pl.multiple_of(8 * j + extra, 8)
             start = pl.multiple_of(8 * j + extra + 8, 8)
-            low = in_plane(v_ref, 0, offset)
+            low = in_plane(s_ref, d_ref, 0, offset)
             carried = None
             for z in range(nodes):
                 below = above = None
                 if z < layers:
-                    high = in_plane(v_ref, z + 1, offset)
+                    high = in_plane(s_ref, d_ref, z + 1, offset)
                     below, above = cell_forces(
                         low, high, lame_ref[z, rows, :], shear_ref[z, rows, :], thermal_ref[z, rows, :]
                     )
@@ -457,61 +494,72 @@
                         terms = carried[c]
                     else:
                         terms = [a + b for a, b in zip(below[c], carried[c])]
-                    here, there = scatter_in_plane(terms)
-                    own_ref[c, z, rows, :] = here
-                    next_ref[c, z, pl.ds(start, 8), :] = there
+                    parts = scatter_in_plane(terms)
+                    for f in range(2):
+                        own_ref[f, c, z, rows, :] = parts[f]
+                        next_ref[f, c, z, pl.ds(start, 8), :] = parts[2 + f]
                 carried = above
             return 0
 
         lax.fori_loop(0, 6, chunk, 0)
 
-    def residual(c, z, j, v, spring):
-        return own_ref[c, z, 8 * j : 8 * j + 8, :] - before(next_ref, c, z, j) - spring * v
+    every = [(f, c) for c in range(3) for f in range(2)]
+
+    def unbalanced(c, z, j, v):
+        here, there = (own_ref[f, c, z, 8 * j : 8 * j + 8, :] + before(f, c, z, j) for f in range(2))
+        total = here + roll_lanes(there, 1)
+        return total + jnp.where(z == 0, spring_stiffness, 0.0) * v
 
     def nodes_of(c, z, j):
-        start = 8 * j if j < 5 else 48
-        return v_ref[c, z, start : start + 8, :]
+        return v_ref[c, z, 8 * j : 8 * j + 8, :]
 
     def sweep(_, carry):
         forces()
 
-        def update(z, _):
-            spring = jnp.where(z == 0, spring_stiffness, 0.0)
-            for c in range(3):
-                shifted_in(next_ref, c, z)
-                for j in range(6):
-                    v = nodes_of(c, z, j)
-                    store_nodes(
-                        c, z, j, v + weight_ref[z, 8 * j : 8 * j + 8, :] * residual(c, z, j, v, spring)
-                    )
+        def update(block, _):
+            zs = [block * BATCH + i for i in range(BATCH)]
+            shifted_in(zs, every)
+            relaxed = []
+            for z in zs:
+                weight = [weight_ref[z, 8 * j : 8 * j + 8, :] for j in range(6)]
+                relaxed.append([])
+                for c in range(3):
+                    v = [nodes_of(c, z, j) for j in range(6)]
+                    relaxed[-1].append([v[j] - weight[j] * unbalanced(c, z, j, v[j]) for j in range(6)])
+            store_nodes(zs, relaxed)
             return 0
 
-        return lax.fori_loop(0, nodes, update, carry)
+        return lax.fori_loop(0, nodes // BATCH, update, carry)
 
     lax.fori_loop(0, ITERS, sweep, 0)
     forces()
 
+    def joined(strip):
+        return jnp.where(place < 8, strip, roll_lanes(strip, -8))
+
+    edge_lane = (lane < HALO) | (lane >= col_cells - HALO)
+
     def merged(inner, strip, k):
-        inner = jnp.where(lane < HALO, roll_lanes(strip, -(GROUP * k + 16)), inner)
-        return jnp.where(
-            lane >= col_cells - HALO, roll_lanes(strip, col_cells - HALO - (GROUP * k + 4)), inner
-        )
-
-    def finish(z, _):
-        spring = jnp.where(z == 0, spring_stiffness, 0.0)
-        for c in range(3):
-            shifted_in(next_ref, c, z)
-            strip = nodes_of(c, z, 5)
-            strip_residual = residual(c, z, 5, strip, spring)
+        return jnp.where(edge_lane, roll_lanes(strip, col_cells - 8 - GROUP * k), inner)
+
+    def finish(block, _):
+        zs = [block * BATCH + i for i in range(BATCH)]
+        shifted_in(zs, every)
+        cases = [(c, z) for z in zs for c in range(3)]
+        strips = [nodes_of(c, z, 5) for c, z in cases]
+        residuals = [-unbalanced(c, z, 5, strip) for (c, z), strip in zip(cases, strips)]
+        strips = [joined(x) for x in strips]
+        residuals = [joined(x) for x in residuals]
+        for (c, z), strip, strip_residual in zip(cases, strips, residuals):
             for j in range(4):
                 v = nodes_of(c, z, j)
                 settled_ref[c, z, 8 * j : 8 * j + 8, :] = merged(v, strip, j)
                 imbalance_ref[c, z, 8 * j : 8 * j + 8, :] = merged(
-                    residual(c, z, j, v, spring), strip_residual, j
+                    -unbalanced(c, z, j, v), strip_residual, j
                 )
         return 0
 
-    lax.fori_loop(0, nodes, finish, 0)
+    lax.fori_loop(0, nodes // BATCH, finish, 0)
 
 
 def exchange_rows(edges):
@@ -575,6 +623,7 @@
     )(displacement, heating, materials, above, below)
     from_right, from_left = exchange_columns(to_left, to_right)
 
+    arrived, from_right, from_left = lax.optimization_barrier((arrived, from_right, from_left))
     metals, *metal_edges = pl.pallas_call(
         functools.partial(unpack_kernel, paired, block_cols),
         out_shape=[f32(2 * layers, row_cells, col_cells)] + [f32(layers, 8, 128)] * edge_count,
@@ -604,9 +653,11 @@
         in_specs=[in_vmem] * 14 + [in_smem] * 3,
         out_specs=[in_vmem] * 2,
         scratch_shapes=[
-            pltpu.VMEM((3, nodes, 64, 128), jnp.float32),
             pltpu.VMEM((3, nodes, 48, 128), jnp.float32),
             pltpu.VMEM((3, nodes, 64, 128), jnp.float32),
+            pltpu.VMEM((3, nodes, 64, 128), jnp.float32),
+            pltpu.VMEM((2, 3, nodes, 48, 128), jnp.float32),
+            pltpu.VMEM((2, 3, nodes, 64, 128), jnp.float32),
             pltpu.VMEM((layers, 48, 128), jnp.float32),
             pltpu.VMEM((layers, 48, 128), jnp.float32),
             pltpu.VMEM((layers, 48, 128), jnp.float32),

time: 78 us -> 54.3 us (0.70)
  Pallas kernels: 37.8 us -> 17.4 us
  starting transfers between devices: 20.7 us -> 18.2 us
  waiting for transfers between devices: 16.1 us -> 15.3 us
    pallas_call x1, Pallas kernels: 33.4 us -> 13.4 us  [body(): pl.pallas_call(functools.partial(sweep_kernel, lax.axis_size('row') * row...]
    all_to_all x1, waiting for transfers between devices: 12 us -> 0.01 us  [body(): lax.all_to_all(packed, 'col', split_axis=0, concat_axis=0, tiled=True)]
    ppermute x2, waiting for transfers between devices: 0.01 us -> 7.4 us  [exchange_rows(): other = lax.ppermute(edges[0], 'row', [(0, 1), (1, 0)])]
    ppermute x2, waiting for transfers between devices: 4.04 us -> 7.42 us  [exchange_columns(): lax.ppermute(to_right, 'col', [(i, i + 1) for i in range(count - 1)])]
    ppermute x2, starting transfers between devices: 7.3 us -> 4.21 us  [exchange_columns(): lax.ppermute(to_left, 'col', [(i, i - 1) for i in range(1, count)])]
  transfers between devices with their start and end apart: 7 -> 7, of which waited for: 2 -> 5; matrix products, arithmetic and copies ran while one was open for 0% -> 0% of each run, Pallas kernels for 3% -> 1%
where the time goes in v1:
time: 54.3 us; the launch traced here: 54 us
  starting transfers between devices  18.2 us (34%)
  Pallas kernels  17.4 us (32%)
  waiting for transfers between devices  15.3 us (28%)
  local copies, waits for them, and re-layouts  2.37 us (4%)
  between operations  0.73 us (1%)
    pallas_call x1, Pallas kernels, body(): pl.pallas_call(functools.partial(sweep_kernel, lax.axis_size('row') * row...  13.4 us
    ppermute x2, waiting for transfers between devices, exchange_columns(): lax.ppermute(to_right, 'col', [(i, i + 1) for i in range(count - 1)])  7.42 us
    ppermute x2, waiting for transfers between devices, exchange_rows(): other = lax.ppermute(edges[0], 'row', [(0, 1), (1, 0)])  7.4 us
    all_to_all x1, starting transfers between devices, body(): lax.all_to_all(packed, 'col', split_axis=0, concat_axis=0, tiled=True)  6.43 us
    ppermute x2, starting transfers between devices, exchange_columns(): lax.ppermute(to_right, 'col', [(i, i + 1) for i in range(count - 1)])  4.44 us
    ppermute x2, starting transfers between devices, exchange_columns(): lax.ppermute(to_left, 'col', [(i, i - 1) for i in range(1, count)])  4.21 us
    ppermute x2, starting transfers between devices, exchange_rows(): other = lax.ppermute(edges[0], 'row', [(0, 1), (1, 0)])  3.11 us
    unnamed x16, local copies, waits for them, and re-layouts  2.37 us
  transfers between devices with their start and end apart: 7, of which 5 were waited for; matrix products, arithmetic and copies ran while one was open for 0% of the time, Pallas kernels for 1%

profile of v1, /device:TPU:8, one launch (start us, length us, event | category | flops | bytes accessed | tf_op | source)
XLA Modules:
  0.0 54.0 jit_solution(9312406853607758022)
XLA Ops:
  0.6 0.0 copy-start.4
  0.6 0.6 %copy-done.4 = s32[1,64]{1,0:T(1,128)S(1)} copy-done((s32[1,64]{1,0:T(1,128)S(1)}, s32[1,64]{1,0:T(1,128)}, u32[]{:S(2)}) %copy-start.4) | copy-done | bytes 280
  1.3 0.0 copy-start.3
  1.3 1.0 %copy-done.3 = f32[1,64,1920]{2,1,0:T(8,128)S(1)} copy-done((f32[1,64,1920]{2,1,0:T(8,128)S(1)}, f32[1,64,1920]{2,1,0:T(8,128)}, u32[]{:S(2)}) %copy-start.3) | copy-done | bytes 491544
  2.3 0.0 copy-start
  2.3 1.9 %pack_blocks.1 = f32[64,16,128]{2,1,0:T(8,128)} custom-call(s32[1,64]{1,0:T(1,128)S(1)} %copy-done.4, f32[64,1920]{1,0:T(8,128)S(1)} %bitcast.1), custom_call_target="tpu_custom_call" | custom-call | tf_op jit(solution)/shard_map/pack_blocks/pallas_call | solution.py:593
  4.2 0.0 copy-start.1
  4.2 0.0 copy-start.2
  4.2 6.4 %all-to-all-start = ((f32[64,16,128]{2,1,0:T(8,128)}), f32[64,16,128]{2,1,0:T(8,128)S(1)}, u32[]{:S(2)}, u32[]{:S(2)}) async-start(f32[64,16,128]{2,1,0:T(8,128)} %pack_blocks.1), calls=%async_computation | async-start | bytes 1048576 | tf_op jit(solution)/shard_map/all_to_all | solution.py:602
  10.6 0.0 copy-done
  10.6 0.0 copy-done.1
  10.6 0.0 copy-done.2
  10.7 1.6 %collective-permute-start = (f32[39,8,128]{2,1,0:T(8,128)S(1)}, f32[39,8,128]{2,1,0:T(8,128)S(1)}, u32[]{:S(2)}, u32[]{:S(2)}) collective-permute-start(f32[39,8,128]{2,1,0:T(8,128)S(1)} %field_edges.1), channel_id=1, source_target_pairs={{0,16},{16,0},{1,17},{17,1},{2,18},{18,2},{3,19},{19,3},{4,20},{20... | collective-permute-start | bytes 479240 | tf_op jit(solution)/shard_map/ppermute | solution.py:568
  12.3 4.7 %collective-permute-done.above_ref.below_ref = f32[39,8,128]{2,1,0:T(8,128)S(1)} collective-permute-done((f32[39,8,128]{2,1,0:T(8,128)S(1)}, f32[39,8,128]{2,1,0:T(8,128)S(1)}, u32[]{:S(2)}, u32[]{:S(2)}) %collective-permute-start) | collective-permute-done | bytes 159776 | tf_op jit(solution)/shard_map/ppermute | solution.py:568
  16.9 0.7 %field_strips.1 = (f32[78,8,128]{2,1,0:T(8,128)S(1)}, f32[13,8,128]{2,1,0:T(8,128)S(1)}, f32[13,8,128]{2,1,0:T(8,128)S(1)}) custom-call(f32[3,16,32,128]{3,2,1,0:T(8,128)S(1)} %copy-done, f32[15,32,128]{2,1,0:T(8,128)S(1)} %copy-done.1, s32[15,32,128]{2,1,0:T(8,128)S(1)} %copy-done.2, f32[39,8,128]{2,1,0:T(8,128)S(1)} %collective-permute-done.above_ref.below_ref, ...), custom_call_target="tpu_custom_call" | custom-call | tf_op jit(solution)/shard_map/field_strips/pallas_call | solution.py:616
  17.6 2.3 %collective-permute-start.1 = (f32[13,8,128]{2,1,0:T(8,128)S(1)}, f32[13,8,128]{2,1,0:T(8,128)S(1)}, u32[]{:S(2)}, u32[]{:S(2)}) collective-permute-start(f32[13,8,128]{2,1,0:T(8,128)S(1)} %get-tuple-element.14), channel_id=1, source_target_pairs={{1,0},{2,1},{3,2},{4,3},{5,4},{6,5},{7,6},{8,7},{9,8},{10,9},{11,1... | collective-permute-start | bytes 159752 | tf_op jit(solution)/shard_map/ppermute | solution.py:577
  19.9 2.0 %collective-permute-start.2 = (f32[13,8,128]{2,1,0:T(8,128)S(1)}, f32[13,8,128]{2,1,0:T(8,128)S(1)}, u32[]{:S(2)}, u32[]{:S(2)}) collective-permute-start(f32[13,8,128]{2,1,0:T(8,128)S(1)} %get-tuple-element.15), channel_id=1, source_target_pairs={{0,1},{1,2},{2,3},{3,4},{4,5},{5,6},{6,7},{7,8},{8,9},{9,10},{10,1... | collective-permute-start | bytes 159752 | tf_op jit(solution)/shard_map/ppermute | solution.py:578
  22.0 0.5 collective-permute-done.1.from_right_ref
  22.4 3.8 %collective-permute-done.2.from_left_ref = f32[13,8,128]{2,1,0:T(8,128)S(1)} collective-permute-done((f32[13,8,128]{2,1,0:T(8,128)S(1)}, f32[13,8,128]{2,1,0:T(8,128)S(1)}, u32[]{:S(2)}, u32[]{:S(2)}) %collective-permute-start.2) | collective-permute-done | bytes 53280 | tf_op jit(solution)/shard_map/ppermute | solution.py:578
  26.3 0.0 all-to-all-done.arrived_ref
  26.3 1.0 %unpack_blocks.1 = (f32[30,32,128]{2,1,0:T(8,128)S(1)}, f32[15,8,128]{2,1,0:T(8,128)S(1)}) custom-call(f32[64,16,128]{2,1,0:T(8,128)S(1)} %all-to-all-done.arrived_ref), custom_call_target="tpu_custom_call" | custom-call | tf_op jit(solution)/shard_map/unpack_blocks/pallas_call | solution.py:627
  27.3 1.6 %collective-permute-start.3 = (f32[15,8,128]{2,1,0:T(8,128)S(1)}, f32[15,8,128]{2,1,0:T(8,128)S(1)}, u32[]{:S(2)}, u32[]{:S(2)}) collective-permute-start(f32[15,8,128]{2,1,0:T(8,128)S(1)} %get-tuple-element.20), channel_id=1, source_target_pairs={{0,16},{16,0},{1,17},{17,1},{2,18},{18,2},{3,19},{19,3},{4,20},{20... | collective-permute-start | bytes 184328 | tf_op jit(solution)/shard_map/ppermute | solution.py:568
  28.8 2.7 %collective-permute-done.3.above_ref.below_ref.metal_above_ref.metal_below_ref = f32[15,8,128]{2,1,0:T(8,128)S(1)} collective-permute-done((f32[15,8,128]{2,1,0:T(8,128)S(1)}, f32[15,8,128]{2,1,0:T(8,128)S(1)}, u32[]{:S(2)}, u32[]{:S(2)}) %collective-permute-start.3) | collective-permute-done | bytes 61472 | tf_op jit(solution)/shard_map/ppermute | solution.py:568
  31.6 0.4 metal_strips.1
  31.9 1.9 %collective-permute-start.4 = (f32[5,8,128]{2,1,0:T(8,128)S(1)}, f32[5,8,128]{2,1,0:T(8,128)S(1)}, u32[]{:S(2)}, u32[]{:S(2)}) collective-permute-start(f32[5,8,128]{2,1,0:T(8,128)S(1)} %get-tuple-element.22), channel_id=1, source_target_pairs={{1,0},{2,1},{3,2},{4,3},{5,4},{6,5},{7,6},{8,7},{9,8},{10,9},{11,1... | collective-permute-start | bytes 61448 | tf_op jit(solution)/shard_map/ppermute | solution.py:577
  33.9 2.4 %collective-permute-start.5 = (f32[5,8,128]{2,1,0:T(8,128)S(1)}, f32[5,8,128]{2,1,0:T(8,128)S(1)}, u32[]{:S(2)}, u32[]{:S(2)}) collective-permute-start(f32[5,8,128]{2,1,0:T(8,128)S(1)} %get-tuple-element.23), channel_id=1, source_target_pairs={{0,1},{1,2},{2,3},{3,4},{4,5},{5,6},{6,7},{7,8},{8,9},{9,10},{10,1... | collective-permute-start | bytes 61448 | tf_op jit(solution)/shard_map/ppermute | solution.py:578
  36.3 0.0 collective-permute-done.4.metal_from_right_ref
  36.3 3.6 %collective-permute-done.5.metal_from_left_ref = f32[5,8,128]{2,1,0:T(8,128)S(1)} collective-permute-done((f32[5,8,128]{2,1,0:T(8,128)S(1)}, f32[5,8,128]{2,1,0:T(8,128)S(1)}, u32[]{:S(2)}, u32[]{:S(2)}) %collective-permute-start.5) | collective-permute-done | bytes 20512 | tf_op jit(solution)/shard_map/ppermute | solution.py:578
  39.9 0.6 %copy-done.5 = f32[8]{0:T(128)S(1)} copy-done((f32[8]{0:T(128)S(1)}, f32[8]{0:T(128)}, u32[]{:S(2)}) %copy-start.5) | copy-done | bytes 56
  40.5 0.0 copy-done.6
  40.5 0.0 copy-done.7
  40.6 13.4 %sweeps.1 = (f32[3,16,32,128]{3,2,1,0:T(8,128)}, f32[3,16,32,128]{3,2,1,0:T(8,128)}) custom-call(f32[3,16,32,128]{3,2,1,0:T(8,128)S(1)} %copy-done, f32[15,32,128]{2,1,0:T(8,128)S(1)} %copy-done.1, s32[15,32,128]{2,1,0:T(8,128)S(1)} %copy-done.2, f32[39,8,128]{2,1,0:T(8,128)S(1)} %collective-permute-done.above_ref.below_ref, ...), custom_call_target="tpu_custom_call" | custom-call | tf_op jit(solution)/shard_map/sweeps/pallas_call | solution.py:648
  (4 shorter events, 0.1 us)
Async XLA Ops:
  0.6 0.7 %copy-start.4 = (s32[1,64]{1,0:T(1,128)S(1)}, s32[1,64]{1,0:T(1,128)}, u32[]{:S(2)}) copy-start(s32[1,64]{1,0:T(1,128)} %target_ref.1) | copy-start | bytes 772
  1.3 1.0 %copy-start.3 = (f32[1,64,1920]{2,1,0:T(8,128)S(1)}, f32[1,64,1920]{2,1,0:T(8,128)}, u32[]{:S(2)}) copy-start(f32[1,64,1920]{2,1,0:T(8,128)} %param.11) | copy-start | bytes 1474564
  2.3 8.3 %copy-start = (f32[3,16,32,128]{3,2,1,0:T(8,128)S(1)}, f32[3,16,32,128]{3,2,1,0:T(8,128)}, u32[]{:S(2)}) copy-start(f32[3,16,32,128]{3,2,1,0:T(8,128)} %displacement_ref.5) | copy-start | bytes 2359300
  4.2 6.4 %copy-start.1 = (f32[15,32,128]{2,1,0:T(8,128)S(1)}, f32[15,32,128]{2,1,0:T(8,128)}, u32[]{:S(2)}) copy-start(f32[15,32,128]{2,1,0:T(8,128)} %heating_ref.5) | copy-start | bytes 737284
  4.2 6.4 %copy-start.2 = (s32[15,32,128]{2,1,0:T(8,128)S(1)}, s32[15,32,128]{2,1,0:T(8,128)}, u32[]{:S(2)}) copy-start(s32[15,32,128]{2,1,0:T(8,128)} %materials_ref.5) | copy-start | bytes 737284
  4.2 22.1 %all-to-all-start = ((f32[64,16,128]{2,1,0:T(8,128)}), f32[64,16,128]{2,1,0:T(8,128)S(1)}, u32[]{:S(2)}, u32[]{:S(2)}) async-start(f32[64,16,128]{2,1,0:T(8,128)} %pack_blocks.1), calls=%async_computation | async-start | bytes 1048576 | tf_op jit(solution)/shard_map/all_to_all | solution.py:602
  10.7 6.2 %collective-permute-start = (f32[39,8,128]{2,1,0:T(8,128)S(1)}, f32[39,8,128]{2,1,0:T(8,128)S(1)}, u32[]{:S(2)}, u32[]{:S(2)}) collective-permute-start(f32[39,8,128]{2,1,0:T(8,128)S(1)} %field_edges.1), channel_id=1, source_target_pairs={{0,16},{16,0},{1,17},{17,1},{2,18},{18,2},{3,19},{19,3},{4,20},{20... | collective-permute-start | bytes 479240 | tf_op jit(solution)/shard_map/ppermute | solution.py:568
  17.6 4.8 %collective-permute-start.1 = (f32[13,8,128]{2,1,0:T(8,128)S(1)}, f32[13,8,128]{2,1,0:T(8,128)S(1)}, u32[]{:S(2)}, u32[]{:S(2)}) collective-permute-start(f32[13,8,128]{2,1,0:T(8,128)S(1)} %get-tuple-element.14), channel_id=1, source_target_pairs={{1,0},{2,1},{3,2},{4,3},{5,4},{6,5},{7,6},{8,7},{9,8},{10,9},{11,1... | collective-permute-start | bytes 159752 | tf_op jit(solution)/shard_map/ppermute | solution.py:577
  19.9 6.4 %collective-permute-start.2 = (f32[13,8,128]{2,1,0:T(8,128)S(1)}, f32[13,8,128]{2,1,0:T(8,128)S(1)}, u32[]{:S(2)}, u32[]{:S(2)}) collective-permute-start(f32[13,8,128]{2,1,0:T(8,128)S(1)} %get-tuple-element.15), channel_id=1, source_target_pairs={{0,1},{1,2},{2,3},{3,4},{4,5},{5,6},{6,7},{7,8},{8,9},{9,10},{10,1... | collective-permute-start | bytes 159752 | tf_op jit(solution)/shard_map/ppermute | solution.py:578
  27.3 4.3 %collective-permute-start.3 = (f32[15,8,128]{2,1,0:T(8,128)S(1)}, f32[15,8,128]{2,1,0:T(8,128)S(1)}, u32[]{:S(2)}, u32[]{:S(2)}) collective-permute-start(f32[15,8,128]{2,1,0:T(8,128)S(1)} %get-tuple-element.20), channel_id=1, source_target_pairs={{0,16},{16,0},{1,17},{17,1},{2,18},{18,2},{3,19},{19,3},{4,20},{20... | collective-permute-start | bytes 184328 | tf_op jit(solution)/shard_map/ppermute | solution.py:568
  31.9 4.3 %collective-permute-start.4 = (f32[5,8,128]{2,1,0:T(8,128)S(1)}, f32[5,8,128]{2,1,0:T(8,128)S(1)}, u32[]{:S(2)}, u32[]{:S(2)}) collective-permute-start(f32[5,8,128]{2,1,0:T(8,128)S(1)} %get-tuple-element.22), channel_id=1, source_target_pairs={{1,0},{2,1},{3,2},{4,3},{5,4},{6,5},{7,6},{8,7},{9,8},{10,9},{11,1... | collective-permute-start | bytes 61448 | tf_op jit(solution)/shard_map/ppermute | solution.py:577
  33.9 6.0 %collective-permute-start.5 = (f32[5,8,128]{2,1,0:T(8,128)S(1)}, f32[5,8,128]{2,1,0:T(8,128)S(1)}, u32[]{:S(2)}, u32[]{:S(2)}) collective-permute-start(f32[5,8,128]{2,1,0:T(8,128)S(1)} %get-tuple-element.23), channel_id=1, source_target_pairs={{0,1},{1,2},{2,3},{3,4},{4,5},{5,6},{6,7},{7,8},{8,9},{9,10},{10,1... | collective-permute-start | bytes 61448 | tf_op jit(solution)/shard_map/ppermute | solution.py:578
  39.9 0.7 %copy-start.5 = (f32[8]{0:T(128)S(1)}, f32[8]{0:T(128)}, u32[]{:S(2)}) copy-start(f32[8]{0:T(128)} %modulus_ref.1) | copy-start | bytes 100
  39.9 0.7 %copy-start.6 = (f32[8]{0:T(128)S(1)}, f32[8]{0:T(128)}, u32[]{:S(2)}) copy-start(f32[8]{0:T(128)} %poisson_ref.1) | copy-start | bytes 100
  39.9 0.7 %copy-start.7 = (f32[8]{0:T(128)S(1)}, f32[8]{0:T(128)}, u32[]{:S(2)}) copy-start(f32[8]{0:T(128)} %expansion_ref.1) | copy-start | bytes 100

commit v2 on v1

--- a/solution.py
+++ b/solution.py
@@ -26,7 +26,9 @@
 solder_expansion = 0.6
 
 in_vmem = pl.BlockSpec(memory_space=pltpu.VMEM)
+in_hbm = pl.BlockSpec(memory_space=pltpu.HBM)
 in_smem = pl.BlockSpec(memory_space=pltpu.SMEM)
+whole_vmem = pltpu.CompilerParams(vmem_limit_bytes=60 * 1024 * 1024)
 roomy = pltpu.CompilerParams(vmem_limit_bytes=48 * 1024 * 1024)
 
 
@@ -58,20 +60,38 @@
     return group, lane - GROUP * group
 
 
-def pack_kernel(tile_blocks, columns, quota, target_ref, density_ref, out_ref, count_ref):
-    rows = density_ref.shape[1] // 128
-    for column in range(columns):
-        count_ref[column] = 0
-    for block in range(density_ref.shape[0]):
-        target = target_ref[0, block]
-        column = lax.div(target, tile_blocks)
-        rank = count_ref[column]
-        count_ref[column] = rank + 1
-        slot = column * quota + rank
-        for c in range(rows):
-            out_ref[slot, c : c + 1, :] = density_ref[block : block + 1, c * 128 : (c + 1) * 128]
-        position = (target - column * tile_blocks).astype(jnp.float32)
-        out_ref[slot, rows : rows + 1, :] = jnp.full((1, 128), position)
+def pack_kernel(
+    tile_blocks, columns, quota, target_hbm, density_hbm, out_ref, target_ref, density_ref, arrived
+):
+    blocks, payload = density_ref.shape
+    rows = payload // 128
+    copies = [pltpu.make_async_copy(target_hbm, target_ref, arrived.at[0])]
+    for k in range(blocks // 8):
+        part = pl.ds(8 * k, 8)
+        copies.append(
+            pltpu.make_async_copy(density_hbm.at[part], density_ref.at[part], arrived.at[1 + k])
+        )
+    for copy in copies:
+        copy.start()
+    square = (blocks, blocks)
+    across = lax.broadcasted_iota(jnp.int32, square, 1)
+    down = lax.broadcasted_iota(jnp.int32, square, 0)
+    copies[0].wait()
+    target_row = jnp.broadcast_to(target_ref[...].astype(jnp.float32), square)
+    target = jnp.sum(jnp.where(across == down, target_row, 0.0), axis=1, keepdims=True)
+    column_row = jnp.floor((target_row + 0.5) * (1.0 / tile_blocks))
+    column = jnp.floor((target + 0.5) * (1.0 / tile_blocks))
+    earlier = (column_row == column) & (across < down)
+    rank = jnp.sum(jnp.where(earlier, 1.0, 0.0), axis=1, keepdims=True)
+    slots = (column * quota + rank).astype(jnp.int32)
+    positions = jnp.broadcast_to(target - column * tile_blocks, (blocks, 128))
+    for k in range(blocks // 8):
+        copies[1 + k].wait()
+        for block in range(8 * k, 8 * k + 8):
+            slot = slots[block, 0]
+            for c in range(rows):
+                out_ref[slot, c : c + 1, :] = density_ref[block : block + 1, c * 128 : (c + 1) * 128]
+            out_ref[slot, rows : rows + 1, :] = positions[block : block + 1, :]
 
 
 def edge_pair(a_low, a_high, b_low, b_high, row):
@@ -119,7 +139,13 @@
             ref[l] = edge
 
 
-def edges_kernel(paired, displacement_ref, heating_ref, materials_ref, *edge_refs):
+def edges_kernel(
+    paired, displacement_ref, heating_ref, materials_ref, modulus_ref, poisson_ref, expansion_ref,
+    tables_ref, *edge_refs
+):
+    for t, ref in enumerate((modulus_ref, poisson_ref, expansion_ref)):
+        for code in range(ref.shape[0]):
+            tables_ref[t, code] = jnp.full((8, 128), ref[code])
     row = lax.axis_index("row") if paired else None
     components, nodes = displacement_ref.shape[:2]
     layers = heating_ref.shape[0]
@@ -161,7 +187,8 @@
     return [jnp.where(place < 8, both, roll_lanes(both, 8)) for both in joined]
 
 
-def write_messages(strips, place, left_ref, right_ref):
+def write_messages(strips, place, first_ref, second_ref):
+    even = lax.axis_index("col") % 2 == 0
     for m in range(0, len(strips), PER_MESSAGE):
         left = jnp.zeros((8, 128), jnp.float32)
         right = left
@@ -169,17 +196,25 @@
             here = (place >= HALO * k) & (place < HALO * (k + 1))
             left = jnp.where(here, roll_lanes(strip, HALO * k - 16), left)
             right = jnp.where(here, roll_lanes(strip, HALO * k - 4), right)
-        left_ref[m // PER_MESSAGE] = left
-        right_ref[m // PER_MESSAGE] = right
-
-
-def with_halo(strip, item, from_right_ref, from_left_ref, place):
+        first_ref[m // PER_MESSAGE] = jnp.where(even, right, left)
+        second_ref[m // PER_MESSAGE] = jnp.where(even, left, right)
+
+
+def read_messages(first_ref, second_ref):
+    even = lax.axis_index("col") % 2 == 0
+    pairs = [(first_ref[m], second_ref[m]) for m in range(first_ref.shape[0])]
+    right = [jnp.where(even, first, second) for first, second in pairs]
+    return right, [jnp.where(even, second, first) for first, second in pairs]
+
+
+def with_halo(strip, item, messages, place):
     m, k = divmod(item, PER_MESSAGE)
+    from_right, from_left = messages
     strip = jnp.where(
-        (place >= 8) & (place < 12), roll_lanes(from_right_ref[m], 8 - HALO * k), strip
+        (place >= 8) & (place < 12), roll_lanes(from_right[m], 8 - HALO * k), strip
     )
     return jnp.where(
-        (place >= 12) & (place < 16), roll_lanes(from_left_ref[m], 12 - HALO * k), strip
+        (place >= 12) & (place < 16), roll_lanes(from_left[m], 12 - HALO * k), strip
     )
 
 
@@ -189,7 +224,7 @@
 
 
 def field_strips_kernel(
-    displacement_ref, heating_ref, materials_ref, above_ref, below_ref, strip_ref, left_ref, right_ref
+    displacement_ref, heating_ref, materials_ref, above_ref, below_ref, strip_ref, first_ref, second_ref
 ):
     components, nodes = displacement_ref.shape[:2]
     layers = heating_ref.shape[0]
@@ -207,10 +242,10 @@
     )
     for k, strip in enumerate(strips):
         strip_ref[k] = strip
-    write_messages(strips, place, left_ref, right_ref)
-
-
-def metal_strips_kernel(metals_ref, above_ref, below_ref, strip_ref, left_ref, right_ref):
+    write_messages(strips, place, first_ref, second_ref)
+
+
+def metal_strips_kernel(metals_ref, above_ref, below_ref, strip_ref, first_ref, second_ref):
     layers = metals_ref.shape[0] // 2
     group, place = strip_groups()
     fields = []
@@ -220,12 +255,11 @@
     strips = strips_of(fields, group, place)
     for k, strip in enumerate(strips):
         strip_ref[k] = strip
-    write_messages(strips, place, left_ref, right_ref)
+    write_messages(strips, place, first_ref, second_ref)
 
 
 def cell_properties(tables, material, copper, solder, heating, valid):
     modulus, poisson, expansion = (table[0] for table in tables)
-    modulus, poisson, expansion = (jnp.full((8, 128), x) for x in (modulus, poisson, expansion))
     for code in range(1, len(tables[0])):
         here = material == float(code)
         modulus = jnp.where(here, tables[0][code], modulus)
@@ -298,17 +332,15 @@
     above_ref,
     below_ref,
     strip_ref,
-    from_right_ref,
-    from_left_ref,
+    first_ref,
+    second_ref,
     metals_ref,
     metal_above_ref,
     metal_below_ref,
     metal_strip_ref,
-    metal_from_right_ref,
-    metal_from_left_ref,
-    modulus_ref,
-    poisson_ref,
-    expansion_ref,
+    metal_first_ref,
+    metal_second_ref,
+    tables_ref,
     settled_ref,
     imbalance_ref,
     v_ref,
@@ -360,6 +392,8 @@
                 s_ref[c, z, 56:64, :] = roll_rows(edge, -2 * c)
                 d_ref[c, z, 56:64, :] = roll_rows(edge, -2 * c - 1)
 
+    messages = read_messages(first_ref, second_ref)
+    metal_messages = read_messages(metal_first_ref, metal_second_ref)
     tile = []
     for z in range(nodes):
         layer = []
@@ -369,17 +403,15 @@
             layer.append(
                 [displacement_ref[c, z, 8 * j : 8 * j + 8, :] for j in range(4)]
                 + [halo_rows(above_ref[k], below_ref[k], z % 2)]
-                + [with_halo(strip_ref[item], item, from_right_ref, from_left_ref, place)]
+                + [with_halo(strip_ref[item], item, messages, place)]
             )
         tile.append(layer)
     store_nodes(range(nodes), tile)
     for k in range(2 * layers):
         item = 3 * nodes + k
-        cell_strip_ref[k] = with_halo(strip_ref[item], item, from_right_ref, from_left_ref, place)
+        cell_strip_ref[k] = with_halo(strip_ref[item], item, messages, place)
     for k in range(2 * layers):
-        cell_strip_ref[2 * layers + k] = with_halo(
-            metal_strip_ref[k], k, metal_from_right_ref, metal_from_left_ref, place
-        )
+        cell_strip_ref[2 * layers + k] = with_halo(metal_strip_ref[k], k, metal_messages, place)
 
     first_x = lax.axis_index("row") * row_cells
     first_y = lax.axis_index("col") * col_cells
@@ -397,12 +429,11 @@
     strip_x = jnp.where(group < 4, 8 * group + sub, halo_x)
     strip_y = jnp.where(place < 12, place + (col_cells - 8), place - 16)
     valid.append(inside(first_x + strip_x, first_y + strip_y) & (group < 5))
-    tables = [
-        [ref[k] for k in range(ref.shape[0])] for ref in (modulus_ref, poisson_ref, expansion_ref)
-    ]
+    codes = tables_ref.shape[1]
     half = 3 * nodes // 2
 
     def properties(l, _):
+        tables = [[tables_ref[t, code] for code in range(codes)] for t in range(3)]
         for j in range(6):
             if j < 4:
                 rows = slice(8 * j, 8 * j + 8)
@@ -572,11 +603,15 @@
     return above, below
 
 
-def exchange_columns(to_left, to_right):
+def exchange_columns(first, second):
     count = lax.axis_size("col")
-    from_right = lax.ppermute(to_left, "col", [(i, i - 1) for i in range(1, count)])
-    from_left = lax.ppermute(to_right, "col", [(i, i + 1) for i in range(count - 1)])
-    return from_right, from_left
+
+    def partner(i, other):
+        return other if 0 <= other < count else i
+
+    one = [(i, partner(i, i + 1 if i % 2 == 0 else i - 1)) for i in range(count)]
+    two = [(i, partner(i, i - 1 if i % 2 == 0 else i + 1)) for i in range(count)]
+    return lax.ppermute(first, "col", one), lax.ppermute(second, "col", two)
 
 
 def body(displacement, materials, heating, densities, block_target, modulus, poisson, expansion):
@@ -593,27 +628,31 @@
     packed = pl.pallas_call(
         functools.partial(pack_kernel, tile_blocks, columns, blocks // columns),
         out_shape=f32(blocks, depth, 128),
-        in_specs=[in_smem, in_vmem],
+        in_specs=[in_hbm, in_hbm],
         out_specs=in_vmem,
-        scratch_shapes=[pltpu.SMEM((columns,), jnp.int32)],
-        compiler_params=roomy,
+        scratch_shapes=[
+            pltpu.VMEM((1, blocks), jnp.int32),
+            pltpu.VMEM((blocks, payload), jnp.float32),
+            pltpu.SemaphoreType.DMA((1 + blocks // 8,)),
+        ],
+        compiler_params=whole_vmem,
         name="pack_blocks",
     )(block_target, densities.reshape(blocks, payload))
     arrived = lax.all_to_all(packed, "col", split_axis=0, concat_axis=0, tiled=True)
 
     pairs = 3 * nodes // 2 + layers
-    edges = pl.pallas_call(
+    tables, *edges = pl.pallas_call(
         functools.partial(edges_kernel, paired),
-        out_shape=[f32(pairs, 8, 128)] * edge_count,
-        in_specs=[in_vmem] * 3,
-        out_specs=[in_vmem] * edge_count,
+        out_shape=[f32(3, modulus.shape[0], 8, 128)] + [f32(pairs, 8, 128)] * edge_count,
+        in_specs=[in_vmem] * 3 + [in_smem] * 3,
+        out_specs=[in_vmem] * (1 + edge_count),
         compiler_params=roomy,
         name="field_edges",
-    )(displacement, heating, materials)
+    )(displacement, heating, materials, modulus, poisson, expansion)
     above, below = exchange_rows(edges)
     fields = 2 * pairs
     messages = pl.cdiv(fields, PER_MESSAGE)
-    strips, to_left, to_right = pl.pallas_call(
+    strips, to_first, to_second = pl.pallas_call(
         field_strips_kernel,
         out_shape=[f32(fields, 8, 128), f32(messages, 8, 128), f32(messages, 8, 128)],
         in_specs=[in_vmem] * 5,
@@ -621,9 +660,9 @@
         compiler_params=roomy,
         name="field_strips",
     )(displacement, heating, materials, above, below)
-    from_right, from_left = exchange_columns(to_left, to_right)
-
-    arrived, from_right, from_left = lax.optimization_barrier((arrived, from_right, from_left))
+    first, second = exchange_columns(to_first, to_second)
+
+    arrived, first, second = lax.optimization_barrier((arrived, first, second))
     metals, *metal_edges = pl.pallas_call(
         functools.partial(unpack_kernel, paired, block_cols),
         out_shape=[f32(2 * layers, row_cells, col_cells)] + [f32(layers, 8, 128)] * edge_count,
@@ -635,7 +674,7 @@
     )(arrived)
     metal_above, metal_below = exchange_rows(metal_edges)
     metal_messages = pl.cdiv(2 * layers, PER_MESSAGE)
-    metal_strips, to_left, to_right = pl.pallas_call(
+    metal_strips, to_first, to_second = pl.pallas_call(
         metal_strips_kernel,
         out_shape=[f32(2 * layers, 8, 128), f32(metal_messages, 8, 128), f32(metal_messages, 8, 128)],
         in_specs=[in_vmem] * 3,
@@ -643,14 +682,14 @@
         compiler_params=roomy,
         name="metal_strips",
     )(metals, metal_above, metal_below)
-    metal_from_right, metal_from_left = exchange_columns(to_left, to_right)
+    metal_first, metal_second = exchange_columns(to_first, to_second)
 
     return pl.pallas_call(
         functools.partial(
             sweep_kernel, lax.axis_size("row") * row_cells, columns * col_cells
         ),
         out_shape=[f32(*displacement.shape)] * 2,
-        in_specs=[in_vmem] * 14 + [in_smem] * 3,
+        in_specs=[in_vmem] * 15,
         out_specs=[in_vmem] * 2,
         scratch_shapes=[
             pltpu.VMEM((3, nodes, 48, 128), jnp.float32),
@@ -667,9 +706,8 @@
         compiler_params=roomy,
         name="sweeps",
     )(
-        displacement, heating, materials, above, below, strips, from_right, from_left,
-        metals, metal_above, metal_below, metal_strips, metal_from_right, metal_from_left,
-        modulus, poisson, expansion,
+        displacement, heating, materials, above, below, strips, first, second,
+        metals, metal_above, metal_below, metal_strips, metal_first, metal_second, tables,
     )
 
 

time: 54.3 us -> 49 us (0.902)
  the two profiles are of different devices: /device:TPU:8 before, /device:TPU:1 now
where the time goes in v2:
time: 49 us; the launch traced here: 48.8 us
  starting transfers between devices  18.8 us (38%)
  Pallas kernels  17.8 us (36%)
  waiting for transfers between devices  11.4 us (23%)
  between operations  0.79 us (2%)
    pallas_call x1, Pallas kernels, body(): pl.pallas_call(functools.partial(sweep_kernel, lax.axis_size('row') * row...  12.8 us
    ppermute x4, starting transfers between devices, exchange_columns(): return (lax.ppermute(first, 'col', one), lax.ppermute(second, 'col', two))  8.7 us
    all_to_all x1, starting transfers between devices, body(): lax.all_to_all(packed, 'col', split_axis=0, concat_axis=0, tiled=True)  7.49 us
    ppermute x2, waiting for transfers between devices, exchange_rows(): other = lax.ppermute(edges[0], 'row', [(0, 1), (1, 0)])  6.3 us
    ppermute x4, waiting for transfers between devices, exchange_columns(): return (lax.ppermute(first, 'col', one), lax.ppermute(second, 'col', two))  5.06 us
    ppermute x2, starting transfers between devices, exchange_rows(): other = lax.ppermute(edges[0], 'row', [(0, 1), (1, 0)])  2.58 us
    pallas_call x1, Pallas kernels, body(): pl.pallas_call(functools.partial(pack_kernel, tile_blocks, columns, block...  2.33 us
    pallas_call x1, Pallas kernels, body(): pl.pallas_call(functools.partial(unpack_kernel, paired, block_cols), out_...  0.99 us
  transfers between devices with their start and end apart: 7, of which 4 were waited for; matrix products, arithmetic and copies ran while one was open for 0% of the time, Pallas kernels for 3%

profile of v2, /device:TPU:1, one launch (start us, length us, event | category | flops | bytes accessed | tf_op | source)
XLA Modules:
  0.0 48.8 jit_solution(10337529529420491528)
XLA Ops:
  0.6 0.0 copy-start
  0.6 2.3 %pack_blocks.1 = f32[64,16,128]{2,1,0:T(8,128)} custom-call(s32[1,64]{1,0:T(1,128)} %target_hbm.1, f32[64,1920]{1,0:T(8,128)} %bitcast.1), custom_call_target="tpu_custom_call" | custom-call | tf_op jit(solution)/shard_map/pack_blocks/pallas_call | solution.py:628
  3.0 0.0 copy-start.1
  3.0 0.0 copy-start.2
  3.0 0.0 copy-start.3
  3.0 0.0 copy-start.4
  3.0 0.0 copy-start.5
  3.0 7.5 %all-to-all-start = ((f32[64,16,128]{2,1,0:T(8,128)}), f32[64,16,128]{2,1,0:T(8,128)S(1)}, u32[]{:S(2)}, u32[]{:S(2)}) async-start(f32[64,16,128]{2,1,0:T(8,128)} %pack_blocks.1), calls=%async_computation | async-start | bytes 1048576 | tf_op jit(solution)/shard_map/all_to_all | solution.py:641
  10.5 0.0 copy-done
  10.5 0.0 copy-done.1
  10.5 0.0 copy-done.2
  10.6 0.0 copy-done.3
  10.6 0.0 copy-done.4
  10.6 0.0 copy-done.5
  10.6 0.6 %field_edges.1 = (f32[3,8,8,128]{3,2,1,0:T(8,128)S(1)}, f32[39,8,128]{2,1,0:T(8,128)S(1)}) custom-call(f32[3,16,32,128]{3,2,1,0:T(8,128)S(1)} %copy-done, f32[15,32,128]{2,1,0:T(8,128)S(1)} %copy-done.1, s32[15,32,128]{2,1,0:T(8,128)S(1)} %copy-done.2, f32[8]{0:T(128)S(1)} %copy-done.3, f32[8]{0:T(128)S(1)} %copy-done.4, f32[8]{0:T(128)S(1)} %copy-done.5), custom_call_target="tpu_custom_call" | custom-call | tf_op jit(solution)/shard_map/field_edges/pallas_call | solution.py:644
  11.2 1.3 %collective-permute-start = (f32[39,8,128]{2,1,0:T(8,128)S(1)}, f32[39,8,128]{2,1,0:T(8,128)S(1)}, u32[]{:S(2)}, u32[]{:S(2)}) collective-permute-start(f32[39,8,128]{2,1,0:T(8,128)S(1)} %get-tuple-element.15), channel_id=1, source_target_pairs={{0,16},{16,0},{1,17},{17,1},{2,18},{18,2},{3,19},{19,3},{4,20},{20... | collective-permute-start | bytes 479240 | tf_op jit(solution)/shard_map/ppermute | solution.py:599
  12.5 4.4 %collective-permute-done.above_ref.below_ref = f32[39,8,128]{2,1,0:T(8,128)S(1)} collective-permute-done((f32[39,8,128]{2,1,0:T(8,128)S(1)}, f32[39,8,128]{2,1,0:T(8,128)S(1)}, u32[]{:S(2)}, u32[]{:S(2)}) %collective-permute-start) | collective-permute-done | bytes 159776 | tf_op jit(solution)/shard_map/ppermute | solution.py:599
  16.9 0.7 %field_strips.1 = (f32[78,8,128]{2,1,0:T(8,128)S(1)}, f32[13,8,128]{2,1,0:T(8,128)S(1)}, f32[13,8,128]{2,1,0:T(8,128)S(1)}) custom-call(f32[3,16,32,128]{3,2,1,0:T(8,128)S(1)} %copy-done, f32[15,32,128]{2,1,0:T(8,128)S(1)} %copy-done.1, s32[15,32,128]{2,1,0:T(8,128)S(1)} %copy-done.2, f32[39,8,128]{2,1,0:T(8,128)S(1)} %collective-permute-done.above_ref.below_ref, ...), custom_call_target="tpu_custom_call" | custom-call | tf_op jit(solution)/shard_map/field_strips/pallas_call | solution.py:655
  17.6 0.9 %collective-permute-start.1 = (f32[13,8,128]{2,1,0:T(8,128)S(1)}, f32[13,8,128]{2,1,0:T(8,128)S(1)}, u32[]{:S(2)}, u32[]{:S(2)}) collective-permute-start(f32[13,8,128]{2,1,0:T(8,128)S(1)} %get-tuple-element.17), channel_id=1, source_target_pairs={{0,1},{1,0},{2,3},{3,2},{4,5},{5,4},{6,7},{7,6},{8,9},{9,8},{10,11... | collective-permute-start | bytes 159752 | tf_op jit(solution)/shard_map/ppermute | solution.py:614
  18.6 3.2 %collective-permute-start.2 = (f32[13,8,128]{2,1,0:T(8,128)S(1)}, f32[13,8,128]{2,1,0:T(8,128)S(1)}, u32[]{:S(2)}, u32[]{:S(2)}) collective-permute-start(f32[13,8,128]{2,1,0:T(8,128)S(1)} %get-tuple-element.18), channel_id=1, source_target_pairs={{0,0},{1,2},{2,1},{3,4},{4,3},{5,6},{6,5},{7,8},{8,7},{9,10},{10,9... | collective-permute-start | bytes 159752 | tf_op jit(solution)/shard_map/ppermute | solution.py:614
  21.8 0.0 collective-permute-done.1.first_ref
  21.8 3.0 %collective-permute-done.2.second_ref = f32[13,8,128]{2,1,0:T(8,128)S(1)} collective-permute-done((f32[13,8,128]{2,1,0:T(8,128)S(1)}, f32[13,8,128]{2,1,0:T(8,128)S(1)}, u32[]{:S(2)}, u32[]{:S(2)}) %collective-permute-start.2) | collective-permute-done | bytes 53280 | tf_op jit(solution)/shard_map/ppermute | solution.py:614
  24.8 0.0 all-to-all-done.arrived_ref
  24.8 1.0 %unpack_blocks.1 = (f32[30,32,128]{2,1,0:T(8,128)S(1)}, f32[15,8,128]{2,1,0:T(8,128)S(1)}) custom-call(f32[64,16,128]{2,1,0:T(8,128)S(1)} %all-to-all-done.arrived_ref), custom_call_target="tpu_custom_call" | custom-call | tf_op jit(solution)/shard_map/unpack_blocks/pallas_call | solution.py:666
  25.8 1.3 %collective-permute-start.3 = (f32[15,8,128]{2,1,0:T(8,128)S(1)}, f32[15,8,128]{2,1,0:T(8,128)S(1)}, u32[]{:S(2)}, u32[]{:S(2)}) collective-permute-start(f32[15,8,128]{2,1,0:T(8,128)S(1)} %get-tuple-element.23), channel_id=1, source_target_pairs={{0,16},{16,0},{1,17},{17,1},{2,18},{18,2},{3,19},{19,3},{4,20},{20... | collective-permute-start | bytes 184328 | tf_op jit(solution)/shard_map/ppermute | solution.py:599
  27.1 1.9 %collective-permute-done.3.above_ref.below_ref.metal_above_ref.metal_below_ref = f32[15,8,128]{2,1,0:T(8,128)S(1)} collective-permute-done((f32[15,8,128]{2,1,0:T(8,128)S(1)}, f32[15,8,128]{2,1,0:T(8,128)S(1)}, u32[]{:S(2)}, u32[]{:S(2)}) %collective-permute-start.3) | collective-permute-done | bytes 61472 | tf_op jit(solution)/shard_map/ppermute | solution.py:599
  28.9 0.4 metal_strips.1
  29.3 1.5 %collective-permute-start.4 = (f32[5,8,128]{2,1,0:T(8,128)S(1)}, f32[5,8,128]{2,1,0:T(8,128)S(1)}, u32[]{:S(2)}, u32[]{:S(2)}) collective-permute-start(f32[5,8,128]{2,1,0:T(8,128)S(1)} %get-tuple-element.25), channel_id=1, source_target_pairs={{0,1},{1,0},{2,3},{3,2},{4,5},{5,4},{6,7},{7,6},{8,9},{9,8},{10,11... | collective-permute-start | bytes 61448 | tf_op jit(solution)/shard_map/ppermute | solution.py:614
  30.9 3.1 %collective-permute-start.5 = (f32[5,8,128]{2,1,0:T(8,128)S(1)}, f32[5,8,128]{2,1,0:T(8,128)S(1)}, u32[]{:S(2)}, u32[]{:S(2)}) collective-permute-start(f32[5,8,128]{2,1,0:T(8,128)S(1)} %get-tuple-element.26), channel_id=1, source_target_pairs={{0,0},{1,2},{2,1},{3,4},{4,3},{5,6},{6,5},{7,8},{8,7},{9,10},{10,9... | collective-permute-start | bytes 61448 | tf_op jit(solution)/shard_map/ppermute | solution.py:614
  33.9 0.0 collective-permute-done.4.metal_first_ref
  33.9 2.0 %collective-permute-done.5.metal_second_ref = f32[5,8,128]{2,1,0:T(8,128)S(1)} collective-permute-done((f32[5,8,128]{2,1,0:T(8,128)S(1)}, f32[5,8,128]{2,1,0:T(8,128)S(1)}, u32[]{:S(2)}, u32[]{:S(2)}) %collective-permute-start.5) | collective-permute-done | bytes 20512 | tf_op jit(solution)/shard_map/ppermute | solution.py:614
  35.9 12.8 %sweeps.1 = (f32[3,16,32,128]{3,2,1,0:T(8,128)}, f32[3,16,32,128]{3,2,1,0:T(8,128)}) custom-call(f32[3,16,32,128]{3,2,1,0:T(8,128)S(1)} %copy-done, f32[15,32,128]{2,1,0:T(8,128)S(1)} %copy-done.1, s32[15,32,128]{2,1,0:T(8,128)S(1)} %copy-done.2, f32[39,8,128]{2,1,0:T(8,128)S(1)} %collective-permute-done.above_ref.below_ref, ...), custom_call_target="tpu_custom_call" | custom-call | tf_op jit(solution)/shard_map/sweeps/pallas_call | solution.py:687
Async XLA Ops:
  0.6 9.9 %copy-start = (f32[3,16,32,128]{3,2,1,0:T(8,128)S(1)}, f32[3,16,32,128]{3,2,1,0:T(8,128)}, u32[]{:S(2)}) copy-start(f32[3,16,32,128]{3,2,1,0:T(8,128)} %displacement_ref.5) | copy-start | bytes 2359300
  3.0 7.6 %copy-start.1 = (f32[15,32,128]{2,1,0:T(8,128)S(1)}, f32[15,32,128]{2,1,0:T(8,128)}, u32[]{:S(2)}) copy-start(f32[15,32,128]{2,1,0:T(8,128)} %heating_ref.5) | copy-start | bytes 737284
  3.0 7.6 %copy-start.2 = (s32[15,32,128]{2,1,0:T(8,128)S(1)}, s32[15,32,128]{2,1,0:T(8,128)}, u32[]{:S(2)}) copy-start(s32[15,32,128]{2,1,0:T(8,128)} %materials_ref.5) | copy-start | bytes 737284
  3.0 7.6 %copy-start.3 = (f32[8]{0:T(128)S(1)}, f32[8]{0:T(128)}, u32[]{:S(2)}) copy-start(f32[8]{0:T(128)} %modulus_ref.1) | copy-start | bytes 100
  3.0 7.6 %copy-start.4 = (f32[8]{0:T(128)S(1)}, f32[8]{0:T(128)}, u32[]{:S(2)}) copy-start(f32[8]{0:T(128)} %poisson_ref.1) | copy-start | bytes 100
  3.0 7.6 %copy-start.5 = (f32[8]{0:T(128)S(1)}, f32[8]{0:T(128)}, u32[]{:S(2)}) copy-start(f32[8]{0:T(128)} %expansion_ref.1) | copy-start | bytes 100
  3.0 21.8 %all-to-all-start = ((f32[64,16,128]{2,1,0:T(8,128)}), f32[64,16,128]{2,1,0:T(8,128)S(1)}, u32[]{:S(2)}, u32[]{:S(2)}) async-start(f32[64,16,128]{2,1,0:T(8,128)} %pack_blocks.1), calls=%async_computation | async-start | bytes 1048576 | tf_op jit(solution)/shard_map/all_to_all | solution.py:641
  11.2 5.7 %collective-permute-start = (f32[39,8,128]{2,1,0:T(8,128)S(1)}, f32[39,8,128]{2,1,0:T(8,128)S(1)}, u32[]{:S(2)}, u32[]{:S(2)}) collective-permute-start(f32[39,8,128]{2,1,0:T(8,128)S(1)} %get-tuple-element.15), channel_id=1, source_target_pairs={{0,16},{16,0},{1,17},{17,1},{2,18},{18,2},{3,19},{19,3},{4,20},{20... | collective-permute-start | bytes 479240 | tf_op jit(solution)/shard_map/ppermute | solution.py:599
  17.6 4.1 %collective-permute-start.1 = (f32[13,8,128]{2,1,0:T(8,128)S(1)}, f32[13,8,128]{2,1,0:T(8,128)S(1)}, u32[]{:S(2)}, u32[]{:S(2)}) collective-permute-start(f32[13,8,128]{2,1,0:T(8,128)S(1)} %get-tuple-element.17), channel_id=1, source_target_pairs={{0,1},{1,0},{2,3},{3,2},{4,5},{5,4},{6,7},{7,6},{8,9},{9,8},{10,11... | collective-permute-start | bytes 159752 | tf_op jit(solution)/shard_map/ppermute | solution.py:614
  18.6 6.2 %collective-permute-start.2 = (f32[13,8,128]{2,1,0:T(8,128)S(1)}, f32[13,8,128]{2,1,0:T(8,128)S(1)}, u32[]{:S(2)}, u32[]{:S(2)}) collective-permute-start(f32[13,8,128]{2,1,0:T(8,128)S(1)} %get-tuple-element.18), channel_id=1, source_target_pairs={{0,0},{1,2},{2,1},{3,4},{4,3},{5,6},{6,5},{7,8},{8,7},{9,10},{10,9... | collective-permute-start | bytes 159752 | tf_op jit(solution)/shard_map/ppermute | solution.py:614
  25.8 3.1 %collective-permute-start.3 = (f32[15,8,128]{2,1,0:T(8,128)S(1)}, f32[15,8,128]{2,1,0:T(8,128)S(1)}, u32[]{:S(2)}, u32[]{:S(2)}) collective-permute-start(f32[15,8,128]{2,1,0:T(8,128)S(1)} %get-tuple-element.23), channel_id=1, source_target_pairs={{0,16},{16,0},{1,17},{17,1},{2,18},{18,2},{3,19},{19,3},{4,20},{20... | collective-permute-start | bytes 184328 | tf_op jit(solution)/shard_map/ppermute | solution.py:599
  29.3 4.6 %collective-permute-start.4 = (f32[5,8,128]{2,1,0:T(8,128)S(1)}, f32[5,8,128]{2,1,0:T(8,128)S(1)}, u32[]{:S(2)}, u32[]{:S(2)}) collective-permute-start(f32[5,8,128]{2,1,0:T(8,128)S(1)} %get-tuple-element.25), channel_id=1, source_target_pairs={{0,1},{1,0},{2,3},{3,2},{4,5},{5,4},{6,7},{7,6},{8,9},{9,8},{10,11... | collective-permute-start | bytes 61448 | tf_op jit(solution)/shard_map/ppermute | solution.py:614
  30.9 5.1 %collective-permute-start.5 = (f32[5,8,128]{2,1,0:T(8,128)S(1)}, f32[5,8,128]{2,1,0:T(8,128)S(1)}, u32[]{:S(2)}, u32[]{:S(2)}) collective-permute-start(f32[5,8,128]{2,1,0:T(8,128)S(1)} %get-tuple-element.26), channel_id=1, source_target_pairs={{0,0},{1,2},{2,1},{3,4},{4,3},{5,6},{6,5},{7,8},{8,7},{9,10},{10,9... | collective-permute-start | bytes 61448 | tf_op jit(solution)/shard_map/ppermute | solution.py:614

commit v3 on v2

--- a/solution.py
+++ b/solution.py
@@ -12,7 +12,6 @@
 ITERS = 3
 HALO = 4
 GROUP = 24
-BATCH = 16
 PER_MESSAGE = 6
 
 hourglass_gain = 0.3
@@ -29,7 +28,7 @@
 in_hbm = pl.BlockSpec(memory_space=pltpu.HBM)
 in_smem = pl.BlockSpec(memory_space=pltpu.SMEM)
 whole_vmem = pltpu.CompilerParams(vmem_limit_bytes=60 * 1024 * 1024)
-roomy = pltpu.CompilerParams(vmem_limit_bytes=48 * 1024 * 1024)
+roomy = pltpu.CompilerParams(vmem_limit_bytes=28 * 1024 * 1024)
 
 
 def f32(*shape):
@@ -323,247 +322,330 @@
     return own_pair - own_diff, own_pair + own_diff, next_pair - next_diff, next_pair + next_diff
 
 
+def chunk_forces(s_ref, d_ref, cell_refs, own_ref, next_ref, rows, offset):
+    nodes = own_ref.shape[2]
+    low = in_plane(s_ref, d_ref, 0, offset)
+    carried = None
+    for z in range(nodes):
+        below = above = None
+        if z < nodes - 1:
+            high = in_plane(s_ref, d_ref, z + 1, offset)
+            below, above = cell_forces(low, high, *(ref[z, rows, :] for ref in cell_refs))
+            low = high
+        for c in range(3):
+            if carried is None:
+                terms = below[c]
+            elif below is None:
+                terms = carried[c]
+            else:
+                terms = [a + b for a, b in zip(below[c], carried[c])]
+            parts = scatter_in_plane(terms)
+            for f in range(2):
+                own_ref[f, c, z, rows, :] = parts[f]
+                next_ref[f, c, z, rows, :] = parts[2 + f]
+        carried = above
+
+
+def inner_forces(s_ref, d_ref, cell_refs, own_ref, next_ref, count):
+    def chunk(j, carry):
+        start = pl.multiple_of(8 * j, 8)
+        chunk_forces(s_ref, d_ref, cell_refs, own_ref, next_ref, pl.ds(start, 8), start)
+        return carry
+
+    lax.fori_loop(0, count, chunk, 0)
+
+
+def strip_forces(s_ref, d_ref, cell_refs, own_ref, next_ref):
+    chunk_forces(s_ref, d_ref, cell_refs, own_ref, next_ref, slice(0, 8), 0)
+
+
+def chunk_of(j):
+    return slice(8 * j, 8 * j + 8)
+
+
+def row_before(x, previous):
+    return jnp.where(sublanes_of() == 0, roll_rows(previous, 1), roll_rows(x, 1))
+
+
+def next_group(x):
+    return jnp.where(lanes_of() < 4 * GROUP, roll_lanes(x, -GROUP), roll_lanes(x, 4 * GROUP))
+
+
+def previous_group(x):
+    return jnp.where(lanes_of() >= GROUP, roll_lanes(x, GROUP), roll_lanes(x, -4 * GROUP))
+
+
+def previous_rows(lasts):
+    packed = []
+    for first in range(0, len(lasts), 8):
+        edge = jnp.zeros((8, 128), jnp.float32)
+        for k, last in enumerate(lasts[first : first + 8]):
+            edge = jnp.where(sublanes_of() == k, roll_rows(last, k - 7), edge)
+        packed.append(edge)
+    packed = [previous_group(edge) for edge in packed]
+    return [roll_rows(packed[k // 8], 7 - k % 8) for k in range(len(lasts))]
+
+
+def store_inner(s_ref, d_ref, v_ref, c, z, j, x):
+    after = roll_lanes(x, -1)
+    pair, diff = x + after, after - x
+    if v_ref is not None:
+        v_ref[c, z, chunk_of(j), :] = x
+    s_ref[c, z, chunk_of(j), :] = pair
+    d_ref[c, z, chunk_of(j), :] = diff
+    if j == 0:
+        s_ref[c, z, 40:48, :] = pair
+        d_ref[c, z, 40:48, :] = diff
+
+
+def store_strips(s_ref, d_ref, v_ref, strips):
+    edges = []
+    after = [[roll_lanes(x, -1) for x in row] for row in strips]
+    packed = []
+    for c, row in enumerate(strips):
+        for z, x in enumerate(row):
+            pair, diff = x + after[c][z], after[c][z] - x
+            v_ref[c, z] = x
+            s_ref[c, z, 0:8, :] = pair
+            d_ref[c, z, 0:8, :] = diff
+            edges += [(s_ref, c, z, pair), (d_ref, c, z, diff)]
+    for first in range(0, len(edges), 8):
+        edge = jnp.zeros((8, 128), jnp.float32)
+        for k, (_, _, _, x) in enumerate(edges[first : first + 8]):
+            edge = jnp.where(sublanes_of() == k, roll_rows(x, k), edge)
+        packed.append(edge)
+    packed = [next_group(edge) for edge in packed]
+    for k, (ref, c, z, _) in enumerate(edges):
+        ref[c, z, 8:16, :] = roll_rows(packed[k // 8], -(k % 8))
+
+
+def cell_diagonals(lame_ref, shear_ref, rows):
+    layers = lame_ref.shape[0]
+    totals, previous = [], None
+    for z in range(layers + 1):
+        term = None
+        if z < layers:
+            term = lame_ref[z, rows, :] + (4.0 + 8.0 * hourglass_gain) * shear_ref[z, rows, :]
+        totals.append(term if previous is None else previous if term is None else term + previous)
+        previous = term
+    rolled = [roll_lanes(total, 1) for total in totals]
+    return [total + after for total, after in zip(totals, rolled)]
+
+
+def weight_of(diagonal, z):
+    if z == 0:
+        diagonal = diagonal + spring_stiffness
+    some = diagonal > 0.0
+    return jnp.where(some, relaxation / jnp.where(some, diagonal, 1.0), 0.0)
+
+
+def unbalanced(here, there, v, z):
+    total = here + roll_lanes(there, 1)
+    return total + spring_stiffness * v if z == 0 else total
+
+
+def inside(x, y, columns_total, rows_total):
+    return (x >= 0) & (x < rows_total - 1) & (y >= 0) & (y < columns_total - 1)
+
+
+def first_cell(row_cells, col_cells):
+    return lax.axis_index("row") * row_cells, lax.axis_index("col") * col_cells
+
+
+def load_tables(tables_ref):
+    return [[tables_ref[t, code] for code in range(tables_ref.shape[1])] for t in range(3)]
+
+
+def assemble(displacement_ref, above_ref, below_ref, s_ref, d_ref):
+    nodes = displacement_ref.shape[1]
+    for c in range(3):
+        for z in range(nodes):
+            for j in range(4):
+                store_inner(s_ref, d_ref, None, c, z, j, displacement_ref[c, z, chunk_of(j), :])
+            k = (c * nodes + z) // 2
+            halo = halo_rows(above_ref[k], below_ref[k], z % 2)
+            store_inner(s_ref, d_ref, None, c, z, 4, halo)
+
+
+def own_rows_kernel(
+    domain, displacement_ref, above_ref, below_ref, heating_ref, materials_ref, metals_ref, tables_ref,
+    s_ref, d_ref, lame_ref, shear_ref, thermal_ref, own_ref, next_ref,
+):
+    assemble(displacement_ref, above_ref, below_ref, s_ref, d_ref)
+    layers, row_cells, col_cells = heating_ref.shape
+    first_x, first_y = first_cell(row_cells, col_cells)
+    valid = [inside(first_x + 8 * j + sublanes_of(), first_y + lanes_of(), *domain) for j in range(4)]
+    cell_refs = (lame_ref, shear_ref, thermal_ref)
+
+    def properties(l, carry):
+        tables = load_tables(tables_ref)
+        for j in range(4):
+            rows = chunk_of(j)
+            values = cell_properties(
+                tables, materials_ref[l, rows, :].astype(jnp.float32), metals_ref[l, rows, :],
+                metals_ref[layers + l, rows, :], heating_ref[l, rows, :], valid[j],
+            )
+            for ref, value in zip(cell_refs, values):
+                ref[l, rows, :] = value
+        return carry
+
+    lax.fori_loop(0, layers, properties, 0)
+    inner_forces(s_ref, d_ref, cell_refs, own_ref, next_ref, 4)
+
+
+def halo_rows_kernel(
+    domain, displacement_ref, above_ref, below_ref, strip_ref, first_ref, second_ref,
+    metal_above_ref, metal_below_ref, tables_ref, s_ref, d_ref,
+    lame_in, shear_in, thermal_in, own_ref, next_ref,
+    lame_ref, shear_ref, thermal_ref, weight_ref, v_out, s_out, d_out, v_strip, s_strip, d_strip,
+    cell_strip_ref, halo_lame, halo_shear, halo_thermal, halo_own, halo_next,
+):
+    nodes, row_cells, col_cells = displacement_ref.shape[1:]
+    layers = nodes - 1
+    sub = sublanes_of()
+    first_x, first_y = first_cell(row_cells, col_cells)
+    halo_x = jnp.where(sub < HALO, sub + row_cells, sub - 8)
+    valid = inside(first_x + halo_x, first_y + lanes_of(), *domain)
+    cell_refs = (lame_ref, shear_ref, thermal_ref)
+    halo_refs = (halo_lame, halo_shear, halo_thermal)
+    half = 3 * nodes // 2
+
+    def properties(l, carry):
+        values = cell_properties(
+            load_tables(tables_ref),
+            halo_rows(above_ref[half + l], below_ref[half + l], 1),
+            halo_rows(metal_above_ref[l], metal_below_ref[l], 0),
+            halo_rows(metal_above_ref[l], metal_below_ref[l], 1),
+            halo_rows(above_ref[half + l], below_ref[half + l], 0),
+            valid,
+        )
+        for ref, inner, halo, value in zip(cell_refs, (lame_in, shear_in, thermal_in), halo_refs, values):
+            ref[l, 0:row_cells, :] = inner[l]
+            ref[l, row_cells : row_cells + 8, :] = value
+            halo[l] = value
+        return carry
+
+    lax.fori_loop(0, layers, properties, 0)
+    chunk_forces(s_ref.at[:, :, 32:48], d_ref.at[:, :, 32:48], halo_refs, halo_own, halo_next, slice(0, 8), 0)
+
+    messages = read_messages(first_ref, second_ref)
+    strips = [
+        with_halo(strip_ref[item], item, messages, place=strip_groups()[1])
+        for item in range(3 * nodes + 2 * layers)
+    ]
+    store_strips(
+        s_strip, d_strip, v_strip, [[strips[c * nodes + z] for z in range(nodes)] for c in range(3)]
+    )
+    for k in range(2 * layers):
+        cell_strip_ref[k] = strips[3 * nodes + k]
+
+    diagonals = [cell_diagonals(lame_ref, shear_ref, chunk_of(j)) for j in range(5)]
+    for z in range(nodes):
+        for j in range(5):
+            x = diagonals[j][z]
+            weight_ref[z, chunk_of(j), :] = weight_of(x + row_before(x, diagonals[(j + 4) % 5][z]), z)
+
+    def here(f, c, z, j):
+        return own_ref[f, c, z, chunk_of(j), :] if j < 4 else halo_own[f, c, z]
+
+    def there(f, c, z, j):
+        if j == 0:
+            return row_before(next_ref[f, c, z, 0:8, :], halo_next[f, c, z])
+        if j == 4:
+            return row_before(halo_next[f, c, z], next_ref[f, c, z, 24:32, :])
+        return next_ref[f, c, z, 8 * j - 1 : 8 * j + 7, :]
+
+    for z in range(nodes):
+        for c in range(3):
+            for j in range(5):
+                if j < 4:
+                    v = displacement_ref[c, z, chunk_of(j), :]
+                else:
+                    k = (c * nodes + z) // 2
+                    v = halo_rows(above_ref[k], below_ref[k], z % 2)
+                parts = [here(f, c, z, j) + there(f, c, z, j) for f in range(2)]
+                v = v - weight_ref[z, chunk_of(j), :] * unbalanced(*parts, v, z)
+                store_inner(s_out, d_out, v_out, c, z, j, v)
+
+
 def sweep_kernel(
-    rows_total,
-    columns_total,
-    displacement_ref,
-    heating_ref,
-    materials_ref,
-    above_ref,
-    below_ref,
-    strip_ref,
-    first_ref,
-    second_ref,
-    metals_ref,
-    metal_above_ref,
-    metal_below_ref,
-    metal_strip_ref,
-    metal_first_ref,
-    metal_second_ref,
-    tables_ref,
-    settled_ref,
-    imbalance_ref,
-    v_ref,
-    s_ref,
-    d_ref,
-    own_ref,
-    next_ref,
-    lame_ref,
-    shear_ref,
-    thermal_ref,
-    weight_ref,
-    cell_strip_ref,
+    domain, lame_ref, shear_ref, thermal_ref, weight_ref, v_in, s_in, d_in, v_strip_in, s_strip_in,
+    d_strip_in, cell_strip_ref, metal_strip_ref, metal_first_ref, metal_second_ref, tables_ref,
+    settled_ref, imbalance_ref,
+    v_ref, s_ref, d_ref, own_ref, next_ref, v_strip, s_strip, d_strip, own_strip, next_strip,
+    lame_strip, shear_strip, thermal_strip, weight_strip,
 ):
-    nodes = displacement_ref.shape[1]
+    nodes, row_cells, col_cells = settled_ref.shape[1:]
     layers = nodes - 1
-    row_cells, col_cells = displacement_ref.shape[2:]
-    lane, sub = lanes_of(), sublanes_of()
+    sub, lane = sublanes_of(), lanes_of()
     group, place = strip_groups()
-
-    def next_group(x):
-        return jnp.where(lane < 4 * GROUP, roll_lanes(x, -GROUP), roll_lanes(x, 4 * GROUP))
-
-    def previous_group(x):
-        return jnp.where(lane >= GROUP, roll_lanes(x, GROUP), roll_lanes(x, -4 * GROUP))
-
-    def store_nodes(zs, layers_of):
-        edges = []
-        for z, v in zip(zs, layers_of):
-            edge = jnp.zeros((8, 128), jnp.float32)
+    cell_refs = (lame_ref, shear_ref, thermal_ref)
+    strip_refs = (lame_strip, shear_strip, thermal_strip)
+
+    first_x, first_y = first_cell(row_cells, col_cells)
+    strip_x = jnp.where(group < 4, 8 * group + sub, jnp.where(sub < HALO, sub + row_cells, sub - 8))
+    strip_y = jnp.where(place < 12, place + (col_cells - 8), place - 16)
+    valid = inside(first_x + strip_x, first_y + strip_y, *domain) & (group < 5)
+    messages = read_messages(metal_first_ref, metal_second_ref)
+    metals = [with_halo(metal_strip_ref[k], k, messages, place) for k in range(2 * layers)]
+    tables = load_tables(tables_ref)
+    for l in range(layers):
+        values = cell_properties(
+            tables, cell_strip_ref[layers + l], metals[l], metals[layers + l], cell_strip_ref[l], valid
+        )
+        for ref, value in zip(strip_refs, values):
+            ref[l] = value
+    diagonals = cell_diagonals(lame_strip, shear_strip, slice(0, 8))
+    before = previous_rows(diagonals)
+    for z in range(nodes):
+        weight_strip[z] = weight_of(diagonals[z] + row_before(diagonals[z], before[z]), z)
+
+    cases = [(c, z) for c in range(3) for z in range(nodes)]
+
+    def strip_parts():
+        before = previous_rows([next_strip[f, c, z] for c, z in cases for f in range(2)])
+        return [
+            [own_strip[f, c, z] + row_before(next_strip[f, c, z], before[2 * k + f]) for f in range(2)]
+            for k, (c, z) in enumerate(cases)
+        ]
+
+    def relax_strips(v_from):
+        relaxed = []
+        for (c, z), parts in zip(cases, strip_parts()):
+            v = v_from[c, z]
+            relaxed.append(v - weight_strip[z] * unbalanced(*parts, v, z))
+        store_strips(
+            s_strip, d_strip, v_strip, [relaxed[c * nodes : (c + 1) * nodes] for c in range(3)]
+        )
+
+    def inner_parts(c, z, j):
+        parts = []
+        for f in range(2):
+            if j == 0:
+                there = row_before(next_ref[f, c, z, 0:8, :], next_ref[f, c, z, 32:40, :])
+            else:
+                there = next_ref[f, c, z, 8 * j - 1 : 8 * j + 7, :]
+            parts.append(own_ref[f, c, z, chunk_of(j), :] + there)
+        return parts
+
+    strip_forces(s_strip_in, d_strip_in, strip_refs, own_strip, next_strip)
+    relax_strips(v_strip_in)
+
+    v_now, s_now, d_now = v_in, s_in, d_in
+    for _ in range(ITERS - 1):
+        strip_forces(s_strip, d_strip, strip_refs, own_strip, next_strip)
+        inner_forces(s_now, d_now, cell_refs, own_ref, next_ref, 5)
+        relax_strips(v_strip)
+        for z in range(nodes):
             for c in range(3):
-                for j in (5, 0, 1, 2, 3, 4):
-                    x = v[c][j]
-                    after = roll_lanes(x, -1)
-                    pair, diff = x + after, after - x
-                    v_ref[c, z, 8 * j : 8 * j + 8, :] = x
-                    start = 8 * j if j < 5 else 48
-                    s_ref[c, z, start : start + 8, :] = pair
-                    d_ref[c, z, start : start + 8, :] = diff
-                    if j == 0:
-                        s_ref[c, z, 40:48, :] = pair
-                        d_ref[c, z, 40:48, :] = diff
-                    if j == 5:
-                        edge = jnp.where(sub == 2 * c, roll_rows(pair, 2 * c), edge)
-                        edge = jnp.where(sub == 2 * c + 1, roll_rows(diff, 2 * c + 1), edge)
-            edges.append(edge)
-        edges = [next_group(edge) for edge in edges]
-        for z, edge in zip(zs, edges):
-            for c in range(3):
-                s_ref[c, z, 56:64, :] = roll_rows(edge, -2 * c)
-                d_ref[c, z, 56:64, :] = roll_rows(edge, -2 * c - 1)
-
-    messages = read_messages(first_ref, second_ref)
-    metal_messages = read_messages(metal_first_ref, metal_second_ref)
-    tile = []
-    for z in range(nodes):
-        layer = []
-        for c in range(3):
-            k = (c * nodes + z) // 2
-            item = c * nodes + z
-            layer.append(
-                [displacement_ref[c, z, 8 * j : 8 * j + 8, :] for j in range(4)]
-                + [halo_rows(above_ref[k], below_ref[k], z % 2)]
-                + [with_halo(strip_ref[item], item, messages, place)]
-            )
-        tile.append(layer)
-    store_nodes(range(nodes), tile)
-    for k in range(2 * layers):
-        item = 3 * nodes + k
-        cell_strip_ref[k] = with_halo(strip_ref[item], item, messages, place)
-    for k in range(2 * layers):
-        cell_strip_ref[2 * layers + k] = with_halo(metal_strip_ref[k], k, metal_messages, place)
-
-    first_x = lax.axis_index("row") * row_cells
-    first_y = lax.axis_index("col") * col_cells
-    last_x = rows_total - 1
-    last_y = columns_total - 1
-
-    def inside(x, y):
-        return (x >= 0) & (x < last_x) & (y >= 0) & (y < last_y)
-
-    valid = []
-    for j in range(4):
-        valid.append(inside(first_x + 8 * j + sub, first_y + lane))
-    halo_x = jnp.where(sub < HALO, sub + row_cells, sub - 8)
-    valid.append(inside(first_x + halo_x, first_y + lane))
-    strip_x = jnp.where(group < 4, 8 * group + sub, halo_x)
-    strip_y = jnp.where(place < 12, place + (col_cells - 8), place - 16)
-    valid.append(inside(first_x + strip_x, first_y + strip_y) & (group < 5))
-    codes = tables_ref.shape[1]
-    half = 3 * nodes // 2
-
-    def properties(l, _):
-        tables = [[tables_ref[t, code] for code in range(codes)] for t in range(3)]
-        for j in range(6):
-            if j < 4:
-                rows = slice(8 * j, 8 * j + 8)
-                heat = heating_ref[l, rows, :]
-                material = materials_ref[l, rows, :].astype(jnp.float32)
-                copper = metals_ref[l, rows, :]
-                solder = metals_ref[layers + l, rows, :]
-            elif j == 4:
-                heat = halo_rows(above_ref[half + l], below_ref[half + l], 0)
-                material = halo_rows(above_ref[half + l], below_ref[half + l], 1)
-                copper = halo_rows(metal_above_ref[l], metal_below_ref[l], 0)
-                solder = halo_rows(metal_above_ref[l], metal_below_ref[l], 1)
-            else:
-                heat = cell_strip_ref[l]
-                material = cell_strip_ref[layers + l]
-                copper = cell_strip_ref[2 * layers + l]
-                solder = cell_strip_ref[3 * layers + l]
-            lame, shear, thermal = cell_properties(tables, material, copper, solder, heat, valid[j])
-            lame_ref[l, 8 * j : 8 * j + 8, :] = lame
-            shear_ref[l, 8 * j : 8 * j + 8, :] = shear
-            thermal_ref[l, 8 * j : 8 * j + 8, :] = thermal
-        return 0
-
-    lax.fori_loop(0, layers, properties, 0)
-
-    def shifted_in(zs, fields):
-        edges = []
-        for z in zs:
-            edge = jnp.zeros((8, 128), jnp.float32)
-            for k, (f, c) in enumerate(fields):
-                next_ref[f, c, z, 0:8, :] = next_ref[f, c, z, 40:48, :]
-                last = next_ref[f, c, z, 56:64, :]
-                edge = jnp.where(sub == k, roll_rows(last, k - 7), edge)
-            edges.append(edge)
-        edges = [previous_group(edge) for edge in edges]
-        for z, edge in zip(zs, edges):
-            for k, (f, c) in enumerate(fields):
-                next_ref[f, c, z, 48:56, :] = roll_rows(edge, 7 - k)
-
-    def before(f, c, z, j):
-        start = 7 + 8 * j + (8 if j == 5 else 0)
-        return next_ref[f, c, z, start : start + 8, :]
-
-    for j in range(6):
-        previous = jnp.zeros((8, 128), jnp.float32)
-        rows = slice(8 * j, 8 * j + 8)
-        start = 8 + 8 * j + (8 if j == 5 else 0)
-        for z in range(nodes):
-            total = previous
-            if z < layers:
-                term = lame_ref[z, rows, :] + (4.0 + 8.0 * hourglass_gain) * shear_ref[z, rows, :]
-                total = total + term
-                previous = term
-            total = total + roll_lanes(total, 1)
-            own_ref[0, 0, z, rows, :] = total
-            next_ref[0, 0, z, start : start + 8, :] = total
-
-    shifted_in(range(nodes), [(0, 0)])
-    for z in range(nodes):
-        spring = spring_stiffness if z == 0 else 0.0
-        for j in range(6):
-            rows = slice(8 * j, 8 * j + 8)
-            diagonal = own_ref[0, 0, z, rows, :] + before(0, 0, z, j) + spring
-            some = diagonal > 0.0
-            weight_ref[z, rows, :] = jnp.where(
-                some, relaxation / jnp.where(some, diagonal, 1.0), 0.0
-            )
-
-    def forces():
-        def chunk(j, _):
-            rows = pl.ds(pl.multiple_of(8 * j, 8), 8)
-            extra = jnp.where(j == 5, 8, 0)
-            offset = pl.multiple_of(8 * j + extra, 8)
-            start = pl.multiple_of(8 * j + extra + 8, 8)
-            low = in_plane(s_ref, d_ref, 0, offset)
-            carried = None
-            for z in range(nodes):
-                below = above = None
-                if z < layers:
-                    high = in_plane(s_ref, d_ref, z + 1, offset)
-                    below, above = cell_forces(
-                        low, high, lame_ref[z, rows, :], shear_ref[z, rows, :], thermal_ref[z, rows, :]
-                    )
-                    low = high
-                for c in range(3):
-                    if carried is None:
-                        terms = below[c]
-                    elif below is None:
-                        terms = carried[c]
-                    else:
-                        terms = [a + b for a, b in zip(below[c], carried[c])]
-                    parts = scatter_in_plane(terms)
-                    for f in range(2):
-                        own_ref[f, c, z, rows, :] = parts[f]
-                        next_ref[f, c, z, pl.ds(start, 8), :] = parts[2 + f]
-                carried = above
-            return 0
-
-        lax.fori_loop(0, 6, chunk, 0)
-
-    every = [(f, c) for c in range(3) for f in range(2)]
-
-    def unbalanced(c, z, j, v):
-        here, there = (own_ref[f, c, z, 8 * j : 8 * j + 8, :] + before(f, c, z, j) for f in range(2))
-        total = here + roll_lanes(there, 1)
-        return total + jnp.where(z == 0, spring_stiffness, 0.0) * v
-
-    def nodes_of(c, z, j):
-        return v_ref[c, z, 8 * j : 8 * j + 8, :]
-
-    def sweep(_, carry):
-        forces()
-
-        def update(block, _):
-            zs = [block * BATCH + i for i in range(BATCH)]
-            shifted_in(zs, every)
-            relaxed = []
-            for z in zs:
-                weight = [weight_ref[z, 8 * j : 8 * j + 8, :] for j in range(6)]
-                relaxed.append([])
-                for c in range(3):
-                    v = [nodes_of(c, z, j) for j in range(6)]
-                    relaxed[-1].append([v[j] - weight[j] * unbalanced(c, z, j, v[j]) for j in range(6)])
-            store_nodes(zs, relaxed)
-            return 0
-
-        return lax.fori_loop(0, nodes // BATCH, update, carry)
-
-    lax.fori_loop(0, ITERS, sweep, 0)
-    forces()
+                for j in range(5):
+                    v = v_now[c, z, chunk_of(j), :]
+                    v = v - weight_ref[z, chunk_of(j), :] * unbalanced(*inner_parts(c, z, j), v, z)
+                    store_inner(s_ref, d_ref, v_ref, c, z, j, v)
+        v_now, s_now, d_now = v_ref, s_ref, d_ref
+
+    strip_forces(s_strip, d_strip, strip_refs, own_strip, next_strip)
+    inner_forces(s_now, d_now, cell_refs, own_ref, next_ref, 5)
 
     def joined(strip):
         return jnp.where(place < 8, strip, roll_lanes(strip, -8))
@@ -573,24 +655,19 @@
     def merged(inner, strip, k):
         return jnp.where(edge_lane, roll_lanes(strip, col_cells - 8 - GROUP * k), inner)
 
-    def finish(block, _):
-        zs = [block * BATCH + i for i in range(BATCH)]
-        shifted_in(zs, every)
-        cases = [(c, z) for z in zs for c in range(3)]
-        strips = [nodes_of(c, z, 5) for c, z in cases]
-        residuals = [-unbalanced(c, z, 5, strip) for (c, z), strip in zip(cases, strips)]
-        strips = [joined(x) for x in strips]
-        residuals = [joined(x) for x in residuals]
-        for (c, z), strip, strip_residual in zip(cases, strips, residuals):
-            for j in range(4):
-                v = nodes_of(c, z, j)
-                settled_ref[c, z, 8 * j : 8 * j + 8, :] = merged(v, strip, j)
-                imbalance_ref[c, z, 8 * j : 8 * j + 8, :] = merged(
-                    -unbalanced(c, z, j, v), strip_residual, j
-                )
-        return 0
-
-    lax.fori_loop(0, nodes // BATCH, finish, 0)
+    strips = [v_strip[c, z] for c, z in cases]
+    residuals = [
+        -unbalanced(*parts, v, z) for (c, z), v, parts in zip(cases, strips, strip_parts())
+    ]
+    strips = [joined(x) for x in strips]
+    residuals = [joined(x) for x in residuals]
+    for (c, z), strip, residual in zip(cases, strips, residuals):
+        for j in range(4):
+            v = v_now[c, z, chunk_of(j), :]
+            settled_ref[c, z, chunk_of(j), :] = merged(v, strip, j)
+            imbalance_ref[c, z, chunk_of(j), :] = merged(
+                -unbalanced(*inner_parts(c, z, j), v, z), residual, j
+            )
 
 
 def exchange_rows(edges):
@@ -662,6 +739,7 @@
     )(displacement, heating, materials, above, below)
     first, second = exchange_columns(to_first, to_second)
 
+    inner_nodes = f32(3, nodes, row_cells + 16, col_cells)
     arrived, first, second = lax.optimization_barrier((arrived, first, second))
     metals, *metal_edges = pl.pallas_call(
         functools.partial(unpack_kernel, paired, block_cols),
@@ -673,6 +751,21 @@
         name="unpack_blocks",
     )(arrived)
     metal_above, metal_below = exchange_rows(metal_edges)
+
+    inner_nodes = f32(3, nodes, row_cells + 16, col_cells)
+    domain = (columns * col_cells, lax.axis_size("row") * row_cells)
+    cells = f32(layers, row_cells, col_cells)
+    parts = f32(2, 3, nodes, row_cells, col_cells)
+    s_start, d_start, lame, shear, thermal, own, after = pl.pallas_call(
+        functools.partial(own_rows_kernel, domain),
+        out_shape=[inner_nodes] * 2 + [cells] * 3 + [parts] * 2,
+        in_specs=[in_vmem] * 7,
+        out_specs=[in_vmem] * 7,
+        compiler_params=roomy,
+        name="own_rows",
+    )(displacement, above, below, heating, materials, metals, tables)
+    metal_above, metal_below, own = lax.optimization_barrier((metal_above, metal_below, own))
+
     metal_messages = pl.cdiv(2 * layers, PER_MESSAGE)
     metal_strips, to_first, to_second = pl.pallas_call(
         metal_strips_kernel,
@@ -684,31 +777,43 @@
     )(metals, metal_above, metal_below)
     metal_first, metal_second = exchange_columns(to_first, to_second)
 
+    all_rows = row_cells + 8
+    strip_nodes = f32(3, nodes, 8, 128), f32(3, nodes, 16, 128), f32(3, nodes, 16, 128)
+    *state, cell_strips = pl.pallas_call(
+        functools.partial(halo_rows_kernel, domain),
+        out_shape=[f32(layers, all_rows, col_cells)] * 3
+        + [f32(nodes, all_rows, col_cells), f32(3, nodes, all_rows, col_cells)]
+        + [inner_nodes] * 2
+        + [*strip_nodes, f32(2 * layers, 8, 128)],
+        in_specs=[in_vmem] * 16,
+        out_specs=[in_vmem] * 11,
+        scratch_shapes=[pltpu.VMEM((layers, 8, 128), jnp.float32)] * 3
+        + [pltpu.VMEM((2, 3, nodes, 8, 128), jnp.float32)] * 2,
+        compiler_params=roomy,
+        name="halo_rows",
+    )(
+        displacement, above, below, strips, first, second, metal_above, metal_below, tables,
+        s_start, d_start, lame, shear, thermal, own, after,
+    )
+
     return pl.pallas_call(
-        functools.partial(
-            sweep_kernel, lax.axis_size("row") * row_cells, columns * col_cells
-        ),
+        functools.partial(sweep_kernel, domain),
         out_shape=[f32(*displacement.shape)] * 2,
         in_specs=[in_vmem] * 15,
         out_specs=[in_vmem] * 2,
         scratch_shapes=[
-            pltpu.VMEM((3, nodes, 48, 128), jnp.float32),
-            pltpu.VMEM((3, nodes, 64, 128), jnp.float32),
-            pltpu.VMEM((3, nodes, 64, 128), jnp.float32),
-            pltpu.VMEM((2, 3, nodes, 48, 128), jnp.float32),
-            pltpu.VMEM((2, 3, nodes, 64, 128), jnp.float32),
-            pltpu.VMEM((layers, 48, 128), jnp.float32),
-            pltpu.VMEM((layers, 48, 128), jnp.float32),
-            pltpu.VMEM((layers, 48, 128), jnp.float32),
-            pltpu.VMEM((nodes, 48, 128), jnp.float32),
-            pltpu.VMEM((4 * layers, 8, 128), jnp.float32),
+            pltpu.VMEM(shape, jnp.float32)
+            for shape in (
+                (3, nodes, all_rows, 128), (3, nodes, all_rows + 8, 128), (3, nodes, all_rows + 8, 128),
+                (2, 3, nodes, all_rows, 128), (2, 3, nodes, all_rows, 128),
+                (3, nodes, 8, 128), (3, nodes, 16, 128), (3, nodes, 16, 128),
+                (2, 3, nodes, 8, 128), (2, 3, nodes, 8, 128),
+                (layers, 8, 128), (layers, 8, 128), (layers, 8, 128), (nodes, 8, 128),
+            )
         ],
         compiler_params=roomy,
         name="sweeps",
-    )(
-        displacement, heating, materials, above, below, strips, first, second,
-        metals, metal_above, metal_below, metal_strips, metal_first, metal_second, tables,
-    )
+    )(*state, cell_strips, metal_strips, metal_first, metal_second, tables)
 
 
 def solution(mesh):

time: 49 us -> 45.7 us (0.933)
  waiting for transfers between devices: 11.4 us -> 7.74 us
  Pallas kernels: 17.8 us -> 18.5 us
    ppermute x2, waiting for transfers between devices: 6.3 us -> 4.45 us  [exchange_rows(): other = lax.ppermute(edges[0], 'row', [(0, 1), (1, 0)])]
    ppermute x4, waiting for transfers between devices: 5.06 us -> 3.29 us  [exchange_columns(): return (lax.ppermute(first, 'col', one), lax.ppermute(second, 'col', two))]
    pallas_call x1 -> x3, Pallas kernels: 12.8 us -> 13.4 us  [the longest x1 9.59 us: body(): pl.pallas_call(functools.partial(sweep_kernel, domain), out_shape=[f32(*d...]
  transfers between devices with their start and end apart: 7 -> 7, of which waited for: 4 -> 3; matrix products, arithmetic and copies ran while one was open for 0% -> 0% of each run, Pallas kernels for 3% -> 11%
where the time goes in v3:
time: 45.7 us; the launch traced here: 45.5 us
  Pallas kernels  18.5 us (40%)
  starting transfers between devices  18.4 us (40%)
  waiting for transfers between devices  7.74 us (17%)
  between operations  0.81 us (2%)
    pallas_call x1, Pallas kernels, body(): pl.pallas_call(functools.partial(sweep_kernel, domain), out_shape=[f32(*d...  9.59 us
    ppermute x4, starting transfers between devices, exchange_columns(): return (lax.ppermute(first, 'col', one), lax.ppermute(second, 'col', two))  8.45 us
    all_to_all x1, starting transfers between devices, body(): lax.all_to_all(packed, 'col', split_axis=0, concat_axis=0, tiled=True)  7.36 us
    ppermute x2, waiting for transfers between devices, exchange_rows(): other = lax.ppermute(edges[0], 'row', [(0, 1), (1, 0)])  4.45 us
    ppermute x4, waiting for transfers between devices, exchange_columns(): return (lax.ppermute(first, 'col', one), lax.ppermute(second, 'col', two))  3.29 us
    ppermute x2, starting transfers between devices, exchange_rows(): other = lax.ppermute(edges[0], 'row', [(0, 1), (1, 0)])  2.58 us
    pallas_call x1, Pallas kernels, body(): pl.pallas_call(functools.partial(pack_kernel, tile_blocks, columns, block...  2.38 us
    pallas_call x1, Pallas kernels, body(): pl.pallas_call(functools.partial(own_rows_kernel, domain), out_shape=[inn...  2.09 us
  transfers between devices with their start and end apart: 7, of which 3 were waited for; matrix products, arithmetic and copies ran while one was open for 0% of the time, Pallas kernels for 11%

profile of v3, /device:TPU:1, one launch (start us, length us, event | category | flops | bytes accessed | tf_op | source)
XLA Modules:
  0.0 45.5 jit_solution(15161070000582114545)
XLA Ops:
  0.6 0.0 copy-start.1
  0.6 0.0 copy-start.3
  0.7 0.0 copy-start.4
  0.7 0.0 copy-start.5
  0.7 0.0 copy-start
  0.7 0.0 copy-start.2
  0.7 2.4 %pack_blocks.1 = f32[64,16,128]{2,1,0:T(8,128)} custom-call(s32[1,64]{1,0:T(1,128)} %target_hbm.1, f32[64,1920]{1,0:T(8,128)} %bitcast.1), custom_call_target="tpu_custom_call" | custom-call | tf_op jit(solution)/shard_map/pack_blocks/pallas_call | solution.py:705
  3.1 7.4 %all-to-all-start = ((f32[64,16,128]{2,1,0:T(8,128)}), f32[64,16,128]{2,1,0:T(8,128)S(1)}, u32[]{:S(2)}, u32[]{:S(2)}) async-start(f32[64,16,128]{2,1,0:T(8,128)} %pack_blocks.1), calls=%async_computation | async-start | bytes 1048576 | tf_op jit(solution)/shard_map/all_to_all | solution.py:718
  10.4 0.0 copy-done.1
  10.4 0.0 copy-done.3
  10.5 0.0 copy-done.4
  10.5 0.0 copy-done.5
  10.5 0.6 %field_edges.1 = (f32[3,8,8,128]{3,2,1,0:T(8,128)S(1)}, f32[39,8,128]{2,1,0:T(8,128)S(1)}) custom-call(f32[3,16,32,128]{3,2,1,0:T(8,128)S(1)} %copy-done, f32[15,32,128]{2,1,0:T(8,128)S(1)} %copy-done.1, s32[15,32,128]{2,1,0:T(8,128)S(1)} %copy-done.2, f32[8]{0:T(128)S(1)} %copy-done.3, f32[8]{0:T(128)S(1)} %copy-done.4, f32[8]{0:T(128)S(1)} %copy-done.5), custom_call_target="tpu_custom_call" | custom-call | tf_op jit(solution)/shard_map/field_edges/pallas_call | solution.py:721
  11.1 1.3 %collective-permute-start = (f32[39,8,128]{2,1,0:T(8,128)S(1)}, f32[39,8,128]{2,1,0:T(8,128)S(1)}, u32[]{:S(2)}, u32[]{:S(2)}) collective-permute-start(f32[39,8,128]{2,1,0:T(8,128)S(1)} %get-tuple-element.36), channel_id=1, source_target_pairs={{0,16},{16,0},{1,17},{17,1},{2,18},{18,2},{3,19},{19,3},{4,20},{20... | collective-permute-start | bytes 479240 | tf_op jit(solution)/shard_map/ppermute | solution.py:676
  12.4 4.4 %collective-permute-done.above_ref.below_ref = f32[39,8,128]{2,1,0:T(8,128)S(1)} collective-permute-done((f32[39,8,128]{2,1,0:T(8,128)S(1)}, f32[39,8,128]{2,1,0:T(8,128)S(1)}, u32[]{:S(2)}, u32[]{:S(2)}) %collective-permute-start) | collective-permute-done | bytes 159776 | tf_op jit(solution)/shard_map/ppermute | solution.py:676
  16.9 0.7 %field_strips.1 = (f32[78,8,128]{2,1,0:T(8,128)S(1)}, f32[13,8,128]{2,1,0:T(8,128)S(1)}, f32[13,8,128]{2,1,0:T(8,128)S(1)}) custom-call(f32[3,16,32,128]{3,2,1,0:T(8,128)S(1)} %copy-done, f32[15,32,128]{2,1,0:T(8,128)S(1)} %copy-done.1, s32[15,32,128]{2,1,0:T(8,128)S(1)} %copy-done.2, f32[39,8,128]{2,1,0:T(8,128)S(1)} %collective-permute-done.above_ref.below_ref, ...), custom_call_target="tpu_custom_call" | custom-call | tf_op jit(solution)/shard_map/field_strips/pallas_call | solution.py:732
  17.6 0.9 %collective-permute-start.1 = (f32[13,8,128]{2,1,0:T(8,128)S(1)}, f32[13,8,128]{2,1,0:T(8,128)S(1)}, u32[]{:S(2)}, u32[]{:S(2)}) collective-permute-start(f32[13,8,128]{2,1,0:T(8,128)S(1)} %get-tuple-element.38), channel_id=1, source_target_pairs={{0,1},{1,0},{2,3},{3,2},{4,5},{5,4},{6,7},{7,6},{8,9},{9,8},{10,11... | collective-permute-start | bytes 159752 | tf_op jit(solution)/shard_map/ppermute | solution.py:691
  18.5 3.2 %collective-permute-start.2 = (f32[13,8,128]{2,1,0:T(8,128)S(1)}, f32[13,8,128]{2,1,0:T(8,128)S(1)}, u32[]{:S(2)}, u32[]{:S(2)}) collective-permute-start(f32[13,8,128]{2,1,0:T(8,128)S(1)} %get-tuple-element.39), channel_id=1, source_target_pairs={{0,0},{1,2},{2,1},{3,4},{4,3},{5,6},{6,5},{7,8},{8,7},{9,10},{10,9... | collective-permute-start | bytes 159752 | tf_op jit(solution)/shard_map/ppermute | solution.py:691
  21.7 0.0 collective-permute-done.1.first_ref
  21.7 3.0 %collective-permute-done.2.second_ref = f32[13,8,128]{2,1,0:T(8,128)S(1)} collective-permute-done((f32[13,8,128]{2,1,0:T(8,128)S(1)}, f32[13,8,128]{2,1,0:T(8,128)S(1)}, u32[]{:S(2)}, u32[]{:S(2)}) %collective-permute-start.2) | collective-permute-done | bytes 53280 | tf_op jit(solution)/shard_map/ppermute | solution.py:691
  24.7 0.0 all-to-all-done.arrived_ref
  24.7 1.0 %unpack_blocks.1 = (f32[30,32,128]{2,1,0:T(8,128)S(1)}, f32[15,8,128]{2,1,0:T(8,128)S(1)}) custom-call(f32[64,16,128]{2,1,0:T(8,128)S(1)} %all-to-all-done.arrived_ref), custom_call_target="tpu_custom_call" | custom-call | tf_op jit(solution)/shard_map/unpack_blocks/pallas_call | solution.py:744
  25.7 1.3 %collective-permute-start.3 = (f32[15,8,128]{2,1,0:T(8,128)S(1)}, f32[15,8,128]{2,1,0:T(8,128)S(1)}, u32[]{:S(2)}, u32[]{:S(2)}) collective-permute-start(f32[15,8,128]{2,1,0:T(8,128)S(1)} %get-tuple-element.43), channel_id=1, source_target_pairs={{0,16},{16,0},{1,17},{17,1},{2,18},{18,2},{3,19},{19,3},{4,20},{20... | collective-permute-start | bytes 184328 | tf_op jit(solution)/shard_map/ppermute | solution.py:676
  27.0 2.1 %own_rows.1 = (f32[3,16,48,128]{3,2,1,0:T(8,128)S(1)}, f32[3,16,48,128]{3,2,1,0:T(8,128)S(1)}, f32[15,32,128]{2,1,0:T(8,128)S(1)}, f32[15,32,128]{2,1,0:T(8,128)...) custom-call(f32[3,16,32,128]{3,2,1,0:T(8,128)S(1)} %copy-done, ...), custom_call_target="tpu_custom_call" | custom-call | tf_op jit(solution)/shard_map/own_rows/pallas_call | solution.py:759
  29.1 0.0 collective-permute-done.3.metal_above_ref.metal_below_ref.above_ref.below_ref
  29.1 0.4 metal_strips.1
  29.5 1.3 %collective-permute-start.4 = (f32[5,8,128]{2,1,0:T(8,128)S(1)}, f32[5,8,128]{2,1,0:T(8,128)S(1)}, u32[]{:S(2)}, u32[]{:S(2)}) collective-permute-start(f32[5,8,128]{2,1,0:T(8,128)S(1)} %get-tuple-element.68), channel_id=1, source_target_pairs={{0,1},{1,0},{2,3},{3,2},{4,5},{5,4},{6,7},{7,6},{8,9},{9,8},{10,11... | collective-permute-start | bytes 61448 | tf_op jit(solution)/shard_map/ppermute | solution.py:691
  30.8 3.1 %collective-permute-start.5 = (f32[5,8,128]{2,1,0:T(8,128)S(1)}, f32[5,8,128]{2,1,0:T(8,128)S(1)}, u32[]{:S(2)}, u32[]{:S(2)}) collective-permute-start(f32[5,8,128]{2,1,0:T(8,128)S(1)} %get-tuple-element.69), channel_id=1, source_target_pairs={{0,0},{1,2},{2,1},{3,4},{4,3},{5,6},{6,5},{7,8},{8,7},{9,10},{10,9... | collective-permute-start | bytes 61448 | tf_op jit(solution)/shard_map/ppermute | solution.py:691
  33.8 1.8 %halo_rows.1 = (f32[15,40,128]{2,1,0:T(8,128)S(1)}, f32[15,40,128]{2,1,0:T(8,128)S(1)}, f32[15,40,128]{2,1,0:T(8,128)S(1)}, f32[16,40,128]{2,1,0:T(8,128)S(1)}, ...) custom-call(f32[3,16,32,128]{3,2,1,0:T(8,128)S(1)} %copy-done, ...), custom_call_target="tpu_custom_call" | custom-call | tf_op jit(solution)/shard_map/halo_rows/pallas_call | solution.py:782
  35.6 0.0 collective-permute-done.4.metal_first_ref
  35.6 0.2 collective-permute-done.5.metal_second_ref
  35.9 9.6 %sweeps.1 = (f32[3,16,32,128]{3,2,1,0:T(8,128)}, f32[3,16,32,128]{3,2,1,0:T(8,128)}) custom-call(f32[15,40,128]{2,1,0:T(8,128)S(1)} %get-tuple-element.56.lame_ref, f32[15,40,128]{2,1,0:T(8,128)S(1)} %get-tuple-element.57.shear_ref, f32[15,40,128]{2,1,0:T(8,128)S(1)} %get-tuple-element.58.thermal_ref, f32[16,40,128]{2,1,0:T(8,128)S(1)} %get-tuple-element.59.weight_ref, ...), custom_call_target="tpu_custom_call" | custom-call | tf_op jit(solution)/shard_map/sweeps/pallas_call | solution.py:799
  (2 shorter events, 0.0 us)
Async XLA Ops:
  0.6 9.8 %copy-start.1 = (f32[15,32,128]{2,1,0:T(8,128)S(1)}, f32[15,32,128]{2,1,0:T(8,128)}, u32[]{:S(2)}) copy-start(f32[15,32,128]{2,1,0:T(8,128)} %heating_ref.5) | copy-start | bytes 737284
  0.6 9.8 %copy-start.3 = (f32[8]{0:T(128)S(1)}, f32[8]{0:T(128)}, u32[]{:S(2)}) copy-start(f32[8]{0:T(128)} %modulus_ref.1) | copy-start | bytes 100
  0.7 9.8 %copy-start.4 = (f32[8]{0:T(128)S(1)}, f32[8]{0:T(128)}, u32[]{:S(2)}) copy-start(f32[8]{0:T(128)} %poisson_ref.1) | copy-start | bytes 100
  0.7 9.8 %copy-start.5 = (f32[8]{0:T(128)S(1)}, f32[8]{0:T(128)}, u32[]{:S(2)}) copy-start(f32[8]{0:T(128)} %expansion_ref.1) | copy-start | bytes 100
  0.7 9.8 %copy-start = (f32[3,16,32,128]{3,2,1,0:T(8,128)S(1)}, f32[3,16,32,128]{3,2,1,0:T(8,128)}, u32[]{:S(2)}) copy-start(f32[3,16,32,128]{3,2,1,0:T(8,128)} %displacement_ref.7) | copy-start | bytes 2359300
  0.7 9.8 %copy-start.2 = (s32[15,32,128]{2,1,0:T(8,128)S(1)}, s32[15,32,128]{2,1,0:T(8,128)}, u32[]{:S(2)}) copy-start(s32[15,32,128]{2,1,0:T(8,128)} %materials_ref.5) | copy-start | bytes 737284
  3.1 21.6 %all-to-all-start = ((f32[64,16,128]{2,1,0:T(8,128)}), f32[64,16,128]{2,1,0:T(8,128)S(1)}, u32[]{:S(2)}, u32[]{:S(2)}) async-start(f32[64,16,128]{2,1,0:T(8,128)} %pack_blocks.1), calls=%async_computation | async-start | bytes 1048576 | tf_op jit(solution)/shard_map/all_to_all | solution.py:718
  11.1 5.7 %collective-permute-start = (f32[39,8,128]{2,1,0:T(8,128)S(1)}, f32[39,8,128]{2,1,0:T(8,128)S(1)}, u32[]{:S(2)}, u32[]{:S(2)}) collective-permute-start(f32[39,8,128]{2,1,0:T(8,128)S(1)} %get-tuple-element.36), channel_id=1, source_target_pairs={{0,16},{16,0},{1,17},{17,1},{2,18},{18,2},{3,19},{19,3},{4,20},{20... | collective-permute-start | bytes 479240 | tf_op jit(solution)/shard_map/ppermute | solution.py:676
  17.6 4.1 %collective-permute-start.1 = (f32[13,8,128]{2,1,0:T(8,128)S(1)}, f32[13,8,128]{2,1,0:T(8,128)S(1)}, u32[]{:S(2)}, u32[]{:S(2)}) collective-permute-start(f32[13,8,128]{2,1,0:T(8,128)S(1)} %get-tuple-element.38), channel_id=1, source_target_pairs={{0,1},{1,0},{2,3},{3,2},{4,5},{5,4},{6,7},{7,6},{8,9},{9,8},{10,11... | collective-permute-start | bytes 159752 | tf_op jit(solution)/shard_map/ppermute | solution.py:691
  18.5 6.2 %collective-permute-start.2 = (f32[13,8,128]{2,1,0:T(8,128)S(1)}, f32[13,8,128]{2,1,0:T(8,128)S(1)}, u32[]{:S(2)}, u32[]{:S(2)}) collective-permute-start(f32[13,8,128]{2,1,0:T(8,128)S(1)} %get-tuple-element.39), channel_id=1, source_target_pairs={{0,0},{1,2},{2,1},{3,4},{4,3},{5,6},{6,5},{7,8},{8,7},{9,10},{10,9... | collective-permute-start | bytes 159752 | tf_op jit(solution)/shard_map/ppermute | solution.py:691
  25.7 3.4 %collective-permute-start.3 = (f32[15,8,128]{2,1,0:T(8,128)S(1)}, f32[15,8,128]{2,1,0:T(8,128)S(1)}, u32[]{:S(2)}, u32[]{:S(2)}) collective-permute-start(f32[15,8,128]{2,1,0:T(8,128)S(1)} %get-tuple-element.43), channel_id=1, source_target_pairs={{0,16},{16,0},{1,17},{17,1},{2,18},{18,2},{3,19},{19,3},{4,20},{20... | collective-permute-start | bytes 184328 | tf_op jit(solution)/shard_map/ppermute | solution.py:676
  29.5 6.1 %collective-permute-start.4 = (f32[5,8,128]{2,1,0:T(8,128)S(1)}, f32[5,8,128]{2,1,0:T(8,128)S(1)}, u32[]{:S(2)}, u32[]{:S(2)}) collective-permute-start(f32[5,8,128]{2,1,0:T(8,128)S(1)} %get-tuple-element.68), channel_id=1, source_target_pairs={{0,1},{1,0},{2,3},{3,2},{4,5},{5,4},{6,7},{7,6},{8,9},{9,8},{10,11... | collective-permute-start | bytes 61448 | tf_op jit(solution)/shard_map/ppermute | solution.py:691
  30.8 5.1 %collective-permute-start.5 = (f32[5,8,128]{2,1,0:T(8,128)S(1)}, f32[5,8,128]{2,1,0:T(8,128)S(1)}, u32[]{:S(2)}, u32[]{:S(2)}) collective-permute-start(f32[5,8,128]{2,1,0:T(8,128)S(1)} %get-tuple-element.69), channel_id=1, source_target_pairs={{0,0},{1,2},{2,1},{3,4},{4,3},{5,6},{6,5},{7,8},{8,7},{9,10},{10,9... | collective-permute-start | bytes 61448 | tf_op jit(solution)/shard_map/ppermute | solution.py:691

commit v4 on v3

--- a/solution.py
+++ b/solution.py
@@ -119,10 +119,13 @@
             swapped = list(tiles)
             for i in range(8):
                 if i & bit == 0:
-                    swapped[i] = jnp.where(stay, tiles[i], roll_lanes(tiles[i + bit], BY * bit))
-                    swapped[i + bit] = jnp.where(
-                        stay, roll_lanes(tiles[i], -BY * bit), tiles[i + bit]
-                    )
+                    moving = jnp.where(stay, tiles[i + bit], tiles[i])
+                    if bit == 4:
+                        moving = roll_lanes(moving, 4 * BY)
+                    else:
+                        moving = jnp.take_along_axis(moving, lane ^ (BY * bit), axis=1)
+                    swapped[i] = jnp.where(stay, tiles[i], moving)
+                    swapped[i + bit] = jnp.where(stay, moving, tiles[i + bit])
             tiles = swapped
         for g in range(8):
             half, a = divmod(g, BX)
@@ -273,10 +276,13 @@
     shear = inverse * (0.5 - nu)
     thermal = (3.0 * lame + 2.0 * shear) * grow * heating
     zero = jnp.zeros((8, 128), jnp.float32)
+    valid_shear = jnp.where(valid, shear * (1.0 / 16.0), zero)
     return (
         jnp.where(valid, lame * (1.0 / 16.0), zero),
-        jnp.where(valid, shear * (1.0 / 16.0), zero),
+        valid_shear,
         jnp.where(valid, thermal * 0.25, zero),
+        valid_shear + valid_shear,
+        (2.0 * hourglass_gain) * valid_shear,
     )
 
 
@@ -289,16 +295,14 @@
     return faces
 
 
-def cell_forces(low, high, lame, shear, thermal):
+def cell_forces(low, high, lame, shear, thermal, twice, weight):
     grad_x = [high[c][2] + low[c][2] for c in range(3)]
     grad_y = [high[c][1] + low[c][1] for c in range(3)]
     grad_z = [high[c][0] - low[c][0] for c in range(3)]
-    weight = (2.0 * hourglass_gain) * shear
-    double = shear + shear
     normal = lame * (grad_x[0] + grad_y[1] + grad_z[2]) - thermal
-    xx = normal + double * grad_x[0]
-    yy = normal + double * grad_y[1]
-    zz = normal + double * grad_z[2]
+    xx = normal + twice * grad_x[0]
+    yy = normal + twice * grad_y[1]
+    zz = normal + twice * grad_z[2]
     xy = shear * (grad_y[0] + grad_x[1])
     xz = shear * (grad_z[0] + grad_x[2])
     yz = shear * (grad_z[1] + grad_y[2])
@@ -307,16 +311,14 @@
     for c in range(3):
         one = weight * (high[c][1] - low[c][1])
         two = weight * (high[c][2] - low[c][2])
-        three = weight * (high[c][3] + low[c][3])
-        four = weight * (high[c][3] - low[c][3])
         sx, sy, sz = along[0][c], along[1][c], along[2][c]
-        below.append((sx - two, sy - one, three - four, -sz))
-        above.append((sx + two, sy + one, three + four, sz))
+        below.append((sx - two, sy - one, -sz))
+        above.append((sx + two, sy + one, sz))
     return below, above
 
 
 def scatter_in_plane(terms):
-    diff_pair, pair_diff, diff_diff, pair_pair = terms
+    diff_pair, pair_diff, pair_pair, diff_diff = terms
     own_pair, next_pair = pair_pair - diff_pair, pair_pair + diff_pair
     own_diff, next_diff = pair_diff - diff_diff, pair_diff + diff_diff
     return own_pair - own_diff, own_pair + own_diff, next_pair - next_diff, next_pair + next_diff
@@ -325,13 +327,16 @@
 def chunk_forces(s_ref, d_ref, cell_refs, own_ref, next_ref, rows, offset):
     nodes = own_ref.shape[2]
     low = in_plane(s_ref, d_ref, 0, offset)
-    carried = None
+    carried = modes = None
     for z in range(nodes):
-        below = above = None
+        below = above = high = None
+        both = modes
         if z < nodes - 1:
             high = in_plane(s_ref, d_ref, z + 1, offset)
-            below, above = cell_forces(low, high, *(ref[z, rows, :] for ref in cell_refs))
-            low = high
+            cell = [ref[z, rows, :] for ref in cell_refs]
+            below, above = cell_forces(low, high, *cell)
+            modes = cell[-1] + cell[-1]
+            both = modes if both is None else both + modes
         for c in range(3):
             if carried is None:
                 terms = below[c]
@@ -339,11 +344,11 @@
                 terms = carried[c]
             else:
                 terms = [a + b for a, b in zip(below[c], carried[c])]
-            parts = scatter_in_plane(terms)
+            parts = scatter_in_plane((*terms, both * low[c][3]))
             for f in range(2):
                 own_ref[f, c, z, rows, :] = parts[f]
                 next_ref[f, c, z, rows, :] = parts[2 + f]
-        carried = above
+        carried, low = above, high
 
 
 def inner_forces(s_ref, d_ref, cell_refs, own_ref, next_ref, count):
@@ -469,13 +474,13 @@
 
 def own_rows_kernel(
     domain, displacement_ref, above_ref, below_ref, heating_ref, materials_ref, metals_ref, tables_ref,
-    s_ref, d_ref, lame_ref, shear_ref, thermal_ref, own_ref, next_ref,
+    s_ref, d_ref, lame_ref, shear_ref, thermal_ref, twice_ref, mode_ref, own_ref, next_ref,
 ):
     assemble(displacement_ref, above_ref, below_ref, s_ref, d_ref)
     layers, row_cells, col_cells = heating_ref.shape
     first_x, first_y = first_cell(row_cells, col_cells)
     valid = [inside(first_x + 8 * j + sublanes_of(), first_y + lanes_of(), *domain) for j in range(4)]
-    cell_refs = (lame_ref, shear_ref, thermal_ref)
+    cell_refs = (lame_ref, shear_ref, thermal_ref, twice_ref, mode_ref)
 
     def properties(l, carry):
         tables = load_tables(tables_ref)
@@ -496,9 +501,10 @@
 def halo_rows_kernel(
     domain, displacement_ref, above_ref, below_ref, strip_ref, first_ref, second_ref,
     metal_above_ref, metal_below_ref, tables_ref, s_ref, d_ref,
-    lame_in, shear_in, thermal_in, own_ref, next_ref,
-    lame_ref, shear_ref, thermal_ref, weight_ref, v_out, s_out, d_out, v_strip, s_strip, d_strip,
-    cell_strip_ref, halo_lame, halo_shear, halo_thermal, halo_own, halo_next,
+    lame_in, shear_in, thermal_in, twice_in, mode_in, own_ref, next_ref,
+    lame_ref, shear_ref, thermal_ref, twice_ref, mode_ref, weight_ref, v_out, s_out, d_out,
+    v_strip, s_strip, d_strip, cell_strip_ref, own_out, next_out,
+    halo_lame, halo_shear, halo_thermal, halo_twice, halo_mode, halo_own, halo_next,
 ):
     nodes, row_cells, col_cells = displacement_ref.shape[1:]
     layers = nodes - 1
@@ -506,8 +512,9 @@
     first_x, first_y = first_cell(row_cells, col_cells)
     halo_x = jnp.where(sub < HALO, sub + row_cells, sub - 8)
     valid = inside(first_x + halo_x, first_y + lanes_of(), *domain)
-    cell_refs = (lame_ref, shear_ref, thermal_ref)
-    halo_refs = (halo_lame, halo_shear, halo_thermal)
+    cell_refs = (lame_ref, shear_ref, thermal_ref, twice_ref, mode_ref)
+    inner_refs = (lame_in, shear_in, thermal_in, twice_in, mode_in)
+    halo_refs = (halo_lame, halo_shear, halo_thermal, halo_twice, halo_mode)
     half = 3 * nodes // 2
 
     def properties(l, carry):
@@ -519,7 +526,7 @@
             halo_rows(above_ref[half + l], below_ref[half + l], 0),
             valid,
         )
-        for ref, inner, halo, value in zip(cell_refs, (lame_in, shear_in, thermal_in), halo_refs, values):
+        for ref, inner, halo, value in zip(cell_refs, inner_refs, halo_refs, values):
             ref[l, 0:row_cells, :] = inner[l]
             ref[l, row_cells : row_cells + 8, :] = value
             halo[l] = value
@@ -567,20 +574,24 @@
                 v = v - weight_ref[z, chunk_of(j), :] * unbalanced(*parts, v, z)
                 store_inner(s_out, d_out, v_out, c, z, j, v)
 
+    inner_forces(s_out, d_out, cell_refs, own_out, next_out, 5)
+
 
 def sweep_kernel(
-    domain, lame_ref, shear_ref, thermal_ref, weight_ref, v_in, s_in, d_in, v_strip_in, s_strip_in,
-    d_strip_in, cell_strip_ref, metal_strip_ref, metal_first_ref, metal_second_ref, tables_ref,
-    settled_ref, imbalance_ref,
+    domain, lame_ref, shear_ref, thermal_ref, twice_ref, mode_ref, weight_ref, v_in, s_in, d_in,
+    v_strip_in, s_strip_in, d_strip_in, cell_strip_ref, own_in, next_in, metal_strip_ref,
+    metal_first_ref, metal_second_ref, tables_ref,
+    settled_out, imbalance_out,
+    settled_ref, imbalance_ref, written,
     v_ref, s_ref, d_ref, own_ref, next_ref, v_strip, s_strip, d_strip, own_strip, next_strip,
-    lame_strip, shear_strip, thermal_strip, weight_strip,
+    lame_strip, shear_strip, thermal_strip, twice_strip, mode_strip, weight_strip,
 ):
     nodes, row_cells, col_cells = settled_ref.shape[1:]
     layers = nodes - 1
     sub, lane = sublanes_of(), lanes_of()
     group, place = strip_groups()
-    cell_refs = (lame_ref, shear_ref, thermal_ref)
-    strip_refs = (lame_strip, shear_strip, thermal_strip)
+    cell_refs = (lame_ref, shear_ref, thermal_ref, twice_ref, mode_ref)
+    strip_refs = (lame_strip, shear_strip, thermal_strip, twice_strip, mode_strip)
 
     first_x, first_y = first_cell(row_cells, col_cells)
     strip_x = jnp.where(group < 4, 8 * group + sub, jnp.where(sub < HALO, sub + row_cells, sub - 8))
@@ -618,56 +629,71 @@
             s_strip, d_strip, v_strip, [relaxed[c * nodes : (c + 1) * nodes] for c in range(3)]
         )
 
-    def inner_parts(c, z, j):
+    def inner_parts(own, after, c, z, j):
         parts = []
         for f in range(2):
             if j == 0:
-                there = row_before(next_ref[f, c, z, 0:8, :], next_ref[f, c, z, 32:40, :])
+                there = row_before(after[f, c, z, 0:8, :], after[f, c, z, 32:40, :])
             else:
-                there = next_ref[f, c, z, 8 * j - 1 : 8 * j + 7, :]
-            parts.append(own_ref[f, c, z, chunk_of(j), :] + there)
+                there = after[f, c, z, 8 * j - 1 : 8 * j + 7, :]
+            parts.append(own[f, c, z, chunk_of(j), :] + there)
         return parts
 
     strip_forces(s_strip_in, d_strip_in, strip_refs, own_strip, next_strip)
     relax_strips(v_strip_in)
 
-    v_now, s_now, d_now = v_in, s_in, d_in
-    for _ in range(ITERS - 1):
+    v_now, s_now, d_now, own_now, next_now = v_in, s_in, d_in, own_in, next_in
+    for sweep in range(1, ITERS):
         strip_forces(s_strip, d_strip, strip_refs, own_strip, next_strip)
-        inner_forces(s_now, d_now, cell_refs, own_ref, next_ref, 5)
+        if sweep > 1:
+            inner_forces(s_now, d_now, cell_refs, own_ref, next_ref, 5)
+            own_now, next_now = own_ref, next_ref
         relax_strips(v_strip)
         for z in range(nodes):
             for c in range(3):
                 for j in range(5):
                     v = v_now[c, z, chunk_of(j), :]
-                    v = v - weight_ref[z, chunk_of(j), :] * unbalanced(*inner_parts(c, z, j), v, z)
+                    parts = inner_parts(own_now, next_now, c, z, j)
+                    v = v - weight_ref[z, chunk_of(j), :] * unbalanced(*parts, v, z)
                     store_inner(s_ref, d_ref, v_ref, c, z, j, v)
         v_now, s_now, d_now = v_ref, s_ref, d_ref
 
+    def joined(strip):
+        return jnp.where(place < 8, strip, roll_lanes(strip, -8))
+
+    edge_lane = (lane < HALO) | (lane >= col_cells - HALO)
+
+    def merged(inner, strip, k):
+        return jnp.where(edge_lane, roll_lanes(strip, col_cells - 8 - GROUP * k), inner)
+
+    def write_out(c):
+        copies = [
+            pltpu.make_async_copy(settled_ref.at[c], settled_out.at[c], written.at[2 * c]),
+            pltpu.make_async_copy(imbalance_ref.at[c], imbalance_out.at[c], written.at[2 * c + 1]),
+        ]
+        for copy in copies:
+            copy.start()
+        return copies
+
     strip_forces(s_strip, d_strip, strip_refs, own_strip, next_strip)
     inner_forces(s_now, d_now, cell_refs, own_ref, next_ref, 5)
-
-    def joined(strip):
-        return jnp.where(place < 8, strip, roll_lanes(strip, -8))
-
-    edge_lane = (lane < HALO) | (lane >= col_cells - HALO)
-
-    def merged(inner, strip, k):
-        return jnp.where(edge_lane, roll_lanes(strip, col_cells - 8 - GROUP * k), inner)
-
     strips = [v_strip[c, z] for c, z in cases]
     residuals = [
         -unbalanced(*parts, v, z) for (c, z), v, parts in zip(cases, strips, strip_parts())
     ]
     strips = [joined(x) for x in strips]
     residuals = [joined(x) for x in residuals]
+    copies = []
     for (c, z), strip, residual in zip(cases, strips, residuals):
         for j in range(4):
             v = v_now[c, z, chunk_of(j), :]
+            parts = inner_parts(own_ref, next_ref, c, z, j)
             settled_ref[c, z, chunk_of(j), :] = merged(v, strip, j)
-            imbalance_ref[c, z, chunk_of(j), :] = merged(
-                -unbalanced(*inner_parts(c, z, j), v, z), residual, j
-            )
+            imbalance_ref[c, z, chunk_of(j), :] = merged(-unbalanced(*parts, v, z), residual, j)
+        if z == nodes - 1:
+            copies += write_out(c)
+    for copy in copies:
+        copy.wait()
 
 
 def exchange_rows(edges):
@@ -756,11 +782,11 @@
     domain = (columns * col_cells, lax.axis_size("row") * row_cells)
     cells = f32(layers, row_cells, col_cells)
     parts = f32(2, 3, nodes, row_cells, col_cells)
-    s_start, d_start, lame, shear, thermal, own, after = pl.pallas_call(
+    s_start, d_start, *own_cells, own, after = pl.pallas_call(
         functools.partial(own_rows_kernel, domain),
-        out_shape=[inner_nodes] * 2 + [cells] * 3 + [parts] * 2,
+        out_shape=[inner_nodes] * 2 + [cells] * 5 + [parts] * 2,
         in_specs=[in_vmem] * 7,
-        out_specs=[in_vmem] * 7,
+        out_specs=[in_vmem] * 9,
         compiler_params=roomy,
         name="own_rows",
     )(displacement, above, below, heating, materials, metals, tables)
@@ -779,41 +805,41 @@
 
     all_rows = row_cells + 8
     strip_nodes = f32(3, nodes, 8, 128), f32(3, nodes, 16, 128), f32(3, nodes, 16, 128)
-    *state, cell_strips = pl.pallas_call(
+    all_parts = f32(2, 3, nodes, all_rows, col_cells)
+    state = pl.pallas_call(
         functools.partial(halo_rows_kernel, domain),
-        out_shape=[f32(layers, all_rows, col_cells)] * 3
+        out_shape=[f32(layers, all_rows, col_cells)] * 5
         + [f32(nodes, all_rows, col_cells), f32(3, nodes, all_rows, col_cells)]
         + [inner_nodes] * 2
-        + [*strip_nodes, f32(2 * layers, 8, 128)],
-        in_specs=[in_vmem] * 16,
-        out_specs=[in_vmem] * 11,
-        scratch_shapes=[pltpu.VMEM((layers, 8, 128), jnp.float32)] * 3
+        + [*strip_nodes, f32(2 * layers, 8, 128), all_parts, all_parts],
+        in_specs=[in_vmem] * 18,
+        out_specs=[in_vmem] * 15,
+        scratch_shapes=[pltpu.VMEM((layers, 8, 128), jnp.float32)] * 5
         + [pltpu.VMEM((2, 3, nodes, 8, 128), jnp.float32)] * 2,
         compiler_params=roomy,
         name="halo_rows",
     )(
         displacement, above, below, strips, first, second, metal_above, metal_below, tables,
-        s_start, d_start, lame, shear, thermal, own, after,
+        s_start, d_start, *own_cells, own, after,
     )
 
+    scratch = [displacement.shape] * 2 + [
+        (3, nodes, all_rows, 128), (3, nodes, all_rows + 8, 128), (3, nodes, all_rows + 8, 128),
+        (2, 3, nodes, all_rows, 128), (2, 3, nodes, all_rows, 128),
+        (3, nodes, 8, 128), (3, nodes, 16, 128), (3, nodes, 16, 128),
+        (2, 3, nodes, 8, 128), (2, 3, nodes, 8, 128),
+    ] + [(layers, 8, 128)] * 5 + [(nodes, 8, 128)]
+    scratch = [pltpu.VMEM(shape, jnp.float32) for shape in scratch]
+    scratch.insert(2, pltpu.SemaphoreType.DMA((6,)))
     return pl.pallas_call(
         functools.partial(sweep_kernel, domain),
         out_shape=[f32(*displacement.shape)] * 2,
-        in_specs=[in_vmem] * 15,
-        out_specs=[in_vmem] * 2,
-        scratch_shapes=[
-            pltpu.VMEM(shape, jnp.float32)
-            for shape in (
-                (3, nodes, all_rows, 128), (3, nodes, all_rows + 8, 128), (3, nodes, all_rows + 8, 128),
-                (2, 3, nodes, all_rows, 128), (2, 3, nodes, all_rows, 128),
-                (3, nodes, 8, 128), (3, nodes, 16, 128), (3, nodes, 16, 128),
-                (2, 3, nodes, 8, 128), (2, 3, nodes, 8, 128),
-                (layers, 8, 128), (layers, 8, 128), (layers, 8, 128), (nodes, 8, 128),
-            )
-        ],
+        in_specs=[in_vmem] * 19,
+        out_specs=[in_hbm] * 2,
+        scratch_shapes=scratch,
         compiler_params=roomy,
         name="sweeps",
-    )(*state, cell_strips, metal_strips, metal_first, metal_second, tables)
+    )(*state, metal_strips, metal_first, metal_second, tables)
 
 
 def solution(mesh):

time: 45.7 us -> 44.2 us (0.967)
  Pallas kernels: 18.5 us -> 17.1 us
    pallas_call x1, Pallas kernels: 9.59 us -> 7.6 us  [body(): pl.pallas_call(functools.partial(sweep_kernel, domain), out_shape=[f32(*d...]
    pallas_call x1, Pallas kernels: 1.76 us -> 2.87 us  [body(): pl.pallas_call(functools.partial(halo_rows_kernel, domain), out_shape=[f3...]
  transfers between devices with their start and end apart: 7 -> 7, of which waited for: 3 -> 2; matrix products, arithmetic and copies ran while one was open for 0% -> 0% of each run, Pallas kernels for 11% -> 14%
where the time goes in v4:
time: 44.2 us; the launch traced here: 43.9 us
  starting transfers between devices  18.5 us (42%)
  Pallas kernels  17.1 us (39%)
  waiting for transfers between devices  7.5 us (17%)
  between operations  0.82 us (2%)
    ppermute x4, starting transfers between devices, exchange_columns(): return (lax.ppermute(first, 'col', one), lax.ppermute(second, 'col', two))  8.53 us
    pallas_call x1, Pallas kernels, body(): pl.pallas_call(functools.partial(sweep_kernel, domain), out_shape=[f32(*d...  7.6 us
    all_to_all x1, starting transfers between devices, body(): lax.all_to_all(packed, 'col', split_axis=0, concat_axis=0, tiled=True)  7.36 us
    ppermute x2, waiting for transfers between devices, exchange_rows(): other = lax.ppermute(edges[0], 'row', [(0, 1), (1, 0)])  4.45 us
    ppermute x4, waiting for transfers between devices, exchange_columns(): return (lax.ppermute(first, 'col', one), lax.ppermute(second, 'col', two))  3.05 us
    pallas_call x1, Pallas kernels, body(): pl.pallas_call(functools.partial(halo_rows_kernel, domain), out_shape=[f3...  2.87 us
    ppermute x2, starting transfers between devices, exchange_rows(): other = lax.ppermute(edges[0], 'row', [(0, 1), (1, 0)])  2.58 us
    pallas_call x1, Pallas kernels, body(): pl.pallas_call(functools.partial(pack_kernel, tile_blocks, columns, block...  2.35 us
  transfers between devices with their start and end apart: 7, of which 2 were waited for; matrix products, arithmetic and copies ran while one was open for 0% of the time, Pallas kernels for 14%

profile of v4, /device:TPU:1, one launch (start us, length us, event | category | flops | bytes accessed | tf_op | source)
XLA Modules:
  0.0 43.9 jit_solution(17552662086285189316)
XLA Ops:
  0.6 0.0 copy-start
  0.6 0.0 copy-start.1
  0.7 0.0 copy-start.2
  0.7 0.0 copy-start.5
  0.7 0.0 copy-start.4
  0.7 0.0 copy-start.3
  0.7 2.3 %pack_blocks.1 = f32[64,16,128]{2,1,0:T(8,128)} custom-call(s32[1,64]{1,0:T(1,128)} %target_hbm.1, f32[64,1920]{1,0:T(8,128)} %bitcast.1), custom_call_target="tpu_custom_call" | custom-call | tf_op jit(solution)/shard_map/pack_blocks/pallas_call | solution.py:731
  3.0 7.4 %all-to-all-start = ((f32[64,16,128]{2,1,0:T(8,128)}), f32[64,16,128]{2,1,0:T(8,128)S(1)}, u32[]{:S(2)}, u32[]{:S(2)}) async-start(f32[64,16,128]{2,1,0:T(8,128)} %pack_blocks.1), calls=%async_computation | async-start | bytes 1048576 | tf_op jit(solution)/shard_map/all_to_all | solution.py:744
  10.4 0.0 copy-done
  10.4 0.0 copy-done.1
  10.4 0.0 copy-done.2
  10.4 0.0 copy-done.5
  10.5 0.6 %field_edges.1 = (f32[3,8,8,128]{3,2,1,0:T(8,128)S(1)}, f32[39,8,128]{2,1,0:T(8,128)S(1)}) custom-call(f32[3,16,32,128]{3,2,1,0:T(8,128)S(1)} %copy-done, f32[15,32,128]{2,1,0:T(8,128)S(1)} %copy-done.1, s32[15,32,128]{2,1,0:T(8,128)S(1)} %copy-done.2, f32[8]{0:T(128)S(1)} %copy-done.3, f32[8]{0:T(128)S(1)} %copy-done.4, f32[8]{0:T(128)S(1)} %copy-done.5), custom_call_target="tpu_custom_call" | custom-call | tf_op jit(solution)/shard_map/field_edges/pallas_call | solution.py:747
  11.1 1.3 %collective-permute-start = (f32[39,8,128]{2,1,0:T(8,128)S(1)}, f32[39,8,128]{2,1,0:T(8,128)S(1)}, u32[]{:S(2)}, u32[]{:S(2)}) collective-permute-start(f32[39,8,128]{2,1,0:T(8,128)S(1)} %get-tuple-element.42), channel_id=1, source_target_pairs={{0,16},{16,0},{1,17},{17,1},{2,18},{18,2},{3,19},{19,3},{4,20},{20... | collective-permute-start | bytes 479240 | tf_op jit(solution)/shard_map/ppermute | solution.py:702
  12.4 4.4 %collective-permute-done.above_ref.below_ref = f32[39,8,128]{2,1,0:T(8,128)S(1)} collective-permute-done((f32[39,8,128]{2,1,0:T(8,128)S(1)}, f32[39,8,128]{2,1,0:T(8,128)S(1)}, u32[]{:S(2)}, u32[]{:S(2)}) %collective-permute-start) | collective-permute-done | bytes 159776 | tf_op jit(solution)/shard_map/ppermute | solution.py:702
  16.8 0.7 %field_strips.1 = (f32[78,8,128]{2,1,0:T(8,128)S(1)}, f32[13,8,128]{2,1,0:T(8,128)S(1)}, f32[13,8,128]{2,1,0:T(8,128)S(1)}) custom-call(f32[3,16,32,128]{3,2,1,0:T(8,128)S(1)} %copy-done, f32[15,32,128]{2,1,0:T(8,128)S(1)} %copy-done.1, s32[15,32,128]{2,1,0:T(8,128)S(1)} %copy-done.2, f32[39,8,128]{2,1,0:T(8,128)S(1)} %collective-permute-done.above_ref.below_ref, ...), custom_call_target="tpu_custom_call" | custom-call | tf_op jit(solution)/shard_map/field_strips/pallas_call | solution.py:758
  17.5 0.9 %collective-permute-start.1 = (f32[13,8,128]{2,1,0:T(8,128)S(1)}, f32[13,8,128]{2,1,0:T(8,128)S(1)}, u32[]{:S(2)}, u32[]{:S(2)}) collective-permute-start(f32[13,8,128]{2,1,0:T(8,128)S(1)} %get-tuple-element.44), channel_id=1, source_target_pairs={{0,1},{1,0},{2,3},{3,2},{4,5},{5,4},{6,7},{7,6},{8,9},{9,8},{10,11... | collective-permute-start | bytes 159752 | tf_op jit(solution)/shard_map/ppermute | solution.py:717
  18.5 3.2 %collective-permute-start.2 = (f32[13,8,128]{2,1,0:T(8,128)S(1)}, f32[13,8,128]{2,1,0:T(8,128)S(1)}, u32[]{:S(2)}, u32[]{:S(2)}) collective-permute-start(f32[13,8,128]{2,1,0:T(8,128)S(1)} %get-tuple-element.45), channel_id=1, source_target_pairs={{0,0},{1,2},{2,1},{3,4},{4,3},{5,6},{6,5},{7,8},{8,7},{9,10},{10,9... | collective-permute-start | bytes 159752 | tf_op jit(solution)/shard_map/ppermute | solution.py:717
  21.6 0.0 collective-permute-done.1.first_ref
  21.6 3.0 %collective-permute-done.2.second_ref = f32[13,8,128]{2,1,0:T(8,128)S(1)} collective-permute-done((f32[13,8,128]{2,1,0:T(8,128)S(1)}, f32[13,8,128]{2,1,0:T(8,128)S(1)}, u32[]{:S(2)}, u32[]{:S(2)}) %collective-permute-start.2) | collective-permute-done | bytes 53280 | tf_op jit(solution)/shard_map/ppermute | solution.py:717
  24.7 0.0 all-to-all-done.arrived_ref
  24.7 0.6 %unpack_blocks.1 = (f32[30,32,128]{2,1,0:T(8,128)S(1)}, f32[15,8,128]{2,1,0:T(8,128)S(1)}) custom-call(f32[64,16,128]{2,1,0:T(8,128)S(1)} %all-to-all-done.arrived_ref), custom_call_target="tpu_custom_call" | custom-call | tf_op jit(solution)/shard_map/unpack_blocks/pallas_call | solution.py:770
  25.3 1.3 %collective-permute-start.3 = (f32[15,8,128]{2,1,0:T(8,128)S(1)}, f32[15,8,128]{2,1,0:T(8,128)S(1)}, u32[]{:S(2)}, u32[]{:S(2)}) collective-permute-start(f32[15,8,128]{2,1,0:T(8,128)S(1)} %get-tuple-element.49), channel_id=1, source_target_pairs={{0,16},{16,0},{1,17},{17,1},{2,18},{18,2},{3,19},{19,3},{4,20},{20... | collective-permute-start | bytes 184328 | tf_op jit(solution)/shard_map/ppermute | solution.py:702
  26.6 2.0 %own_rows.1 = (f32[3,16,48,128]{3,2,1,0:T(8,128)S(1)}, f32[3,16,48,128]{3,2,1,0:T(8,128)S(1)}, f32[15,32,128]{2,1,0:T(8,128)S(1)}, f32[15,32,128]{2,1,0:T(8,128)...) custom-call(f32[3,16,32,128]{3,2,1,0:T(8,128)S(1)} %copy-done, ...), custom_call_target="tpu_custom_call" | custom-call | tf_op jit(solution)/shard_map/own_rows/pallas_call | solution.py:785
  28.6 0.0 collective-permute-done.3.metal_above_ref.metal_below_ref.above_ref.below_ref
  28.6 0.4 metal_strips.1
  29.0 1.4 %collective-permute-start.4 = (f32[5,8,128]{2,1,0:T(8,128)S(1)}, f32[5,8,128]{2,1,0:T(8,128)S(1)}, u32[]{:S(2)}, u32[]{:S(2)}) collective-permute-start(f32[5,8,128]{2,1,0:T(8,128)S(1)} %get-tuple-element.80), channel_id=1, source_target_pairs={{0,1},{1,0},{2,3},{3,2},{4,5},{5,4},{6,7},{7,6},{8,9},{9,8},{10,11... | collective-permute-start | bytes 61448 | tf_op jit(solution)/shard_map/ppermute | solution.py:717
  30.4 3.1 %collective-permute-start.5 = (f32[5,8,128]{2,1,0:T(8,128)S(1)}, f32[5,8,128]{2,1,0:T(8,128)S(1)}, u32[]{:S(2)}, u32[]{:S(2)}) collective-permute-start(f32[5,8,128]{2,1,0:T(8,128)S(1)} %get-tuple-element.81), channel_id=1, source_target_pairs={{0,0},{1,2},{2,1},{3,4},{4,3},{5,6},{6,5},{7,8},{8,7},{9,10},{10,9... | collective-permute-start | bytes 61448 | tf_op jit(solution)/shard_map/ppermute | solution.py:717
  33.4 2.9 %halo_rows.1 = (f32[15,40,128]{2,1,0:T(8,128)S(1)}, f32[15,40,128]{2,1,0:T(8,128)S(1)}, f32[15,40,128]{2,1,0:T(8,128)S(1)}, f32[15,40,128]{2,1,0:T(8,128)S(1)}, ...) custom-call(f32[3,16,32,128]{3,2,1,0:T(8,128)S(1)} %copy-done, ...), custom_call_target="tpu_custom_call" | custom-call | tf_op jit(solution)/shard_map/halo_rows/pallas_call | solution.py:809
  36.3 0.0 collective-permute-done.4.metal_first_ref
  36.3 0.0 collective-permute-done.5.metal_second_ref
  36.3 7.6 %sweeps.1 = (f32[3,16,32,128]{3,2,1,0:T(8,128)}, f32[3,16,32,128]{3,2,1,0:T(8,128)}) custom-call(f32[15,40,128]{2,1,0:T(8,128)S(1)} %get-tuple-element.64.lame_ref, f32[15,40,128]{2,1,0:T(8,128)S(1)} %get-tuple-element.65.shear_ref, f32[15,40,128]{2,1,0:T(8,128)S(1)} %get-tuple-element.66.thermal_ref, f32[15,40,128]{2,1,0:T(8,128)S(1)} %get-tuple-element.67.twice_ref, ...), custom_call_target="tpu_custom_call" | custom-call | tf_op jit(solution)/shard_map/sweeps/pallas_call | solution.py:834
  (2 shorter events, 0.0 us)
Async XLA Ops:
  0.6 9.8 %copy-start = (f32[3,16,32,128]{3,2,1,0:T(8,128)S(1)}, f32[3,16,32,128]{3,2,1,0:T(8,128)}, u32[]{:S(2)}) copy-start(f32[3,16,32,128]{3,2,1,0:T(8,128)} %displacement_ref.7) | copy-start | bytes 2359300
  0.6 9.8 %copy-start.1 = (f32[15,32,128]{2,1,0:T(8,128)S(1)}, f32[15,32,128]{2,1,0:T(8,128)}, u32[]{:S(2)}) copy-start(f32[15,32,128]{2,1,0:T(8,128)} %heating_ref.5) | copy-start | bytes 737284
  0.7 9.8 %copy-start.2 = (s32[15,32,128]{2,1,0:T(8,128)S(1)}, s32[15,32,128]{2,1,0:T(8,128)}, u32[]{:S(2)}) copy-start(s32[15,32,128]{2,1,0:T(8,128)} %materials_ref.5) | copy-start | bytes 737284
  0.7 9.8 %copy-start.5 = (f32[8]{0:T(128)S(1)}, f32[8]{0:T(128)}, u32[]{:S(2)}) copy-start(f32[8]{0:T(128)} %expansion_ref.1) | copy-start | bytes 100
  0.7 9.8 %copy-start.4 = (f32[8]{0:T(128)S(1)}, f32[8]{0:T(128)}, u32[]{:S(2)}) copy-start(f32[8]{0:T(128)} %poisson_ref.1) | copy-start | bytes 100
  0.7 9.8 %copy-start.3 = (f32[8]{0:T(128)S(1)}, f32[8]{0:T(128)}, u32[]{:S(2)}) copy-start(f32[8]{0:T(128)} %modulus_ref.1) | copy-start | bytes 100
  3.0 21.6 %all-to-all-start = ((f32[64,16,128]{2,1,0:T(8,128)}), f32[64,16,128]{2,1,0:T(8,128)S(1)}, u32[]{:S(2)}, u32[]{:S(2)}) async-start(f32[64,16,128]{2,1,0:T(8,128)} %pack_blocks.1), calls=%async_computation | async-start | bytes 1048576 | tf_op jit(solution)/shard_map/all_to_all | solution.py:744
  11.1 5.7 %collective-permute-start = (f32[39,8,128]{2,1,0:T(8,128)S(1)}, f32[39,8,128]{2,1,0:T(8,128)S(1)}, u32[]{:S(2)}, u32[]{:S(2)}) collective-permute-start(f32[39,8,128]{2,1,0:T(8,128)S(1)} %get-tuple-element.42), channel_id=1, source_target_pairs={{0,16},{16,0},{1,17},{17,1},{2,18},{18,2},{3,19},{19,3},{4,20},{20... | collective-permute-start | bytes 479240 | tf_op jit(solution)/shard_map/ppermute | solution.py:702
  17.5 4.1 %collective-permute-start.1 = (f32[13,8,128]{2,1,0:T(8,128)S(1)}, f32[13,8,128]{2,1,0:T(8,128)S(1)}, u32[]{:S(2)}, u32[]{:S(2)}) collective-permute-start(f32[13,8,128]{2,1,0:T(8,128)S(1)} %get-tuple-element.44), channel_id=1, source_target_pairs={{0,1},{1,0},{2,3},{3,2},{4,5},{5,4},{6,7},{7,6},{8,9},{9,8},{10,11... | collective-permute-start | bytes 159752 | tf_op jit(solution)/shard_map/ppermute | solution.py:717
  18.5 6.2 %collective-permute-start.2 = (f32[13,8,128]{2,1,0:T(8,128)S(1)}, f32[13,8,128]{2,1,0:T(8,128)S(1)}, u32[]{:S(2)}, u32[]{:S(2)}) collective-permute-start(f32[13,8,128]{2,1,0:T(8,128)S(1)} %get-tuple-element.45), channel_id=1, source_target_pairs={{0,0},{1,2},{2,1},{3,4},{4,3},{5,6},{6,5},{7,8},{8,7},{9,10},{10,9... | collective-permute-start | bytes 159752 | tf_op jit(solution)/shard_map/ppermute | solution.py:717
  25.3 3.3 %collective-permute-start.3 = (f32[15,8,128]{2,1,0:T(8,128)S(1)}, f32[15,8,128]{2,1,0:T(8,128)S(1)}, u32[]{:S(2)}, u32[]{:S(2)}) collective-permute-start(f32[15,8,128]{2,1,0:T(8,128)S(1)} %get-tuple-element.49), channel_id=1, source_target_pairs={{0,16},{16,0},{1,17},{17,1},{2,18},{18,2},{3,19},{19,3},{4,20},{20... | collective-permute-start | bytes 184328 | tf_op jit(solution)/shard_map/ppermute | solution.py:702
  29.0 7.3 %collective-permute-start.4 = (f32[5,8,128]{2,1,0:T(8,128)S(1)}, f32[5,8,128]{2,1,0:T(8,128)S(1)}, u32[]{:S(2)}, u32[]{:S(2)}) collective-permute-start(f32[5,8,128]{2,1,0:T(8,128)S(1)} %get-tuple-element.80), channel_id=1, source_target_pairs={{0,1},{1,0},{2,3},{3,2},{4,5},{5,4},{6,7},{7,6},{8,9},{9,8},{10,11... | collective-permute-start | bytes 61448 | tf_op jit(solution)/shard_map/ppermute | solution.py:717
  30.4 6.0 %collective-permute-start.5 = (f32[5,8,128]{2,1,0:T(8,128)S(1)}, f32[5,8,128]{2,1,0:T(8,128)S(1)}, u32[]{:S(2)}, u32[]{:S(2)}) collective-permute-start(f32[5,8,128]{2,1,0:T(8,128)S(1)} %get-tuple-element.81), channel_id=1, source_target_pairs={{0,0},{1,2},{2,1},{3,4},{4,3},{5,6},{6,5},{7,8},{8,7},{9,10},{10,9... | collective-permute-start | bytes 61448 | tf_op jit(solution)/shard_map/ppermute | solution.py:717

commit v5 on v4

--- a/solution.py
+++ b/solution.py
@@ -312,7 +312,7 @@
         one = weight * (high[c][1] - low[c][1])
         two = weight * (high[c][2] - low[c][2])
         sx, sy, sz = along[0][c], along[1][c], along[2][c]
-        below.append((sx - two, sy - one, -sz))
+        below.append((sx - two, sy - one, sz))
         above.append((sx + two, sy + one, sz))
     return below, above
 
@@ -324,7 +324,7 @@
     return own_pair - own_diff, own_pair + own_diff, next_pair - next_diff, next_pair + next_diff
 
 
-def chunk_forces(s_ref, d_ref, cell_refs, own_ref, next_ref, rows, offset):
+def chunk_forces(s_ref, d_ref, cell_refs, own_ref, next_ref, rows, next_rows, offset, beside=None):
     nodes = own_ref.shape[2]
     low = in_plane(s_ref, d_ref, 0, offset)
     carried = modes = None
@@ -339,29 +339,67 @@
             both = modes if both is None else both + modes
         for c in range(3):
             if carried is None:
-                terms = below[c]
+                terms = (*below[c][:2], -below[c][2])
             elif below is None:
                 terms = carried[c]
             else:
-                terms = [a + b for a, b in zip(below[c], carried[c])]
+                terms = [a + b for a, b in zip(below[c][:2], carried[c])]
+                terms.append(carried[c][2] - below[c][2])
             parts = scatter_in_plane((*terms, both * low[c][3]))
             for f in range(2):
                 own_ref[f, c, z, rows, :] = parts[f]
-                next_ref[f, c, z, rows, :] = parts[2 + f]
+                next_ref[f, c, z, next_rows, :] = parts[2 + f]
         carried, low = above, high
-
-
-def inner_forces(s_ref, d_ref, cell_refs, own_ref, next_ref, count):
+        if beside is not None:
+            beside(z)
+
+
+def inner_forces(s_ref, d_ref, cell_refs, own_ref, next_ref, count, pad=0):
     def chunk(j, carry):
         start = pl.multiple_of(8 * j, 8)
-        chunk_forces(s_ref, d_ref, cell_refs, own_ref, next_ref, pl.ds(start, 8), start)
+        next_rows = pl.ds(pl.multiple_of(8 * j + pad, 8), 8)
+        chunk_forces(s_ref, d_ref, cell_refs, own_ref, next_ref, pl.ds(start, 8), next_rows, start)
         return carry
 
     lax.fori_loop(0, count, chunk, 0)
 
 
-def strip_forces(s_ref, d_ref, cell_refs, own_ref, next_ref):
-    chunk_forces(s_ref, d_ref, cell_refs, own_ref, next_ref, slice(0, 8), 0)
+def strip_forces(s_ref, d_ref, cell_refs, own_ref, next_ref, beside=None):
+    chunk_forces(s_ref, d_ref, cell_refs, own_ref, next_ref, slice(0, 8), slice(8, 16), 0, beside)
+    next_ref.copy_row(15, 7, previous_group)
+
+
+class Rows:
+    def __init__(self, ref, *sizes):
+        self.ref = ref
+        count = 1
+        for size in sizes:
+            count *= size
+        self.count, self.height = count, ref.shape[0] // count
+        self.sizes = sizes
+        self.shape = (*sizes, self.height, 128)
+
+    def rows(self, index):
+        *lead, rows, _ = index
+        slab = 0
+        for size, i in zip(self.sizes, lead):
+            slab = slab * size + i
+        start = slab * self.height
+        if isinstance(rows, slice):
+            return slice(start + rows.start, start + rows.stop)
+        return pl.ds(start + rows.start, rows.size)
+
+    def __getitem__(self, index):
+        return self.ref[self.rows(index), :]
+
+    def __setitem__(self, index, value):
+        self.ref[self.rows(index), :] = value
+
+    def copy_row(self, source, target, change=lambda x: x):
+        for slab in range(0, self.count, 8):
+            first = slab * self.height
+            x = self.ref[pl.ds(first + source, 8, stride=self.height), :]
+            self.ref[pl.ds(first + target, 8, stride=self.height), :] = change(x)
 
 
 def chunk_of(j):
@@ -369,15 +407,18 @@
 
 
 def row_before(x, previous):
-    return jnp.where(sublanes_of() == 0, roll_rows(previous, 1), roll_rows(x, 1))
+    return roll_rows(jnp.where(sublanes_of() == 7, previous, x), 1)
 
 
 def next_group(x):
-    return jnp.where(lanes_of() < 4 * GROUP, roll_lanes(x, -GROUP), roll_lanes(x, 4 * GROUP))
+    lane = lanes_of()
+    from_lane = jnp.where(lane < 4 * GROUP, lane + GROUP, jnp.maximum(lane - 4 * GROUP, 0))
+    return jnp.take_along_axis(x, from_lane, axis=1)
 
 
 def previous_group(x):
-    return jnp.where(lanes_of() >= GROUP, roll_lanes(x, GROUP), roll_lanes(x, -4 * GROUP))
+    lane = lanes_of()
+    return jnp.take_along_axis(x, jnp.where(lane >= GROUP, lane - GROUP, lane + 4 * GROUP), axis=1)
 
 
 def previous_rows(lasts):
@@ -404,24 +445,14 @@
 
 
 def store_strips(s_ref, d_ref, v_ref, strips):
-    edges = []
     after = [[roll_lanes(x, -1) for x in row] for row in strips]
-    packed = []
     for c, row in enumerate(strips):
         for z, x in enumerate(row):
-            pair, diff = x + after[c][z], after[c][z] - x
             v_ref[c, z] = x
-            s_ref[c, z, 0:8, :] = pair
-            d_ref[c, z, 0:8, :] = diff
-            edges += [(s_ref, c, z, pair), (d_ref, c, z, diff)]
-    for first in range(0, len(edges), 8):
-        edge = jnp.zeros((8, 128), jnp.float32)
-        for k, (_, _, _, x) in enumerate(edges[first : first + 8]):
-            edge = jnp.where(sublanes_of() == k, roll_rows(x, k), edge)
-        packed.append(edge)
-    packed = [next_group(edge) for edge in packed]
-    for k, (ref, c, z, _) in enumerate(edges):
-        ref[c, z, 8:16, :] = roll_rows(packed[k // 8], -(k % 8))
+            s_ref[c, z, 0:8, :] = x + after[c][z]
+            d_ref[c, z, 0:8, :] = after[c][z] - x
+    s_ref.copy_row(0, 8, next_group)
+    d_ref.copy_row(0, 8, next_group)
 
 
 def cell_diagonals(lame_ref, shear_ref, rows):
@@ -473,10 +504,26 @@
 
 
 def own_rows_kernel(
-    domain, displacement_ref, above_ref, below_ref, heating_ref, materials_ref, metals_ref, tables_ref,
+    domain, displacement_ref, above_ref, below_ref, strip_ref, first_ref, second_ref,
+    heating_ref, materials_ref, metals_ref, tables_ref,
     s_ref, d_ref, lame_ref, shear_ref, thermal_ref, twice_ref, mode_ref, own_ref, next_ref,
+    v_strip, s_strip, d_strip, cell_strip_ref,
 ):
+    nodes, layers = displacement_ref.shape[1], heating_ref.shape[0]
     assemble(displacement_ref, above_ref, below_ref, s_ref, d_ref)
+
+    s_strip, d_strip = Rows(s_strip, 3, nodes), Rows(d_strip, 3, nodes)
+    messages = read_messages(first_ref, second_ref)
+    strips = [
+        with_halo(strip_ref[item], item, messages, place=strip_groups()[1])
+        for item in range(3 * nodes + 2 * layers)
+    ]
+    store_strips(
+        s_strip, d_strip, v_strip, [[strips[c * nodes + z] for z in range(nodes)] for c in range(3)]
+    )
+    for k in range(2 * layers):
+        cell_strip_ref[k] = strips[3 * nodes + k]
+
     layers, row_cells, col_cells = heating_ref.shape
     first_x, first_y = first_cell(row_cells, col_cells)
     valid = [inside(first_x + 8 * j + sublanes_of(), first_y + lanes_of(), *domain) for j in range(4)]
@@ -499,11 +546,11 @@
 
 
 def halo_rows_kernel(
-    domain, displacement_ref, above_ref, below_ref, strip_ref, first_ref, second_ref,
+    domain, displacement_ref, above_ref, below_ref,
     metal_above_ref, metal_below_ref, tables_ref, s_ref, d_ref,
     lame_in, shear_in, thermal_in, twice_in, mode_in, own_ref, next_ref,
     lame_ref, shear_ref, thermal_ref, twice_ref, mode_ref, weight_ref, v_out, s_out, d_out,
-    v_strip, s_strip, d_strip, cell_strip_ref, own_out, next_out,
+    own_out, next_out,
     halo_lame, halo_shear, halo_thermal, halo_twice, halo_mode, halo_own, halo_next,
 ):
     nodes, row_cells, col_cells = displacement_ref.shape[1:]
@@ -533,18 +580,7 @@
         return carry
 
     lax.fori_loop(0, layers, properties, 0)
-    chunk_forces(s_ref.at[:, :, 32:48], d_ref.at[:, :, 32:48], halo_refs, halo_own, halo_next, slice(0, 8), 0)
-
-    messages = read_messages(first_ref, second_ref)
-    strips = [
-        with_halo(strip_ref[item], item, messages, place=strip_groups()[1])
-        for item in range(3 * nodes + 2 * layers)
-    ]
-    store_strips(
-        s_strip, d_strip, v_strip, [[strips[c * nodes + z] for z in range(nodes)] for c in range(3)]
-    )
-    for k in range(2 * layers):
-        cell_strip_ref[k] = strips[3 * nodes + k]
+    chunk_forces(s_ref.at[:, :, 32:48], d_ref.at[:, :, 32:48], halo_refs, halo_own, halo_next, slice(0, 8), slice(0, 8), 0)
 
     diagonals = [cell_diagonals(lame_ref, shear_ref, chunk_of(j)) for j in range(5)]
     for z in range(nodes):
@@ -574,7 +610,9 @@
                 v = v - weight_ref[z, chunk_of(j), :] * unbalanced(*parts, v, z)
                 store_inner(s_out, d_out, v_out, c, z, j, v)
 
-    inner_forces(s_out, d_out, cell_refs, own_out, next_out, 5)
+    next_out = Rows(next_out, 2, 3, nodes)
+    inner_forces(s_out, d_out, cell_refs, own_out, next_out, 5, 8)
+    next_out.copy_row(47, 7)
 
 
 def sweep_kernel(
@@ -592,6 +630,10 @@
     group, place = strip_groups()
     cell_refs = (lame_ref, shear_ref, thermal_ref, twice_ref, mode_ref)
     strip_refs = (lame_strip, shear_strip, thermal_strip, twice_strip, mode_strip)
+    s_strip, d_strip, s_strip_in, d_strip_in = (
+        Rows(ref, 3, nodes) for ref in (s_strip, d_strip, s_strip_in, d_strip_in)
+    )
+    next_in, next_ref, next_strip = (Rows(ref, 2, 3, nodes) for ref in (next_in, next_ref, next_strip))
 
     first_x, first_y = first_cell(row_cells, col_cells)
     strip_x = jnp.where(group < 4, 8 * group + sub, jnp.where(sub < HALO, sub + row_cells, sub - 8))
@@ -614,10 +656,8 @@
     cases = [(c, z) for c in range(3) for z in range(nodes)]
 
     def strip_parts():
-        before = previous_rows([next_strip[f, c, z] for c, z in cases for f in range(2)])
         return [
-            [own_strip[f, c, z] + row_before(next_strip[f, c, z], before[2 * k + f]) for f in range(2)]
-            for k, (c, z) in enumerate(cases)
+            [own_strip[f, c, z] + next_strip[f, c, z, 7:15, :] for f in range(2)] for c, z in cases
         ]
 
     def relax_strips(v_from):
@@ -630,33 +670,32 @@
         )
 
     def inner_parts(own, after, c, z, j):
-        parts = []
-        for f in range(2):
-            if j == 0:
-                there = row_before(after[f, c, z, 0:8, :], after[f, c, z, 32:40, :])
-            else:
-                there = after[f, c, z, 8 * j - 1 : 8 * j + 7, :]
-            parts.append(own[f, c, z, chunk_of(j), :] + there)
-        return parts
+        return [
+            own[f, c, z, chunk_of(j), :] + after[f, c, z, 8 * j + 7 : 8 * j + 15, :]
+            for f in range(2)
+        ]
 
     strip_forces(s_strip_in, d_strip_in, strip_refs, own_strip, next_strip)
     relax_strips(v_strip_in)
 
-    v_now, s_now, d_now, own_now, next_now = v_in, s_in, d_in, own_in, next_in
+    v_now, own_now, next_now = v_in, own_in, next_in
     for sweep in range(1, ITERS):
-        strip_forces(s_strip, d_strip, strip_refs, own_strip, next_strip)
         if sweep > 1:
-            inner_forces(s_now, d_now, cell_refs, own_ref, next_ref, 5)
+            inner_forces(s_ref, d_ref, cell_refs, own_ref, next_ref, 5, 8)
+            next_ref.copy_row(47, 7)
             own_now, next_now = own_ref, next_ref
-        relax_strips(v_strip)
-        for z in range(nodes):
+
+        def relax_rows(z):
             for c in range(3):
                 for j in range(5):
                     v = v_now[c, z, chunk_of(j), :]
                     parts = inner_parts(own_now, next_now, c, z, j)
                     v = v - weight_ref[z, chunk_of(j), :] * unbalanced(*parts, v, z)
                     store_inner(s_ref, d_ref, v_ref, c, z, j, v)
-        v_now, s_now, d_now = v_ref, s_ref, d_ref
+
+        strip_forces(s_strip, d_strip, strip_refs, own_strip, next_strip, relax_rows)
+        relax_strips(v_strip)
+        v_now = v_ref
 
     def joined(strip):
         return jnp.where(place < 8, strip, roll_lanes(strip, -8))
@@ -666,32 +705,34 @@
     def merged(inner, strip, k):
         return jnp.where(edge_lane, roll_lanes(strip, col_cells - 8 - GROUP * k), inner)
 
-    def write_out(c):
-        copies = [
-            pltpu.make_async_copy(settled_ref.at[c], settled_out.at[c], written.at[2 * c]),
-            pltpu.make_async_copy(imbalance_ref.at[c], imbalance_out.at[c], written.at[2 * c + 1]),
-        ]
-        for copy in copies:
-            copy.start()
-        return copies
-
+    def write_out(ref, out, c, first, count, semaphore):
+        part = pl.ds(first, count)
+        copy = pltpu.make_async_copy(ref.at[c, part], out.at[c, part], written.at[semaphore])
+        copy.start()
+        return copy
+
+    strips = [joined(v_strip[c, z]) for c, z in cases]
+    for (c, z), strip in zip(cases, strips):
+        for j in range(4):
+            settled_ref[c, z, chunk_of(j), :] = merged(v_ref[c, z, chunk_of(j), :], strip, j)
+    copies = [write_out(settled_ref, settled_out, c, 0, nodes, c) for c in range(3)]
     strip_forces(s_strip, d_strip, strip_refs, own_strip, next_strip)
-    inner_forces(s_now, d_now, cell_refs, own_ref, next_ref, 5)
-    strips = [v_strip[c, z] for c, z in cases]
     residuals = [
-        -unbalanced(*parts, v, z) for (c, z), v, parts in zip(cases, strips, strip_parts())
+        joined(-unbalanced(*parts, v_strip[c, z], z)) for (c, z), parts in zip(cases, strip_parts())
     ]
-    strips = [joined(x) for x in strips]
-    residuals = [joined(x) for x in residuals]
-    copies = []
-    for (c, z), strip, residual in zip(cases, strips, residuals):
+    inner_forces(s_ref, d_ref, cell_refs, own_ref, next_ref, 5, 8)
+    next_ref.copy_row(47, 7)
+    half = nodes // 2
+    for (c, z), residual in zip(cases, residuals):
         for j in range(4):
-            v = v_now[c, z, chunk_of(j), :]
+            v = v_ref[c, z, chunk_of(j), :]
             parts = inner_parts(own_ref, next_ref, c, z, j)
-            settled_ref[c, z, chunk_of(j), :] = merged(v, strip, j)
             imbalance_ref[c, z, chunk_of(j), :] = merged(-unbalanced(*parts, v, z), residual, j)
-        if z == nodes - 1:
-            copies += write_out(c)
+        if (z + 1) % half == 0:
+            part = z // half
+            copies.append(
+                write_out(imbalance_ref, imbalance_out, c, part * half, half, 3 + 2 * c + part)
+            )
     for copy in copies:
         copy.wait()
 
@@ -714,7 +755,8 @@
 
     one = [(i, partner(i, i + 1 if i % 2 == 0 else i - 1)) for i in range(count)]
     two = [(i, partner(i, i - 1 if i % 2 == 0 else i + 1)) for i in range(count)]
-    return lax.ppermute(first, "col", one), lax.ppermute(second, "col", two)
+    from_second = lax.ppermute(second, "col", two)
+    return lax.ppermute(first, "col", one), from_second
 
 
 def body(displacement, materials, heating, densities, block_target, modulus, poisson, expansion):
@@ -782,14 +824,16 @@
     domain = (columns * col_cells, lax.axis_size("row") * row_cells)
     cells = f32(layers, row_cells, col_cells)
     parts = f32(2, 3, nodes, row_cells, col_cells)
-    s_start, d_start, *own_cells, own, after = pl.pallas_call(
+    strip_nodes = f32(3, nodes, 8, 128), f32(3 * nodes * 16, 128), f32(3 * nodes * 16, 128)
+    s_start, d_start, *own_cells, own, after, v_strip, s_strip, d_strip, cell_strips = pl.pallas_call(
         functools.partial(own_rows_kernel, domain),
-        out_shape=[inner_nodes] * 2 + [cells] * 5 + [parts] * 2,
-        in_specs=[in_vmem] * 7,
-        out_specs=[in_vmem] * 9,
+        out_shape=[inner_nodes] * 2 + [cells] * 5 + [parts] * 2
+        + [*strip_nodes, f32(2 * layers, 8, 128)],
+        in_specs=[in_vmem] * 10,
+        out_specs=[in_vmem] * 13,
         compiler_params=roomy,
         name="own_rows",
-    )(displacement, above, below, heating, materials, metals, tables)
+    )(displacement, above, below, strips, first, second, heating, materials, metals, tables)
     metal_above, metal_below, own = lax.optimization_barrier((metal_above, metal_below, own))
 
     metal_messages = pl.cdiv(2 * layers, PER_MESSAGE)
@@ -804,33 +848,32 @@
     metal_first, metal_second = exchange_columns(to_first, to_second)
 
     all_rows = row_cells + 8
-    strip_nodes = f32(3, nodes, 8, 128), f32(3, nodes, 16, 128), f32(3, nodes, 16, 128)
-    all_parts = f32(2, 3, nodes, all_rows, col_cells)
-    state = pl.pallas_call(
+    all_parts = f32(2, 3, nodes, all_rows, col_cells), f32(2 * 3 * nodes * (all_rows + 8), col_cells)
+    *state, own, after = pl.pallas_call(
         functools.partial(halo_rows_kernel, domain),
         out_shape=[f32(layers, all_rows, col_cells)] * 5
         + [f32(nodes, all_rows, col_cells), f32(3, nodes, all_rows, col_cells)]
         + [inner_nodes] * 2
-        + [*strip_nodes, f32(2 * layers, 8, 128), all_parts, all_parts],
-        in_specs=[in_vmem] * 18,
-        out_specs=[in_vmem] * 15,
+        + [*all_parts],
+        in_specs=[in_vmem] * 15,
+        out_specs=[in_vmem] * 11,
         scratch_shapes=[pltpu.VMEM((layers, 8, 128), jnp.float32)] * 5
         + [pltpu.VMEM((2, 3, nodes, 8, 128), jnp.float32)] * 2,
         compiler_params=roomy,
         name="halo_rows",
     )(
-        displacement, above, below, strips, first, second, metal_above, metal_below, tables,
+        displacement, above, below, metal_above, metal_below, tables,
         s_start, d_start, *own_cells, own, after,
     )
 
     scratch = [displacement.shape] * 2 + [
         (3, nodes, all_rows, 128), (3, nodes, all_rows + 8, 128), (3, nodes, all_rows + 8, 128),
-        (2, 3, nodes, all_rows, 128), (2, 3, nodes, all_rows, 128),
-        (3, nodes, 8, 128), (3, nodes, 16, 128), (3, nodes, 16, 128),
-        (2, 3, nodes, 8, 128), (2, 3, nodes, 8, 128),
+        (2, 3, nodes, all_rows, 128), (2 * 3 * nodes * (all_rows + 8), 128),
+        (3, nodes, 8, 128), (3 * nodes * 16, 128), (3 * nodes * 16, 128),
+        (2, 3, nodes, 8, 128), (2 * 3 * nodes * 16, 128),
     ] + [(layers, 8, 128)] * 5 + [(nodes, 8, 128)]
     scratch = [pltpu.VMEM(shape, jnp.float32) for shape in scratch]
-    scratch.insert(2, pltpu.SemaphoreType.DMA((6,)))
+    scratch.insert(2, pltpu.SemaphoreType.DMA((9,)))
     return pl.pallas_call(
         functools.partial(sweep_kernel, domain),
         out_shape=[f32(*displacement.shape)] * 2,
@@ -839,7 +882,10 @@
         scratch_shapes=scratch,
         compiler_params=roomy,
         name="sweeps",
-    )(*state, metal_strips, metal_first, metal_second, tables)
+    )(
+        *state, v_strip, s_strip, d_strip, cell_strips, own, after,
+        metal_strips, metal_first, metal_second, tables,
+    )
 
 
 def solution(mesh):

time: 44.2 us -> 43.6 us (0.986)
  no operation moved by 1% of the time
where the time goes in v5:
time: 43.6 us; the launch traced here: 43.3 us
  starting transfers between devices  18.2 us (42%)
  Pallas kernels  16.8 us (39%)
  waiting for transfers between devices  7.5 us (17%)
  between operations  0.82 us (2%)
    all_to_all x1, starting transfers between devices, body(): lax.all_to_all(packed, 'col', split_axis=0, concat_axis=0, tiled=True)  7.36 us
    pallas_call x1, Pallas kernels, body(): pl.pallas_call(functools.partial(sweep_kernel, domain), out_shape=[f32(*d...  7.35 us
    ppermute x2, starting transfers between devices, exchange_columns(): from_second = lax.ppermute(second, 'col', two)  6.24 us
    ppermute x2, waiting for transfers between devices, exchange_rows(): other = lax.ppermute(edges[0], 'row', [(0, 1), (1, 0)])  4.45 us
    ppermute x2, waiting for transfers between devices, exchange_columns(): from_second = lax.ppermute(second, 'col', two)  3.05 us
    ppermute x2, starting transfers between devices, exchange_rows(): other = lax.ppermute(edges[0], 'row', [(0, 1), (1, 0)])  2.58 us
    pallas_call x1, Pallas kernels, body(): pl.pallas_call(functools.partial(halo_rows_kernel, domain), out_shape=[f3...  2.51 us
    pallas_call x1, Pallas kernels, body(): pl.pallas_call(functools.partial(pack_kernel, tile_blocks, columns, block...  2.35 us
  transfers between devices with their start and end apart: 7, of which 2 were waited for; matrix products, arithmetic and copies ran while one was open for 0% of the time, Pallas kernels for 14%

profile of v5, /device:TPU:1, one launch (start us, length us, event | category | flops | bytes accessed | tf_op | source)
XLA Modules:
  0.0 43.3 jit_solution(7619385680929088444)
XLA Ops:
  0.6 0.0 copy-start
  0.6 0.0 copy-start.1
  0.7 0.0 copy-start.2
  0.7 0.0 copy-start.5
  0.7 0.0 copy-start.4
  0.7 2.3 %pack_blocks.1 = f32[64,16,128]{2,1,0:T(8,128)} custom-call(s32[1,64]{1,0:T(1,128)} %target_hbm.1, f32[64,1920]{1,0:T(8,128)} %bitcast.1), custom_call_target="tpu_custom_call" | custom-call | tf_op jit(solution)/shard_map/pack_blocks/pallas_call | solution.py:773
  3.0 7.4 %all-to-all-start = ((f32[64,16,128]{2,1,0:T(8,128)}), f32[64,16,128]{2,1,0:T(8,128)S(1)}, u32[]{:S(2)}, u32[]{:S(2)}) async-start(f32[64,16,128]{2,1,0:T(8,128)} %pack_blocks.1), calls=%async_computation | async-start | bytes 1048576 | tf_op jit(solution)/shard_map/all_to_all | solution.py:786
  10.4 0.0 copy-done.1
  10.4 0.0 copy-done.2
  10.4 0.0 copy-done.5
  10.4 0.0 copy-done.4
  10.5 0.0 copy-done.3
  10.5 0.6 %field_edges.1 = (f32[3,8,8,128]{3,2,1,0:T(8,128)S(1)}, f32[39,8,128]{2,1,0:T(8,128)S(1)}) custom-call(f32[3,16,32,128]{3,2,1,0:T(8,128)S(1)} %copy-done, f32[15,32,128]{2,1,0:T(8,128)S(1)} %copy-done.1, s32[15,32,128]{2,1,0:T(8,128)S(1)} %copy-done.2, f32[8]{0:T(128)S(1)} %copy-done.3, f32[8]{0:T(128)S(1)} %copy-done.4, f32[8]{0:T(128)S(1)} %copy-done.5), custom_call_target="tpu_custom_call" | custom-call | tf_op jit(solution)/shard_map/field_edges/pallas_call | solution.py:789
  11.1 1.3 %collective-permute-start = (f32[39,8,128]{2,1,0:T(8,128)S(1)}, f32[39,8,128]{2,1,0:T(8,128)S(1)}, u32[]{:S(2)}, u32[]{:S(2)}) collective-permute-start(f32[39,8,128]{2,1,0:T(8,128)S(1)} %get-tuple-element.42), channel_id=1, source_target_pairs={{0,16},{16,0},{1,17},{17,1},{2,18},{18,2},{3,19},{19,3},{4,20},{20... | collective-permute-start | bytes 479240 | tf_op jit(solution)/shard_map/ppermute | solution.py:743
  12.4 4.4 %collective-permute-done.above_ref.below_ref = f32[39,8,128]{2,1,0:T(8,128)S(1)} collective-permute-done((f32[39,8,128]{2,1,0:T(8,128)S(1)}, f32[39,8,128]{2,1,0:T(8,128)S(1)}, u32[]{:S(2)}, u32[]{:S(2)}) %collective-permute-start) | collective-permute-done | bytes 159776 | tf_op jit(solution)/shard_map/ppermute | solution.py:743
  16.8 0.7 %field_strips.1 = (f32[78,8,128]{2,1,0:T(8,128)S(1)}, f32[13,8,128]{2,1,0:T(8,128)S(1)}, f32[13,8,128]{2,1,0:T(8,128)S(1)}) custom-call(f32[3,16,32,128]{3,2,1,0:T(8,128)S(1)} %copy-done, f32[15,32,128]{2,1,0:T(8,128)S(1)} %copy-done.1, s32[15,32,128]{2,1,0:T(8,128)S(1)} %copy-done.2, f32[39,8,128]{2,1,0:T(8,128)S(1)} %collective-permute-done.above_ref.below_ref, ...), custom_call_target="tpu_custom_call" | custom-call | tf_op jit(solution)/shard_map/field_strips/pallas_call | solution.py:800
  17.5 0.9 %collective-permute-start.1 = (f32[13,8,128]{2,1,0:T(8,128)S(1)}, f32[13,8,128]{2,1,0:T(8,128)S(1)}, u32[]{:S(2)}, u32[]{:S(2)}) collective-permute-start(f32[13,8,128]{2,1,0:T(8,128)S(1)} %get-tuple-element.43), channel_id=1, source_target_pairs={{0,1},{1,0},{2,3},{3,2},{4,5},{5,4},{6,7},{7,6},{8,9},{9,8},{10,11... | collective-permute-start | bytes 159752 | tf_op jit(solution)/shard_map/ppermute | solution.py:759
  18.5 3.2 %collective-permute-start.2 = (f32[13,8,128]{2,1,0:T(8,128)S(1)}, f32[13,8,128]{2,1,0:T(8,128)S(1)}, u32[]{:S(2)}, u32[]{:S(2)}) collective-permute-start(f32[13,8,128]{2,1,0:T(8,128)S(1)} %get-tuple-element.44), channel_id=1, source_target_pairs={{0,0},{1,2},{2,1},{3,4},{4,3},{5,6},{6,5},{7,8},{8,7},{9,10},{10,9... | collective-permute-start | bytes 159752 | tf_op jit(solution)/shard_map/ppermute | solution.py:758
  21.6 0.0 collective-permute-done.1.first_ref
  21.6 3.0 %collective-permute-done.2.second_ref = f32[13,8,128]{2,1,0:T(8,128)S(1)} collective-permute-done((f32[13,8,128]{2,1,0:T(8,128)S(1)}, f32[13,8,128]{2,1,0:T(8,128)S(1)}, u32[]{:S(2)}, u32[]{:S(2)}) %collective-permute-start.2) | collective-permute-done | bytes 53280 | tf_op jit(solution)/shard_map/ppermute | solution.py:758
  24.7 0.0 all-to-all-done.arrived_ref
  24.7 0.6 %unpack_blocks.1 = (f32[30,32,128]{2,1,0:T(8,128)S(1)}, f32[15,8,128]{2,1,0:T(8,128)S(1)}) custom-call(f32[64,16,128]{2,1,0:T(8,128)S(1)} %all-to-all-done.arrived_ref), custom_call_target="tpu_custom_call" | custom-call | tf_op jit(solution)/shard_map/unpack_blocks/pallas_call | solution.py:812
  25.3 1.3 %collective-permute-start.3 = (f32[15,8,128]{2,1,0:T(8,128)S(1)}, f32[15,8,128]{2,1,0:T(8,128)S(1)}, u32[]{:S(2)}, u32[]{:S(2)}) collective-permute-start(f32[15,8,128]{2,1,0:T(8,128)S(1)} %get-tuple-element.46), channel_id=1, source_target_pairs={{0,16},{16,0},{1,17},{17,1},{2,18},{18,2},{3,19},{19,3},{4,20},{20... | collective-permute-start | bytes 184328 | tf_op jit(solution)/shard_map/ppermute | solution.py:743
  26.6 2.3 %own_rows.1 = (f32[3,16,48,128]{3,2,1,0:T(8,128)S(1)}, f32[3,16,48,128]{3,2,1,0:T(8,128)S(1)}, f32[15,32,128]{2,1,0:T(8,128)S(1)}, f32[15,32,128]{2,1,0:T(8,128)...) custom-call(f32[3,16,32,128]{3,2,1,0:T(8,128)S(1)} %copy-done, ...), custom_call_target="tpu_custom_call" | custom-call | tf_op jit(solution)/shard_map/own_rows/pallas_call | solution.py:828
  28.9 0.0 collective-permute-done.3.metal_above_ref.metal_below_ref.above_ref.below_ref
  28.9 0.4 metal_strips.1
  29.3 1.1 %collective-permute-start.4 = (f32[5,8,128]{2,1,0:T(8,128)S(1)}, f32[5,8,128]{2,1,0:T(8,128)S(1)}, u32[]{:S(2)}, u32[]{:S(2)}) collective-permute-start(f32[5,8,128]{2,1,0:T(8,128)S(1)} %get-tuple-element.80), channel_id=1, source_target_pairs={{0,1},{1,0},{2,3},{3,2},{4,5},{5,4},{6,7},{7,6},{8,9},{9,8},{10,11... | collective-permute-start | bytes 61448 | tf_op jit(solution)/shard_map/ppermute | solution.py:759
  30.3 3.1 %collective-permute-start.5 = (f32[5,8,128]{2,1,0:T(8,128)S(1)}, f32[5,8,128]{2,1,0:T(8,128)S(1)}, u32[]{:S(2)}, u32[]{:S(2)}) collective-permute-start(f32[5,8,128]{2,1,0:T(8,128)S(1)} %get-tuple-element.81), channel_id=1, source_target_pairs={{0,0},{1,2},{2,1},{3,4},{4,3},{5,6},{6,5},{7,8},{8,7},{9,10},{10,9... | collective-permute-start | bytes 61448 | tf_op jit(solution)/shard_map/ppermute | solution.py:758
  33.4 2.5 %halo_rows.1 = (f32[15,40,128]{2,1,0:T(8,128)S(1)}, f32[15,40,128]{2,1,0:T(8,128)S(1)}, f32[15,40,128]{2,1,0:T(8,128)S(1)}, f32[15,40,128]{2,1,0:T(8,128)S(1)}, ...) custom-call(f32[3,16,32,128]{3,2,1,0:T(8,128)S(1)} %copy-done, ...), custom_call_target="tpu_custom_call" | custom-call | tf_op jit(solution)/shard_map/halo_rows/pallas_call | solution.py:852
  35.9 0.0 collective-permute-done.4.metal_first_ref
  36.0 0.0 collective-permute-done.5.metal_second_ref
  36.0 7.3 %sweeps.1 = (f32[3,16,32,128]{3,2,1,0:T(8,128)}, f32[3,16,32,128]{3,2,1,0:T(8,128)}) custom-call(f32[15,40,128]{2,1,0:T(8,128)S(1)} %get-tuple-element.64.lame_ref, f32[15,40,128]{2,1,0:T(8,128)S(1)} %get-tuple-element.65.shear_ref, f32[15,40,128]{2,1,0:T(8,128)S(1)} %get-tuple-element.66.thermal_ref, f32[15,40,128]{2,1,0:T(8,128)S(1)} %get-tuple-element.67.twice_ref, ...), custom_call_target="tpu_custom_call" | custom-call | tf_op jit(solution)/shard_map/sweeps/pallas_call | solution.py:877
  (2 shorter events, 0.0 us)
Async XLA Ops:
  0.6 9.8 %copy-start = (f32[3,16,32,128]{3,2,1,0:T(8,128)S(1)}, f32[3,16,32,128]{3,2,1,0:T(8,128)}, u32[]{:S(2)}) copy-start(f32[3,16,32,128]{3,2,1,0:T(8,128)} %displacement_ref.7) | copy-start | bytes 2359300
  0.6 9.8 %copy-start.1 = (f32[15,32,128]{2,1,0:T(8,128)S(1)}, f32[15,32,128]{2,1,0:T(8,128)}, u32[]{:S(2)}) copy-start(f32[15,32,128]{2,1,0:T(8,128)} %heating_ref.5) | copy-start | bytes 737284
  0.7 9.8 %copy-start.2 = (s32[15,32,128]{2,1,0:T(8,128)S(1)}, s32[15,32,128]{2,1,0:T(8,128)}, u32[]{:S(2)}) copy-start(s32[15,32,128]{2,1,0:T(8,128)} %materials_ref.5) | copy-start | bytes 737284
  0.7 9.8 %copy-start.5 = (f32[8]{0:T(128)S(1)}, f32[8]{0:T(128)}, u32[]{:S(2)}) copy-start(f32[8]{0:T(128)} %expansion_ref.1) | copy-start | bytes 100
  0.7 9.8 %copy-start.4 = (f32[8]{0:T(128)S(1)}, f32[8]{0:T(128)}, u32[]{:S(2)}) copy-start(f32[8]{0:T(128)} %poisson_ref.1) | copy-start | bytes 100
  0.7 9.8 %copy-start.3 = (f32[8]{0:T(128)S(1)}, f32[8]{0:T(128)}, u32[]{:S(2)}) copy-start(f32[8]{0:T(128)} %modulus_ref.1) | copy-start | bytes 100
  3.0 21.6 %all-to-all-start = ((f32[64,16,128]{2,1,0:T(8,128)}), f32[64,16,128]{2,1,0:T(8,128)S(1)}, u32[]{:S(2)}, u32[]{:S(2)}) async-start(f32[64,16,128]{2,1,0:T(8,128)} %pack_blocks.1), calls=%async_computation | async-start | bytes 1048576 | tf_op jit(solution)/shard_map/all_to_all | solution.py:786
  11.1 5.7 %collective-permute-start = (f32[39,8,128]{2,1,0:T(8,128)S(1)}, f32[39,8,128]{2,1,0:T(8,128)S(1)}, u32[]{:S(2)}, u32[]{:S(2)}) collective-permute-start(f32[39,8,128]{2,1,0:T(8,128)S(1)} %get-tuple-element.42), channel_id=1, source_target_pairs={{0,16},{16,0},{1,17},{17,1},{2,18},{18,2},{3,19},{19,3},{4,20},{20... | collective-permute-start | bytes 479240 | tf_op jit(solution)/shard_map/ppermute | solution.py:743
  17.5 4.1 %collective-permute-start.1 = (f32[13,8,128]{2,1,0:T(8,128)S(1)}, f32[13,8,128]{2,1,0:T(8,128)S(1)}, u32[]{:S(2)}, u32[]{:S(2)}) collective-permute-start(f32[13,8,128]{2,1,0:T(8,128)S(1)} %get-tuple-element.43), channel_id=1, source_target_pairs={{0,1},{1,0},{2,3},{3,2},{4,5},{5,4},{6,7},{7,6},{8,9},{9,8},{10,11... | collective-permute-start | bytes 159752 | tf_op jit(solution)/shard_map/ppermute | solution.py:759
  18.5 6.2 %collective-permute-start.2 = (f32[13,8,128]{2,1,0:T(8,128)S(1)}, f32[13,8,128]{2,1,0:T(8,128)S(1)}, u32[]{:S(2)}, u32[]{:S(2)}) collective-permute-start(f32[13,8,128]{2,1,0:T(8,128)S(1)} %get-tuple-element.44), channel_id=1, source_target_pairs={{0,0},{1,2},{2,1},{3,4},{4,3},{5,6},{6,5},{7,8},{8,7},{9,10},{10,9... | collective-permute-start | bytes 159752 | tf_op jit(solution)/shard_map/ppermute | solution.py:758
  25.3 3.6 %collective-permute-start.3 = (f32[15,8,128]{2,1,0:T(8,128)S(1)}, f32[15,8,128]{2,1,0:T(8,128)S(1)}, u32[]{:S(2)}, u32[]{:S(2)}) collective-permute-start(f32[15,8,128]{2,1,0:T(8,128)S(1)} %get-tuple-element.46), channel_id=1, source_target_pairs={{0,16},{16,0},{1,17},{17,1},{2,18},{18,2},{3,19},{19,3},{4,20},{20... | collective-permute-start | bytes 184328 | tf_op jit(solution)/shard_map/ppermute | solution.py:743
  29.3 6.7 %collective-permute-start.4 = (f32[5,8,128]{2,1,0:T(8,128)S(1)}, f32[5,8,128]{2,1,0:T(8,128)S(1)}, u32[]{:S(2)}, u32[]{:S(2)}) collective-permute-start(f32[5,8,128]{2,1,0:T(8,128)S(1)} %get-tuple-element.80), channel_id=1, source_target_pairs={{0,1},{1,0},{2,3},{3,2},{4,5},{5,4},{6,7},{7,6},{8,9},{9,8},{10,11... | collective-permute-start | bytes 61448 | tf_op jit(solution)/shard_map/ppermute | solution.py:759
  30.3 5.6 %collective-permute-start.5 = (f32[5,8,128]{2,1,0:T(8,128)S(1)}, f32[5,8,128]{2,1,0:T(8,128)S(1)}, u32[]{:S(2)}, u32[]{:S(2)}) collective-permute-start(f32[5,8,128]{2,1,0:T(8,128)S(1)} %get-tuple-element.81), channel_id=1, source_target_pairs={{0,0},{1,2},{2,1},{3,4},{4,3},{5,6},{6,5},{7,8},{8,7},{9,10},{10,9... | collective-permute-start | bytes 61448 | tf_op jit(solution)/shard_map/ppermute | solution.py:758

commit v6 on v5

--- a/solution.py
+++ b/solution.py
@@ -676,26 +676,26 @@
         ]
 
     strip_forces(s_strip_in, d_strip_in, strip_refs, own_strip, next_strip)
-    relax_strips(v_strip_in)
-
     v_now, own_now, next_now = v_in, own_in, next_in
     for sweep in range(1, ITERS):
         if sweep > 1:
             inner_forces(s_ref, d_ref, cell_refs, own_ref, next_ref, 5, 8)
             next_ref.copy_row(47, 7)
             own_now, next_now = own_ref, next_ref
-
-        def relax_rows(z):
+            relax_strips(v_strip)
+            strip_forces(s_strip, d_strip, strip_refs, own_strip, next_strip)
+        for z in range(nodes):
             for c in range(3):
                 for j in range(5):
                     v = v_now[c, z, chunk_of(j), :]
                     parts = inner_parts(own_now, next_now, c, z, j)
                     v = v - weight_ref[z, chunk_of(j), :] * unbalanced(*parts, v, z)
                     store_inner(s_ref, d_ref, v_ref, c, z, j, v)
-
-        strip_forces(s_strip, d_strip, strip_refs, own_strip, next_strip, relax_rows)
-        relax_strips(v_strip)
+        if sweep == 1:
+            relax_strips(v_strip_in)
+            strip_forces(s_strip, d_strip, strip_refs, own_strip, next_strip)
         v_now = v_ref
+    relax_strips(v_strip)
 
     def joined(strip):
         return jnp.where(place < 8, strip, roll_lanes(strip, -8))

time: 43.6 us -> 43.4 us (level)
  no operation moved by 1% of the time
where the time goes in v6:
time: 43.4 us; the launch traced here: 43.1 us
  starting transfers between devices  18.2 us (42%)
  Pallas kernels  16.6 us (38%)
  waiting for transfers between devices  7.5 us (17%)
  between operations  0.82 us (2%)
    all_to_all x1, starting transfers between devices, body(): lax.all_to_all(packed, 'col', split_axis=0, concat_axis=0, tiled=True)  7.36 us
    pallas_call x1, Pallas kernels, body(): pl.pallas_call(functools.partial(sweep_kernel, domain), out_shape=[f32(*d...  7.16 us
    ppermute x2, starting transfers between devices, exchange_columns(): from_second = lax.ppermute(second, 'col', two)  6.24 us
    ppermute x2, waiting for transfers between devices, exchange_rows(): other = lax.ppermute(edges[0], 'row', [(0, 1), (1, 0)])  4.45 us
    ppermute x2, waiting for transfers between devices, exchange_columns(): from_second = lax.ppermute(second, 'col', two)  3.05 us
    ppermute x2, starting transfers between devices, exchange_rows(): other = lax.ppermute(edges[0], 'row', [(0, 1), (1, 0)])  2.58 us
    pallas_call x1, Pallas kernels, body(): pl.pallas_call(functools.partial(halo_rows_kernel, domain), out_shape=[f3...  2.51 us
    pallas_call x1, Pallas kernels, body(): pl.pallas_call(functools.partial(pack_kernel, tile_blocks, columns, block...  2.35 us
  transfers between devices with their start and end apart: 7, of which 2 were waited for; matrix products, arithmetic and copies ran while one was open for 0% of the time, Pallas kernels for 14%

profile of v6, /device:TPU:1, one launch (start us, length us, event | category | flops | bytes accessed | tf_op | source)
XLA Modules:
  0.0 43.1 jit_solution(8150673101590943587)
XLA Ops:
  0.6 0.0 copy-start
  0.6 0.0 copy-start.1
  0.7 0.0 copy-start.2
  0.7 0.0 copy-start.5
  0.7 0.0 copy-start.4
  0.7 0.0 copy-start.3
  0.7 2.3 %pack_blocks.1 = f32[64,16,128]{2,1,0:T(8,128)} custom-call(s32[1,64]{1,0:T(1,128)} %target_hbm.1, f32[64,1920]{1,0:T(8,128)} %bitcast.1), custom_call_target="tpu_custom_call" | custom-call | tf_op jit(solution)/shard_map/pack_blocks/pallas_call | solution.py:773
  3.0 7.4 %all-to-all-start = ((f32[64,16,128]{2,1,0:T(8,128)}), f32[64,16,128]{2,1,0:T(8,128)S(1)}, u32[]{:S(2)}, u32[]{:S(2)}) async-start(f32[64,16,128]{2,1,0:T(8,128)} %pack_blocks.1), calls=%async_computation | async-start | bytes 1048576 | tf_op jit(solution)/shard_map/all_to_all | solution.py:786
  10.4 0.0 copy-done
  10.4 0.0 copy-done.1
  10.4 0.0 copy-done.2
  10.4 0.0 copy-done.5
  10.5 0.6 %field_edges.1 = (f32[3,8,8,128]{3,2,1,0:T(8,128)S(1)}, f32[39,8,128]{2,1,0:T(8,128)S(1)}) custom-call(f32[3,16,32,128]{3,2,1,0:T(8,128)S(1)} %copy-done, f32[15,32,128]{2,1,0:T(8,128)S(1)} %copy-done.1, s32[15,32,128]{2,1,0:T(8,128)S(1)} %copy-done.2, f32[8]{0:T(128)S(1)} %copy-done.3, f32[8]{0:T(128)S(1)} %copy-done.4, f32[8]{0:T(128)S(1)} %copy-done.5), custom_call_target="tpu_custom_call" | custom-call | tf_op jit(solution)/shard_map/field_edges/pallas_call | solution.py:789
  11.1 1.3 %collective-permute-start = (f32[39,8,128]{2,1,0:T(8,128)S(1)}, f32[39,8,128]{2,1,0:T(8,128)S(1)}, u32[]{:S(2)}, u32[]{:S(2)}) collective-permute-start(f32[39,8,128]{2,1,0:T(8,128)S(1)} %get-tuple-element.42), channel_id=1, source_target_pairs={{0,16},{16,0},{1,17},{17,1},{2,18},{18,2},{3,19},{19,3},{4,20},{20... | collective-permute-start | bytes 479240 | tf_op jit(solution)/shard_map/ppermute | solution.py:743
  12.4 4.4 %collective-permute-done.above_ref.below_ref = f32[39,8,128]{2,1,0:T(8,128)S(1)} collective-permute-done((f32[39,8,128]{2,1,0:T(8,128)S(1)}, f32[39,8,128]{2,1,0:T(8,128)S(1)}, u32[]{:S(2)}, u32[]{:S(2)}) %collective-permute-start) | collective-permute-done | bytes 159776 | tf_op jit(solution)/shard_map/ppermute | solution.py:743
  16.8 0.7 %field_strips.1 = (f32[78,8,128]{2,1,0:T(8,128)S(1)}, f32[13,8,128]{2,1,0:T(8,128)S(1)}, f32[13,8,128]{2,1,0:T(8,128)S(1)}) custom-call(f32[3,16,32,128]{3,2,1,0:T(8,128)S(1)} %copy-done, f32[15,32,128]{2,1,0:T(8,128)S(1)} %copy-done.1, s32[15,32,128]{2,1,0:T(8,128)S(1)} %copy-done.2, f32[39,8,128]{2,1,0:T(8,128)S(1)} %collective-permute-done.above_ref.below_ref, ...), custom_call_target="tpu_custom_call" | custom-call | tf_op jit(solution)/shard_map/field_strips/pallas_call | solution.py:800
  17.5 0.9 %collective-permute-start.1 = (f32[13,8,128]{2,1,0:T(8,128)S(1)}, f32[13,8,128]{2,1,0:T(8,128)S(1)}, u32[]{:S(2)}, u32[]{:S(2)}) collective-permute-start(f32[13,8,128]{2,1,0:T(8,128)S(1)} %get-tuple-element.43), channel_id=1, source_target_pairs={{0,1},{1,0},{2,3},{3,2},{4,5},{5,4},{6,7},{7,6},{8,9},{9,8},{10,11... | collective-permute-start | bytes 159752 | tf_op jit(solution)/shard_map/ppermute | solution.py:759
  18.5 3.2 %collective-permute-start.2 = (f32[13,8,128]{2,1,0:T(8,128)S(1)}, f32[13,8,128]{2,1,0:T(8,128)S(1)}, u32[]{:S(2)}, u32[]{:S(2)}) collective-permute-start(f32[13,8,128]{2,1,0:T(8,128)S(1)} %get-tuple-element.44), channel_id=1, source_target_pairs={{0,0},{1,2},{2,1},{3,4},{4,3},{5,6},{6,5},{7,8},{8,7},{9,10},{10,9... | collective-permute-start | bytes 159752 | tf_op jit(solution)/shard_map/ppermute | solution.py:758
  21.6 0.0 collective-permute-done.1.first_ref
  21.6 3.0 %collective-permute-done.2.second_ref = f32[13,8,128]{2,1,0:T(8,128)S(1)} collective-permute-done((f32[13,8,128]{2,1,0:T(8,128)S(1)}, f32[13,8,128]{2,1,0:T(8,128)S(1)}, u32[]{:S(2)}, u32[]{:S(2)}) %collective-permute-start.2) | collective-permute-done | bytes 53280 | tf_op jit(solution)/shard_map/ppermute | solution.py:758
  24.7 0.0 all-to-all-done.arrived_ref
  24.7 0.6 %unpack_blocks.1 = (f32[30,32,128]{2,1,0:T(8,128)S(1)}, f32[15,8,128]{2,1,0:T(8,128)S(1)}) custom-call(f32[64,16,128]{2,1,0:T(8,128)S(1)} %all-to-all-done.arrived_ref), custom_call_target="tpu_custom_call" | custom-call | tf_op jit(solution)/shard_map/unpack_blocks/pallas_call | solution.py:812
  25.3 1.3 %collective-permute-start.3 = (f32[15,8,128]{2,1,0:T(8,128)S(1)}, f32[15,8,128]{2,1,0:T(8,128)S(1)}, u32[]{:S(2)}, u32[]{:S(2)}) collective-permute-start(f32[15,8,128]{2,1,0:T(8,128)S(1)} %get-tuple-element.46), channel_id=1, source_target_pairs={{0,16},{16,0},{1,17},{17,1},{2,18},{18,2},{3,19},{19,3},{4,20},{20... | collective-permute-start | bytes 184328 | tf_op jit(solution)/shard_map/ppermute | solution.py:743
  26.6 2.3 %own_rows.1 = (f32[3,16,48,128]{3,2,1,0:T(8,128)S(1)}, f32[3,16,48,128]{3,2,1,0:T(8,128)S(1)}, f32[15,32,128]{2,1,0:T(8,128)S(1)}, f32[15,32,128]{2,1,0:T(8,128)...) custom-call(f32[3,16,32,128]{3,2,1,0:T(8,128)S(1)} %copy-done, ...), custom_call_target="tpu_custom_call" | custom-call | tf_op jit(solution)/shard_map/own_rows/pallas_call | solution.py:828
  28.9 0.0 collective-permute-done.3.metal_above_ref.metal_below_ref.above_ref.below_ref
  28.9 0.4 metal_strips.1
  29.3 1.1 %collective-permute-start.4 = (f32[5,8,128]{2,1,0:T(8,128)S(1)}, f32[5,8,128]{2,1,0:T(8,128)S(1)}, u32[]{:S(2)}, u32[]{:S(2)}) collective-permute-start(f32[5,8,128]{2,1,0:T(8,128)S(1)} %get-tuple-element.80), channel_id=1, source_target_pairs={{0,1},{1,0},{2,3},{3,2},{4,5},{5,4},{6,7},{7,6},{8,9},{9,8},{10,11... | collective-permute-start | bytes 61448 | tf_op jit(solution)/shard_map/ppermute | solution.py:759
  30.3 3.1 %collective-permute-start.5 = (f32[5,8,128]{2,1,0:T(8,128)S(1)}, f32[5,8,128]{2,1,0:T(8,128)S(1)}, u32[]{:S(2)}, u32[]{:S(2)}) collective-permute-start(f32[5,8,128]{2,1,0:T(8,128)S(1)} %get-tuple-element.81), channel_id=1, source_target_pairs={{0,0},{1,2},{2,1},{3,4},{4,3},{5,6},{6,5},{7,8},{8,7},{9,10},{10,9... | collective-permute-start | bytes 61448 | tf_op jit(solution)/shard_map/ppermute | solution.py:758
  33.4 2.5 %halo_rows.1 = (f32[15,40,128]{2,1,0:T(8,128)S(1)}, f32[15,40,128]{2,1,0:T(8,128)S(1)}, f32[15,40,128]{2,1,0:T(8,128)S(1)}, f32[15,40,128]{2,1,0:T(8,128)S(1)}, ...) custom-call(f32[3,16,32,128]{3,2,1,0:T(8,128)S(1)} %copy-done, ...), custom_call_target="tpu_custom_call" | custom-call | tf_op jit(solution)/shard_map/halo_rows/pallas_call | solution.py:852
  35.9 0.0 collective-permute-done.4.metal_first_ref
  36.0 0.0 collective-permute-done.5.metal_second_ref
  36.0 7.2 %sweeps.1 = (f32[3,16,32,128]{3,2,1,0:T(8,128)}, f32[3,16,32,128]{3,2,1,0:T(8,128)}) custom-call(f32[15,40,128]{2,1,0:T(8,128)S(1)} %get-tuple-element.64.lame_ref, f32[15,40,128]{2,1,0:T(8,128)S(1)} %get-tuple-element.65.shear_ref, f32[15,40,128]{2,1,0:T(8,128)S(1)} %get-tuple-element.66.thermal_ref, f32[15,40,128]{2,1,0:T(8,128)S(1)} %get-tuple-element.67.twice_ref, ...), custom_call_target="tpu_custom_call" | custom-call | tf_op jit(solution)/shard_map/sweeps/pallas_call | solution.py:877
  (2 shorter events, 0.0 us)
Async XLA Ops:
  0.6 9.8 %copy-start = (f32[3,16,32,128]{3,2,1,0:T(8,128)S(1)}, f32[3,16,32,128]{3,2,1,0:T(8,128)}, u32[]{:S(2)}) copy-start(f32[3,16,32,128]{3,2,1,0:T(8,128)} %displacement_ref.7) | copy-start | bytes 2359300
  0.6 9.8 %copy-start.1 = (f32[15,32,128]{2,1,0:T(8,128)S(1)}, f32[15,32,128]{2,1,0:T(8,128)}, u32[]{:S(2)}) copy-start(f32[15,32,128]{2,1,0:T(8,128)} %heating_ref.5) | copy-start | bytes 737284
  0.7 9.8 %copy-start.2 = (s32[15,32,128]{2,1,0:T(8,128)S(1)}, s32[15,32,128]{2,1,0:T(8,128)}, u32[]{:S(2)}) copy-start(s32[15,32,128]{2,1,0:T(8,128)} %materials_ref.5) | copy-start | bytes 737284
  0.7 9.8 %copy-start.5 = (f32[8]{0:T(128)S(1)}, f32[8]{0:T(128)}, u32[]{:S(2)}) copy-start(f32[8]{0:T(128)} %expansion_ref.1) | copy-start | bytes 100
  0.7 9.8 %copy-start.4 = (f32[8]{0:T(128)S(1)}, f32[8]{0:T(128)}, u32[]{:S(2)}) copy-start(f32[8]{0:T(128)} %poisson_ref.1) | copy-start | bytes 100
  0.7 9.8 %copy-start.3 = (f32[8]{0:T(128)S(1)}, f32[8]{0:T(128)}, u32[]{:S(2)}) copy-start(f32[8]{0:T(128)} %modulus_ref.1) | copy-start | bytes 100
  3.0 21.6 %all-to-all-start = ((f32[64,16,128]{2,1,0:T(8,128)}), f32[64,16,128]{2,1,0:T(8,128)S(1)}, u32[]{:S(2)}, u32[]{:S(2)}) async-start(f32[64,16,128]{2,1,0:T(8,128)} %pack_blocks.1), calls=%async_computation | async-start | bytes 1048576 | tf_op jit(solution)/shard_map/all_to_all | solution.py:786
  11.1 5.7 %collective-permute-start = (f32[39,8,128]{2,1,0:T(8,128)S(1)}, f32[39,8,128]{2,1,0:T(8,128)S(1)}, u32[]{:S(2)}, u32[]{:S(2)}) collective-permute-start(f32[39,8,128]{2,1,0:T(8,128)S(1)} %get-tuple-element.42), channel_id=1, source_target_pairs={{0,16},{16,0},{1,17},{17,1},{2,18},{18,2},{3,19},{19,3},{4,20},{20... | collective-permute-start | bytes 479240 | tf_op jit(solution)/shard_map/ppermute | solution.py:743
  17.5 4.1 %collective-permute-start.1 = (f32[13,8,128]{2,1,0:T(8,128)S(1)}, f32[13,8,128]{2,1,0:T(8,128)S(1)}, u32[]{:S(2)}, u32[]{:S(2)}) collective-permute-start(f32[13,8,128]{2,1,0:T(8,128)S(1)} %get-tuple-element.43), channel_id=1, source_target_pairs={{0,1},{1,0},{2,3},{3,2},{4,5},{5,4},{6,7},{7,6},{8,9},{9,8},{10,11... | collective-permute-start | bytes 159752 | tf_op jit(solution)/shard_map/ppermute | solution.py:759
  18.5 6.2 %collective-permute-start.2 = (f32[13,8,128]{2,1,0:T(8,128)S(1)}, f32[13,8,128]{2,1,0:T(8,128)S(1)}, u32[]{:S(2)}, u32[]{:S(2)}) collective-permute-start(f32[13,8,128]{2,1,0:T(8,128)S(1)} %get-tuple-element.44), channel_id=1, source_target_pairs={{0,0},{1,2},{2,1},{3,4},{4,3},{5,6},{6,5},{7,8},{8,7},{9,10},{10,9... | collective-permute-start | bytes 159752 | tf_op jit(solution)/shard_map/ppermute | solution.py:758
  25.3 3.6 %collective-permute-start.3 = (f32[15,8,128]{2,1,0:T(8,128)S(1)}, f32[15,8,128]{2,1,0:T(8,128)S(1)}, u32[]{:S(2)}, u32[]{:S(2)}) collective-permute-start(f32[15,8,128]{2,1,0:T(8,128)S(1)} %get-tuple-element.46), channel_id=1, source_target_pairs={{0,16},{16,0},{1,17},{17,1},{2,18},{18,2},{3,19},{19,3},{4,20},{20... | collective-permute-start | bytes 184328 | tf_op jit(solution)/shard_map/ppermute | solution.py:743
  29.3 6.7 %collective-permute-start.4 = (f32[5,8,128]{2,1,0:T(8,128)S(1)}, f32[5,8,128]{2,1,0:T(8,128)S(1)}, u32[]{:S(2)}, u32[]{:S(2)}) collective-permute-start(f32[5,8,128]{2,1,0:T(8,128)S(1)} %get-tuple-element.80), channel_id=1, source_target_pairs={{0,1},{1,0},{2,3},{3,2},{4,5},{5,4},{6,7},{7,6},{8,9},{9,8},{10,11... | collective-permute-start | bytes 61448 | tf_op jit(solution)/shard_map/ppermute | solution.py:759
  30.3 5.6 %collective-permute-start.5 = (f32[5,8,128]{2,1,0:T(8,128)S(1)}, f32[5,8,128]{2,1,0:T(8,128)S(1)}, u32[]{:S(2)}, u32[]{:S(2)}) collective-permute-start(f32[5,8,128]{2,1,0:T(8,128)S(1)} %get-tuple-element.81), channel_id=1, source_target_pairs={{0,0},{1,2},{2,1},{3,4},{4,3},{5,6},{6,5},{7,8},{8,7},{9,10},{10,9... | collective-permute-start | bytes 61448 | tf_op jit(solution)/shard_map/ppermute | solution.py:758
